TPU v7x, 128 devices: a whole 4x4x4 slice. The times are simulated.
128 devices in a mesh: exc: 4 (over y_lo, core), space: 32 (over x, y_hi, z).
Axes of the slice: x: 4, y: 4 (y_hi: 2, y_lo: 2; y = y_hi * 2 + y_lo), z: 4, core: 2. Of those that a mesh axis runs over, the one named last changes fastest.
Arguments:
- forward_fields: float32 [4, 6, 32, 256, 1024], P('exc', None, None, 'space'), may hold values from -6 to 6
- forward_sums: float32 [4, 6, 8, 256, 1024], P('exc', None, None, 'space'), may hold values from -6 to 6
- adjoint_fields: float32 [4, 6, 32, 256, 1024], P('exc', None, None, 'space'), may hold values from -6 to 6
- adjoint_sums: float32 [4, 6, 8, 256, 1024], P('exc', None, None, 'space'), may hold values from -6 to 6
- monitor_sums: float32 [4, 2, 32, 256], P('exc', None, None, 'space'), may hold values from -6 to 6
- density: float32 [1024, 256], P('exc', 'space'), may hold values from 0 to 1
- labels: int32 [256, 1024], P('space'), may hold values from 0 to 2
- source_plane: int32 [4], P('exc'), may hold values from 0 to 1023
- monitor_plane: int32 [4], P('exc'), may hold values from 0 to 1023
- mode_numbers: int32 [4], P('exc'), may hold values from 0 to 3
- frequency: float32 [4], P('exc'), may hold values from 0.3 to 1.2
- start_phase: float32 [4], P('exc'), may hold values from -3.140625 to 3.140625
Outputs:
- design_gradient: float32 [1024, 256], P('exc', 'space')
- figure_of_merit: float32 [4], P('exc')
All inputs are finite; a program needn't handle non-finite values.
Results may differ from a plain program's by a relative error of at most 0.0003.
Values sent between devices are 32-bit elements; how exact they have to be, the bound alone decides.
No kernel may reach another device: no remote copies, remote signals or barrier semaphores. Data moves between devices by JAX's collectives and lax.ppermute only.
A program may use at most 128 MiB of HBM per device.

v0:
```python
import math

import jax
import jax.numpy as jnp
from jax import lax
from jax.sharding import PartitionSpec as P

STEPS = 2
R = 4


COURANT = 0.5
OXIDE_PERMITTIVITY = 2.1
SILICON_PERMITTIVITY = 12.1
AIR_PERMITTIVITY = 1.0
SHARPNESS = 4.0
MIDPOINT = 0.5


def padded_2(block, sides, width):
    for axis, dim in sides:
        count = lax.axis_size(axis)
        forward = [(i, i + 1) for i in range(count - 1)]
        backward = [(target, source) for source, target in forward]
        low = lax.ppermute(
            lax.slice_in_dim(block, block.shape[dim] - width, None, axis=dim), axis, forward
        )
        high = lax.ppermute(lax.slice_in_dim(block, 0, width, axis=dim), axis, backward)
        block = jnp.concatenate([low, block, high], axis=dim)
    return block


def passed_along(block, axis, distance):
    devices = range(lax.axis_size(axis))
    route = [(i - distance, i) for i in devices if i - distance in devices]
    return lax.ppermute(block, axis, route)


def smooth(padded, radius):
    row_total = padded.shape[0] - 2 * radius
    column_total = padded.shape[1] - 2 * radius
    across = None
    for offset in range(2 * radius + 1):
        weight = (radius + 1.0 - abs(offset - radius)) / ((radius + 1.0) * (radius + 1.0))
        addend = weight * padded[:, offset : offset + column_total]
        across = addend if across is None else across + addend
    result = None
    for offset in range(2 * radius + 1):
        weight = (radius + 1.0 - abs(offset - radius)) / ((radius + 1.0) * (radius + 1.0))
        addend = weight * across[offset : offset + row_total, :]
        result = addend if result is None else result + addend
    return result


def project(filtered):
    lower = math.tanh(SHARPNESS * MIDPOINT)
    spread = lower + math.tanh(SHARPNESS * (1.0 - MIDPOINT))
    bent = jnp.tanh(SHARPNESS * (filtered - MIDPOINT))
    return ((lower + bent) / spread, SHARPNESS * (1.0 - bent * bent) / spread)


def slab_inverse(labels, projected):
    material = jnp.where(labels == 1, SILICON_PERMITTIVITY, OXIDE_PERMITTIVITY)
    mixed = OXIDE_PERMITTIVITY + (SILICON_PERMITTIVITY - OXIDE_PERMITTIVITY) * projected
    return 1.0 / jnp.where(labels == 2, mixed, material)


def layered(inverse_rows, layer_count, slab_start, slab_layers):
    row_total, column_total = inverse_rows.shape
    beneath = jnp.full((slab_start, row_total, column_total), 1.0 / OXIDE_PERMITTIVITY, jnp.float32)
    middle = jnp.broadcast_to(inverse_rows[None], (slab_layers, row_total, column_total))
    overhead = jnp.full(
        (layer_count - slab_start - slab_layers, row_total, column_total),
        1.0 / AIR_PERMITTIVITY,
        jnp.float32,
    )
    return jnp.concatenate((beneath, middle, overhead), 0)


def profile(modes, rows, layer_count, grid_rows):
    layers = jnp.arange(layer_count, dtype=jnp.float32) + 0.5
    order = (modes + 1).astype(jnp.float32)
    across_z = jnp.sin(math.pi * order[:, None] * layers[None, :] / layer_count)
    ramp = 1.0 + 2.0 * (rows + 0.5) / grid_rows
    return across_z[:, :, None] * ramp[None, None, :]


def upward(field, axis):
    size = field.shape[axis]
    later = jnp.concatenate(
        (
            lax.slice_in_dim(field, 1, size, axis=axis),
            jnp.zeros_like(lax.slice_in_dim(field, 0, 1, axis=axis)),
        ),
        axis,
    )
    return later - field


def downward(field, axis):
    size = field.shape[axis]
    earlier = jnp.concatenate(
        (
            jnp.zeros_like(lax.slice_in_dim(field, 0, 1, axis=axis)),
            lax.slice_in_dim(field, 0, size - 1, axis=axis),
        ),
        axis,
    )
    return field - earlier


def upward_rows(field, upper):
    return jnp.concatenate((field[:, :, 1:], upper[:, :, None]), 2) - field


def downward_rows(field, lower):
    return field - jnp.concatenate((lower[:, :, None], field[:, :, :-1]), 2)


def local(
    forward_fields,
    forward_sums,
    adjoint_fields,
    adjoint_sums,
    monitor_sums,
    density,
    labels,
    source_plane,
    monitor_plane,
    mode_numbers,
    frequency,
    start_phase,
):
    groups = lax.axis_size("exc")
    strips = lax.axis_size("space")
    row_count, column_count = labels.shape
    layer_count = forward_fields.shape[2]
    slab_layers = forward_sums.shape[2]
    slab_start = (layer_count - slab_layers) // 2
    grid_rows = row_count * strips
    base_row = lax.axis_index("space") * row_count
    gathered = lax.all_gather(density, "exc", axis=0, tiled=True)
    widened = padded_2(gathered, (("space", 1),), R)
    filtered = smooth(jnp.pad(widened, ((R, R), (0, 0))), R).T
    projected, steepness = project(filtered)
    inverse_slab = slab_inverse(labels, projected)
    margin = 0
    rows_global = base_row + jnp.arange(row_count, dtype=jnp.int32)

    def fetch_above(lead_x, lead_z):
        edge_rows = jnp.stack((lead_x[:, :, 0], lead_z[:, :, 0]), 1)
        return passed_along(edge_rows, "space", -1)

    def fetch_below(lead_x, lead_z):
        edge_rows = jnp.stack((lead_x[:, :, -1], lead_z[:, :, -1]), 1)
        return passed_along(edge_rows, "space", 1)

    inverse = layered(inverse_slab, layer_count, slab_start, slab_layers)
    shapes = profile(mode_numbers, rows_global.astype(jnp.float32), layer_count, grid_rows)
    interior = slice(margin, margin + row_count)
    column_ids = jnp.arange(column_count, dtype=jnp.int32)

    def advance(fields, sums, plane, cosine_weight, sine_weight, watched):
        electric_x, electric_y, electric_z = (fields[:, 0], fields[:, 1], fields[:, 2])
        magnetic_x, magnetic_y, magnetic_z = (fields[:, 3], fields[:, 4], fields[:, 5])
        column_mask = (column_ids[None, :] == plane[:, None]).astype(jnp.float32)
        for step_index in range(STEPS):
            phase_now = start_phase + frequency * step_index
            cosine = jnp.cos(phase_now)
            sine_part = jnp.sin(phase_now)
            strength = cosine_weight * cosine + sine_weight * sine_part
            upper = fetch_above(electric_x, electric_z)
            magnetic_x = magnetic_x - COURANT * (
                upward_rows(electric_z, upper[:, 1]) - upward(electric_y, 1)
            )
            magnetic_y = magnetic_y - COURANT * (upward(electric_x, 1) - upward(electric_z, 3))
            magnetic_z = magnetic_z - COURANT * (
                upward(electric_y, 3) - upward_rows(electric_x, upper[:, 0])
            )
            magnetic_x, magnetic_y, magnetic_z = (magnetic_x, magnetic_y, magnetic_z)
            lower = fetch_below(magnetic_x, magnetic_z)
            source = (shapes * strength[:, None, None])[..., None] * column_mask[:, None, None, :]
            electric_x = electric_x + COURANT * inverse * (
                downward_rows(magnetic_z, lower[:, 1]) - downward(magnetic_y, 1)
            )
            electric_y = electric_y + COURANT * inverse * (
                downward(magnetic_x, 1) - downward(magnetic_z, 3)
            )
            electric_z = electric_z + COURANT * inverse * (
                downward(magnetic_y, 3) - downward_rows(magnetic_x, lower[:, 0]) - source
            )
            electric_x, electric_y, electric_z = (electric_x, electric_y, electric_z)
            recorded = jnp.stack((electric_x, electric_y, electric_z), 1)[
                :, :, slab_start : slab_start + slab_layers, interior
            ]
            sums = jnp.concatenate(
                (
                    sums[:, :3] + recorded * cosine[:, None, None, None, None],
                    sums[:, 3:] - recorded * sine_part[:, None, None, None, None],
                ),
                1,
            )
            if watched is not None:
                index = jnp.broadcast_to(
                    plane[:, None, None, None], (plane.shape[0], layer_count, row_count, 1)
                )
                column = jnp.take_along_axis(electric_z, index, axis=3)[..., 0]
                watched = jnp.stack(
                    (
                        watched[:, 0] + column * cosine[:, None, None],
                        watched[:, 1] - column * sine_part[:, None, None],
                    ),
                    1,
                )
        return (sums, watched)

    forward_done, watched = advance(
        forward_fields, forward_sums, source_plane, 1.0, 0.0, monitor_sums
    )
    partial_value = jnp.stack(
        (
            jnp.sum(watched[:, 0] * shapes, axis=(1, 2)),
            jnp.sum(watched[:, 1] * shapes, axis=(1, 2)),
        ),
        1,
    )
    intersection = lax.psum(partial_value, "space") / math.sqrt(layer_count * grid_rows)
    intersection_real = intersection[:, 0]
    intersection_imaginary = intersection[:, 1]
    merits = intersection_real * intersection_real + intersection_imaginary * intersection_imaginary
    adjoint_done, unused = advance(
        adjoint_fields, adjoint_sums, monitor_plane, intersection_real, intersection_imaginary, None
    )
    product = forward_done[:, :3] * adjoint_done[:, :3] - forward_done[:, 3:] * adjoint_done[:, 3:]
    per_source = jnp.sum(product, axis=(1, 2))
    weighted = jnp.sum((frequency * frequency)[:, None, None] * per_source, axis=0)
    design = (labels == 2).astype(jnp.float32)
    scale = 1.0 / math.sqrt(forward_fields.shape[0] * groups * slab_layers)
    sensitivity = (
        weighted * (scale * (SILICON_PERMITTIVITY - OXIDE_PERMITTIVITY)) * design * steepness
    ).T
    bordered = padded_2(sensitivity, (("space", 1),), R)
    smoothed = smooth(jnp.pad(bordered, ((R, R), (0, 0))), R)
    design_gradient = lax.psum_scatter(smoothed, "exc", scatter_dimension=0, tiled=True)
    return (design_gradient, merits)


def solution(mesh):
    in_specs = (
        P("exc", None, None, "space", None),
        P("exc", None, None, "space", None),
        P("exc", None, None, "space", None),
        P("exc", None, None, "space", None),
        P("exc", None, None, "space"),
        P("exc", "space"),
        P("space", None),
        P("exc"),
        P("exc"),
        P("exc"),
        P("exc"),
        P("exc"),
    )
    out_specs = (P("exc", "space"), P("exc"))
    return jax.shard_map(local, mesh=mesh, in_specs=in_specs, out_specs=out_specs, check_vma=False)
```

profile of v0, /device:TPU:6, one launch (start us, length us, event | category | flops | bytes accessed | tf_op | source)
XLA Modules:
  0.0 285.7 jit_solution(7002441702405182453)
XLA Ops:
  7.2 5.5 %all_gather.3 = f32[1024,8]{0,1:T(8,128)S(1)} all-gather(f32[256,8]{0,1:T(8,128)} %param.19), channel_id=1, replica_groups=mesh['exc'=4,'space'=32] {'exc'}, dimensions={0}, use_global_device_ids=true | all-gather | bytes 40960 | tf_op jit(solution)/shard_map/all_gather | solution.py:142
  12.8 3.8 %collective-permute-start = (f32[1024,4]{0,1:T(4,128)S(1)}, f32[1024,4]{0,1:T(4,128)S(1)}, u32[]{:S(2)}, u32[]{:S(2)}) collective-permute-start(f32[1024,4]{0,1:T(4,128)S(1)} %get-tuple-element.51), channel_id=1, source_target_pairs={{0,1},{1,2},{2,3},{3,4},{4,5},{5,6},{6,7},{7,8},{8,9},{9,10},{10,1... | collective-permute-start | bytes 49160 | tf_op jit(solution)/shard_map/ppermute | solution.py:25
  16.6 6.9 %collective-permute-start.1 = (f32[1024,4]{0,1:T(4,128)S(1)}, f32[1024,4]{0,1:T(4,128)S(1)}, u32[]{:S(2)}, u32[]{:S(2)}) collective-permute-start(f32[1024,4]{0,1:T(4,128)S(1)} %get-tuple-element.52), channel_id=1, source_target_pairs={{1,0},{2,1},{3,2},{4,3},{5,4},{6,5},{7,6},{8,7},{9,8},{10,9},{11,1... | collective-permute-start | bytes 49160 | tf_op jit(solution)/shard_map/ppermute | solution.py:28
  23.6 3.1 %slice_bitcast_fusion.4 = (f32[1,32,8,1024]{3,2,1,0:T(8,128)}, f32[1,32,8,1024]{3,2,1,0:T(8,128)S(1)}, f32[1,32,8,1024]{3,2,1,0:T(8,128)S(1)}) fusion(f32[1,6,32,8,1024]{4,3,2,1,0:T(8,128)} %param.14), kind=kLoop, calls=%fused_computation.92 | loop fusion | bytes 6291456 | tf_op jit(solution)/shard_map/squeeze | solution.py:164
  27.8 3.9 %collective-permute-start.2 = (f32[1,2,32,1024]{3,0,2,1:T(1,128)}, f32[1,2,32,1024]{3,0,2,1:T(1,128)}, u32[]{:S(2)}, u32[]{:S(2)}) collective-permute-start(f32[1,2,32,1024]{3,0,2,1:T(1,128)} %pad_maximum_fusion.8), channel_id=1, source_target_pairs={{1,0},{2,1},{3,2},{4,3},{5,4},{6,5},{7,6},{8,7},{9,8},{10,9},{11,1... | collective-permute-start | bytes 786440 | tf_op jit(solution)/shard_map/ppermute | solution.py:36
  41.2 2.3 slice.615
  53.7 3.6 %bitcast_subtract_fusion.1 = (f32[1,32,8,1024]{3,2,1,0:T(8,128)S(1)}, f32[1,32,8,1024]{3,2,1,0:T(8,128)S(1)}, f32[1,32,8,1024]{3,2,1,0:T(8,128)S(1)}) fusion(f32[1,32,8,1023]{3,2,1,0:T(8,128)S(1)} %slice.621, f32[1,31,8,1024]{3,2,1,0:T(8,128)} %slice.620, f32[1,6,32,8,1024]{4,3,2,1,0:T(8,128)S(1)} %bitcast.288, f32[1,32,1,1024]{3,2,1,0:T(1,128)S(1)} %get-tuple-element.45, ...), kind=kLoop, calls=%fused_computation.85 | loop fusion | flops 4456448 | bytes 15661056 | tf_op jit(solution)/shard_map/sub | solution.py:176
  59.7 3.5 %collective-permute-start.3 = (f32[1,2,32,1024]{3,0,2,1:T(1,128)}, f32[1,2,32,1024]{3,0,2,1:T(1,128)S(1)}, u32[]{:S(2)}, u32[]{:S(2)}) collective-permute-start(f32[1,2,32,1024]{3,0,2,1:T(1,128)} %pad_maximum_fusion.9), channel_id=1, source_target_pairs={{0,1},{1,2},{2,3},{3,4},{4,5},{5,6},{6,7},{7,8},{8,9},{9,10},{10,1... | collective-permute-start | bytes 786440 | tf_op jit(solution)/shard_map/ppermute | solution.py:36
  64.4 3.8 %bitcast_subtract_fusion = (f32[1,32,8,1024]{3,2,1,0:T(8,128)}, f32[1,32,8,1024]{3,2,1,0:T(8,128)S(1)}, f32[1,32,8,1024]{3,2,1,0:T(8,128)S(1)}) fusion(f32[1,32,8,1023]{3,2,1,0:T(8,128)S(1)} %slice.661, f32[1,31,8,1024]{3,2,1,0:T(8,128)} %slice.660, f32[1,6,32,8,1024]{4,3,2,1,0:T(8,128)S(1)} %bitcast.286, f32[1,32,1,1024]{3,2,1,0:T(1,128)S(1)} %get-tuple-element.47, ...), kind=kLoop, calls=%fused_computation.84 | loop fusion | flops 4456448 | bytes 15661056 | tf_op jit(solution)/shard_map/sub | solution.py:176
  71.4 2.3 collective-permute-done.3
  75.6 2.5 fusion.13
  79.0 6.3 %collective-permute-start.4 = (f32[1,2,32,1024]{3,0,2,1:T(1,128)}, f32[1,2,32,1024]{3,0,2,1:T(1,128)}, u32[]{:S(2)}, u32[]{:S(2)}) collective-permute-start(f32[1,2,32,1024]{3,0,2,1:T(1,128)} %pad_maximum_fusion.10), channel_id=1, source_target_pairs={{1,0},{2,1},{3,2},{4,3},{5,4},{6,5},{7,6},{8,7},{9,8},{10,9},{11,1... | collective-permute-start | bytes 786440 | tf_op jit(solution)/shard_map/ppermute | solution.py:36
  86.9 2.5 slice.663
  103.2 5.5 %multiply_subtract_fusion.1 = (f32[1,32,8,1024]{3,2,1,0:T(8,128)S(1)}, f32[1,32,8,1024]{3,2,1,0:T(8,128)S(1)}, f32[1,32,8,1024]{3,2,1,0:T(8,128)S(1)}) fusion(f32[1,32,8,1024]{3,2,1,0:T(8,128)} %copy-done.10, f32[1,32,8,1024]{3,2,1,0:T(8,128)S(1)} %get-tuple-element.10, f32[1,32,8,1023]{3,2,1,0:T(8,128)} %slice.641, f32[1,32,8,1024]{3,2,1,0:T(8,128)} %copy-done, ...), kind=kLoop, calls=%fused_computation.90 | loop fusion | flops 4456448 | bytes 15661056 | tf_op jit(solution)/shard_map/sub | solution.py:176
  111.4 3.8 %fusion.21 = (f32[1,32,8,1024]{3,2,1,0:T(8,128)}, f32[1,32,8,1024]{3,2,1,0:T(8,128)S(1)}) fusion(f32[1,8,8,1024]{3,2,1,0:T(8,128)S(1)} %broadcast_in_dim.18, f32[1,32,8,1024]{3,2,1,0:T(8,128)S(1)} %copy-done.12, f32[1,32,8,1023]{3,2,1,0:T(8,128)S(1)} %bitcast.278, f32[1,32,8,1024]{3,2,1,0:T(8,128)S(1)} %copy-done.3, f32[1,31,8,1024]{3,2,1,0:T(8,128)S(1)} %copy-done.26, ...), kind=kLoop, calls=%fused_computation.24 | loop fusion | flops 3670016 | bytes 11730176 | tf_op jit(solution)/shard_map/add | solution.py:186
  115.2 7.2 %collective-permute-done.5 = f32[1,2,32,1024]{3,0,2,1:T(1,128)S(1)} collective-permute-done((f32[1,2,32,1024]{3,0,2,1:T(1,128)S(1)}, f32[1,2,32,1024]{3,0,2,1:T(1,128)S(1)}, u32[]{:S(2)}, u32[]{:S(2)}) %collective-permute-start.5) | collective-permute-done | bytes 262176 | tf_op jit(solution)/shard_map/ppermute | solution.py:36
  130.6 79.2 %psum.7 = f32[1,2]{1,0:T(1,128)S(1)} all-reduce(f32[1,2]{1,0:T(1,128)S(1)} %pad_maximum_fusion.16), channel_id=1, replica_groups=mesh['exc'=4,'space'=32] {'space'}, use_global_device_ids=true, to_apply=%region_2.4 | all-reduce | flops 2 | bytes 16 | tf_op jit(solution)/shard_map/psum | solution.py:227
  213.6 3.5 %fusion.22 = f32[1,32,8,1024]{3,2,1,0:T(8,128)S(1)} fusion(f32[1,8,8,1024]{3,2,1,0:T(8,128)S(1)} %broadcast_in_dim.18, f32[1,32,8,1024]{3,2,1,0:T(8,128)} %copy-done.2, f32[1,32,7,1024]{3,2,1,0:T(8,128)} %bitcast.273, f32[1,32,1,1024]{3,2,1,0:T(1,128)} %get-tuple-element.40, f32[1,32,8,1024]{3,2,1,0:T(8,128)} %get-tuple-element.17, ...), kind=kLoop, calls=%fused_computation.25 | loop fusion | flops 2883584 | bytes 6557952 | tf_op jit(solution)/shard_map/add | solution.py:189
  217.5 4.0 %collective-permute-start.8 = (f32[1,2,32,1024]{3,0,2,1:T(1,128)S(1)}, f32[1,2,32,1024]{3,0,2,1:T(1,128)S(1)}, u32[]{:S(2)}, u32[]{:S(2)}) collective-permute-start(f32[1,2,32,1024]{3,0,2,1:T(1,128)S(1)} %pad_maximum_fusion.14), channel_id=1, source_target_pairs={{1,0},{2,1},{3,2},{4,3},{5,4},{6,5},{7,6},{8,7},{9,8},{10,9},{11,1... | collective-permute-start | bytes 786440 | tf_op jit(solution)/shard_map/ppermute | solution.py:36
  225.8 3.3 %multiply_subtract_fusion = (f32[1,32,8,1024]{3,2,1,0:T(8,128)S(1)}, f32[1,32,8,1024]{3,2,1,0:T(8,128)S(1)}, f32[1,32,8,1024]{3,2,1,0:T(8,128)S(1)}) fusion(f32[1,32,8,1024]{3,2,1,0:T(8,128)S(1)} %copy-done.9, f32[1,32,8,1024]{3,2,1,0:T(8,128)S(1)} %fusion.22, f32[1,32,8,1023]{3,2,1,0:T(8,128)S(1)} %slice.684, f32[1,32,8,1024]{3,2,1,0:T(8,128)S(1)} %get-tuple-element.8, ...), kind=kLoop, calls=%fused_computation.86 | loop fusion | flops 4456448 | bytes 15661056 | tf_op jit(solution)/shard_map/sub | solution.py:176
  229.6 4.1 %collective-permute-start.9 = (f32[1,2,32,1024]{3,0,2,1:T(1,128)S(1)}, f32[1,2,32,1024]{3,0,2,1:T(1,128)S(1)}, u32[]{:S(2)}, u32[]{:S(2)}) collective-permute-start(f32[1,2,32,1024]{3,0,2,1:T(1,128)S(1)} %pad_maximum_fusion.15), channel_id=1, source_target_pairs={{0,1},{1,2},{2,3},{3,4},{4,5},{5,6},{6,7},{7,8},{8,9},{9,10},{10,1... | collective-permute-start | bytes 786440 | tf_op jit(solution)/shard_map/ppermute | solution.py:36
  235.3 7.2 %collective-permute-done.9 = f32[1,2,32,1024]{3,0,2,1:T(1,128)S(1)} collective-permute-done((f32[1,2,32,1024]{3,0,2,1:T(1,128)S(1)}, f32[1,2,32,1024]{3,0,2,1:T(1,128)S(1)}, u32[]{:S(2)}, u32[]{:S(2)}) %collective-permute-start.9) | collective-permute-done | bytes 262176 | tf_op jit(solution)/shard_map/ppermute | solution.py:36
  248.0 8.4 %collective-permute-start.11 = (f32[1024,4]{0,1:T(4,128)S(1)}, f32[1024,4]{0,1:T(4,128)S(1)}, u32[]{:S(2)}, u32[]{:S(2)}) collective-permute-start(f32[1024,4]{0,1:T(4,128)S(1)} %get-tuple-element.50), channel_id=1, source_target_pairs={{1,0},{2,1},{3,2},{4,3},{5,4},{6,5},{7,6},{8,7},{9,8},{10,9},{11,1... | collective-permute-start | bytes 49160 | tf_op jit(solution)/shard_map/ppermute | solution.py:28
  261.3 16.4 %reduce-scatter.2.cloned.1.call-done = f32[256,8]{0,1:T(8,128)} async-done(((f32[1024,8]{0,1:T(8,128)}), f32[256,8]{0,1:T(8,128)}) %reduce-scatter.2.cloned.1.call-update) | async-done | bytes 8208 | tf_op jit(solution)/shard_map/reduce_scatter | solution.py:244
  (213 shorter events, 67.9 us)
Async XLA Ops:
  7.2 270.5 %reduce-scatter.2.cloned.1.call-start = ((), (), s32[]{:S(2)}) async-start(), calls=%async_computation.1 | async-start | bytes 40960 | tf_op jit(solution)/shard_map/reduce_scatter | solution.py:244
  7.2 24.5 %copy-start.19 = (f32[1,6,32,8,1024]{4,3,2,1,0:T(8,128)S(1)}, f32[1,6,32,8,1024]{4,3,2,1,0:T(8,128)}, u32[]{:S(2)}) copy-start(f32[1,6,32,8,1024]{4,3,2,1,0:T(8,128)} %param.16) | copy-start | bytes 18874372
  12.8 39.0 %collective-permute-start = (f32[1024,4]{0,1:T(4,128)S(1)}, f32[1024,4]{0,1:T(4,128)S(1)}, u32[]{:S(2)}, u32[]{:S(2)}) collective-permute-start(f32[1024,4]{0,1:T(4,128)S(1)} %get-tuple-element.51), channel_id=1, source_target_pairs={{0,1},{1,2},{2,3},{3,4},{4,5},{5,6},{6,7},{7,8},{8,9},{9,10},{10,1... | collective-permute-start | bytes 49160 | tf_op jit(solution)/shard_map/ppermute | solution.py:25
  16.6 23.9 %copy-start.38 = (f32[1,2,32,8]{2,3,1,0:T(8,128)S(1)}, f32[1,2,32,8]{2,3,1,0:T(8,128)}, u32[]{:S(2)}) copy-start(f32[1,2,32,8]{2,3,1,0:T(8,128)} %param.18) | copy-start | bytes 6148
  16.6 35.2 %collective-permute-start.1 = (f32[1024,4]{0,1:T(4,128)S(1)}, f32[1024,4]{0,1:T(4,128)S(1)}, u32[]{:S(2)}, u32[]{:S(2)}) collective-permute-start(f32[1024,4]{0,1:T(4,128)S(1)} %get-tuple-element.52), channel_id=1, source_target_pairs={{1,0},{2,1},{3,2},{4,3},{5,4},{6,5},{7,6},{8,7},{9,8},{10,9},{11,1... | collective-permute-start | bytes 49160 | tf_op jit(solution)/shard_map/ppermute | solution.py:28
  27.8 24.9 %collective-permute-start.2 = (f32[1,2,32,1024]{3,0,2,1:T(1,128)}, f32[1,2,32,1024]{3,0,2,1:T(1,128)}, u32[]{:S(2)}, u32[]{:S(2)}) collective-permute-start(f32[1,2,32,1024]{3,0,2,1:T(1,128)} %pad_maximum_fusion.8), channel_id=1, source_target_pairs={{1,0},{2,1},{3,2},{4,3},{5,4},{6,5},{7,6},{8,7},{9,8},{10,9},{11,1... | collective-permute-start | bytes 786440 | tf_op jit(solution)/shard_map/ppermute | solution.py:36
  35.0 29.3 %collective-permute-start.6 = (f32[1,2,32,1024]{3,0,2,1:T(1,128)}, f32[1,2,32,1024]{3,0,2,1:T(1,128)S(1)}, u32[]{:S(2)}, u32[]{:S(2)}) collective-permute-start(f32[1,2,32,1024]{3,0,2,1:T(1,128)} %pad_maximum_fusion.12), channel_id=1, source_target_pairs={{1,0},{2,1},{3,2},{4,3},{5,4},{6,5},{7,6},{8,7},{9,8},{10,9},{11,1... | collective-permute-start | bytes 786440 | tf_op jit(solution)/shard_map/ppermute | solution.py:36
  51.8 59.6 %copy-start.36 = (f32[32]{0:T(128)}, f32[32]{0:T(128)S(1)}, u32[]{:S(2)}) copy-start(f32[32]{0:T(128)S(1)} %pad.111.clone) | copy-start | bytes 388
  53.7 10.7 %slice-start.1 = ((s8[6291456]{0:T(1024)(128)(4,1)}), s8[4194304]{0:T(1024)(128)(4,1)S(1)}, s32[]{:S(2)}) async-start(s8[6291456]{0:T(1024)(128)(4,1)} %bitcast.285), calls=%async_computation.3 | async-start | bytes 8388608
  57.4 18.2 %copy-start.10 = (f32[1,32,8,1024]{3,2,1,0:T(8,128)}, f32[1,32,8,1024]{3,2,1,0:T(8,128)S(1)}, u32[]{:S(2)}) copy-start(f32[1,32,8,1024]{3,2,1,0:T(8,128)S(1)} %get-tuple-element.11) | copy-start | bytes 3145732
  57.4 18.2 %copy-start.16 = (f32[1,32,8,1024]{3,2,1,0:T(8,128)}, f32[1,32,8,1024]{3,2,1,0:T(8,128)S(1)}, u32[]{:S(2)}) copy-start(f32[1,32,8,1024]{3,2,1,0:T(8,128)S(1)} %get-tuple-element.13) | copy-start | bytes 3145732
  59.7 14.0 %collective-permute-start.3 = (f32[1,2,32,1024]{3,0,2,1:T(1,128)}, f32[1,2,32,1024]{3,0,2,1:T(1,128)S(1)}, u32[]{:S(2)}, u32[]{:S(2)}) collective-permute-start(f32[1,2,32,1024]{3,0,2,1:T(1,128)} %pad_maximum_fusion.9), channel_id=1, source_target_pairs={{0,1},{1,2},{2,3},{3,4},{4,5},{5,6},{6,7},{7,8},{8,9},{9,10},{10,1... | collective-permute-start | bytes 786440 | tf_op jit(solution)/shard_map/ppermute | solution.py:36
  69.4 31.1 %collective-permute-start.7 = (f32[1,2,32,1024]{3,0,2,1:T(1,128)}, f32[1,2,32,1024]{3,0,2,1:T(1,128)}, u32[]{:S(2)}, u32[]{:S(2)}) collective-permute-start(f32[1,2,32,1024]{3,0,2,1:T(1,128)} %pad_maximum_fusion.13), channel_id=1, source_target_pairs={{0,1},{1,2},{2,3},{3,4},{4,5},{5,6},{6,7},{7,8},{8,9},{9,10},{10,1... | collective-permute-start | bytes 786440 | tf_op jit(solution)/shard_map/ppermute | solution.py:36
  75.4 21.1 %copy-start = (f32[1,32,8,1024]{3,2,1,0:T(8,128)}, f32[1,32,8,1024]{3,2,1,0:T(8,128)S(1)}, u32[]{:S(2)}) copy-start(f32[1,32,8,1024]{3,2,1,0:T(8,128)S(1)} %fusion.12) | copy-start | bytes 3145732
  79.0 23.1 %collective-permute-start.4 = (f32[1,2,32,1024]{3,0,2,1:T(1,128)}, f32[1,2,32,1024]{3,0,2,1:T(1,128)}, u32[]{:S(2)}, u32[]{:S(2)}) collective-permute-start(f32[1,2,32,1024]{3,0,2,1:T(1,128)} %pad_maximum_fusion.10), channel_id=1, source_target_pairs={{1,0},{2,1},{3,2},{4,3},{5,4},{6,5},{7,6},{8,7},{9,8},{10,9},{11,1... | collective-permute-start | bytes 786440 | tf_op jit(solution)/shard_map/ppermute | solution.py:36
  108.8 13.7 %copy-start.14 = (f32[1,32,8,1024]{3,2,1,0:T(8,128)}, f32[1,32,8,1024]{3,2,1,0:T(8,128)S(1)}, u32[]{:S(2)}) copy-start(f32[1,32,8,1024]{3,2,1,0:T(8,128)S(1)} %get-tuple-element.32) | copy-start | bytes 3145732
  108.8 13.7 %copy-start.17 = (f32[1,32,8,1024]{3,2,1,0:T(8,128)}, f32[1,32,8,1024]{3,2,1,0:T(8,128)S(1)}, u32[]{:S(2)}) copy-start(f32[1,32,8,1024]{3,2,1,0:T(8,128)S(1)} %get-tuple-element.30) | copy-start | bytes 3145732
  109.3 13.2 %copy-start.35 = (f32[32,8]{1,0:T(8,128)S(1)}, f32[32,8]{1,0:T(8,128)}, u32[]{:S(2)}) copy-start(f32[32,8]{1,0:T(8,128)} %get-tuple-element.57) | copy-start | bytes 3076
  109.3 13.1 %collective-permute-start.5 = (f32[1,2,32,1024]{3,0,2,1:T(1,128)S(1)}, f32[1,2,32,1024]{3,0,2,1:T(1,128)S(1)}, u32[]{:S(2)}, u32[]{:S(2)}) collective-permute-start(f32[1,2,32,1024]{3,0,2,1:T(1,128)S(1)} %pad_maximum_fusion.11), channel_id=1, source_target_pairs={{0,1},{1,2},{2,3},{3,4},{4,5},{5,6},{6,7},{7,8},{8,9},{9,10},{10,1... | collective-permute-start | bytes 786440 | tf_op jit(solution)/shard_map/ppermute | solution.py:36
  209.7 12.8 %copy-start.7 = (f32[1,32,8,1024]{3,2,1,0:T(8,128)S(1)}, f32[1,32,8,1024]{3,2,1,0:T(8,128)}, u32[]{:S(2)}) copy-start(f32[1,32,8,1024]{3,2,1,0:T(8,128)} %get-tuple-element.7) | copy-start | bytes 3145732
  217.5 8.3 %collective-permute-start.8 = (f32[1,2,32,1024]{3,0,2,1:T(1,128)S(1)}, f32[1,2,32,1024]{3,0,2,1:T(1,128)S(1)}, u32[]{:S(2)}, u32[]{:S(2)}) collective-permute-start(f32[1,2,32,1024]{3,0,2,1:T(1,128)S(1)} %pad_maximum_fusion.14), channel_id=1, source_target_pairs={{1,0},{2,1},{3,2},{4,3},{5,4},{6,5},{7,6},{8,7},{9,8},{10,9},{11,1... | collective-permute-start | bytes 786440 | tf_op jit(solution)/shard_map/ppermute | solution.py:36
  229.6 12.9 %collective-permute-start.9 = (f32[1,2,32,1024]{3,0,2,1:T(1,128)S(1)}, f32[1,2,32,1024]{3,0,2,1:T(1,128)S(1)}, u32[]{:S(2)}, u32[]{:S(2)}) collective-permute-start(f32[1,2,32,1024]{3,0,2,1:T(1,128)S(1)} %pad_maximum_fusion.15), channel_id=1, source_target_pairs={{0,1},{1,2},{2,3},{3,4},{4,5},{5,6},{6,7},{7,8},{8,9},{9,10},{10,1... | collective-permute-start | bytes 786440 | tf_op jit(solution)/shard_map/ppermute | solution.py:36
  246.1 10.4 %collective-permute-start.10 = (f32[1024,4]{0,1:T(4,128)S(1)}, f32[1024,4]{0,1:T(4,128)S(1)}, u32[]{:S(2)}, u32[]{:S(2)}) collective-permute-start(f32[1024,4]{0,1:T(4,128)S(1)} %get-tuple-element.49), channel_id=1, source_target_pairs={{0,1},{1,2},{2,3},{3,4},{4,5},{5,6},{6,7},{7,8},{8,9},{9,10},{10,1... | collective-permute-start | bytes 49160 | tf_op jit(solution)/shard_map/ppermute | solution.py:25
  248.0 9.9 %collective-permute-start.11 = (f32[1024,4]{0,1:T(4,128)S(1)}, f32[1024,4]{0,1:T(4,128)S(1)}, u32[]{:S(2)}, u32[]{:S(2)}) collective-permute-start(f32[1024,4]{0,1:T(4,128)S(1)} %get-tuple-element.50), channel_id=1, source_target_pairs={{1,0},{2,1},{3,2},{4,3},{5,4},{6,5},{7,6},{8,7},{9,8},{10,9},{11,1... | collective-permute-start | bytes 49160 | tf_op jit(solution)/shard_map/ppermute | solution.py:28
  (35 other events, 211.4 us)
Sparse Core Ops, SparseCore 0:
  258.9 18.7 reduce-scatter.1
where the time goes:
time: 288 us; the launch traced here: 286 us
  blocking collectives  84.7 us (29%)
  starting transfers between devices  49.3 us (17%)
  local copies, waits for them, and re-layouts  46.2 us (16%)
  other arithmetic  45 us (16%)
  waiting for transfers between devices  35.5 us (12%)
  between operations  25 us (9%)
    psum x1, blocking collectives, local(): lax.psum(partial_value, 'space') / math.sqrt(layer_count * grid_rows)  79.2 us
    ppermute x8, starting transfers between devices, passed_along(): return lax.ppermute(block, axis, route)  28.1 us
    ppermute x8, waiting for transfers between devices, passed_along(): return lax.ppermute(block, axis, route)  17.7 us
    reduce_scatter x1, waiting for transfers between devices, local(): lax.psum_scatter(smoothed, 'exc', scatter_dimension=0, tiled=True)  16.4 us
    sub x4, other arithmetic, advance(): magnetic_y - COURANT * (upward(electric_x, 1) - upward(electric_z, 3))  16.2 us
    ppermute x2, starting transfers between devices, padded_2(): lax.ppermute(lax.slice_in_dim(block, 0, width, axis=dim), axis, backward)  15.4 us
    slice x17, local copies, waits for them, and re-layouts, upward(): lax.slice_in_dim(field, 1, size, axis=axis)  14.6 us
    slice x8, local copies, waits for them, and re-layouts, downward(): lax.slice_in_dim(field, 0, size - 1, axis=axis)  7.39 us
  transfers between devices with their start and end apart: 13, of which 6 were waited for; matrix products, arithmetic and copies ran while one was open for 22% of the time, Pallas kernels for 0%

commit v1 on v0

v1 whole, which is shorter than its diff:
```python
import math

import jax
import jax.numpy as jnp
from jax import lax
from jax.experimental import pallas as pl
from jax.experimental.pallas import tpu as pltpu
from jax.sharding import PartitionSpec as P

R = 4
COURANT = 0.5
OXIDE = 2.1
SILICON = 12.1
SHARPNESS = 4.0
MIDPOINT = 0.5

ROWS = 8
NX = 1024
NZ = 32
SLAB = 12
DZ = 8
UP_ROWS = 64
DOWN_ROWS = 40
PACK = 16 + 2 * UP_ROWS
WEIGHTS = [(R + 1.0 - abs(k - R)) / ((R + 1.0) * (R + 1.0)) for k in range(2 * R + 1)]
VMEM_LIMIT = 50 * 1024 * 1024

SMEM_SPEC = pl.BlockSpec(memory_space=pltpu.SMEM)
VMEM_SPEC = pl.BlockSpec(memory_space=pltpu.VMEM)
ANY_SPEC = pl.BlockSpec(memory_space=pl.ANY)


def slot(z):
    return (z - SLAB) % 16


def lanes(shape):
    return lax.broadcasted_iota(jnp.int32, shape, len(shape) - 1)


def sublanes(shape):
    return lax.broadcasted_iota(jnp.int32, shape, len(shape) - 2)


def x_up(f):
    n = f.shape[-1]
    return jnp.where(lanes(f.shape) == n - 1, 0.0, pltpu.roll(f, n - 1, len(f.shape) - 1))


def x_down(f):
    return jnp.where(lanes(f.shape) == 0, 0.0, pltpu.roll(f, 1, len(f.shape) - 1))


def roll_up(f):
    return pltpu.roll(f, f.shape[0] - 1, 0)


def roll_down(f):
    return pltpu.roll(f, 1, 0)


def y_smooth(f, count):
    total = None
    for k, w in enumerate(WEIGHTS):
        part = w * f[k : k + count]
        total = part if total is None else total + part
    return total


def x_smooth(f):
    n = f.shape[-1]
    ids = lanes(f.shape)
    total = WEIGHTS[R] * f
    for a in range(1, R + 1):
        ahead = jnp.where(ids < n - a, pltpu.roll(f, n - a, 1), 0.0)
        behind = jnp.where(ids >= a, pltpu.roll(f, a, 1), 0.0)
        total = total + WEIGHTS[R + a] * (ahead + behind)
    return total


def pack_kernel(ip, ff, af, dens, lab, ev, od, rows, up, down, sem, out_sem):
    copies = []
    for p, f in enumerate((ff, af)):
        for k, r in enumerate((0, 1, 6, 7)):
            copies.append(pltpu.make_async_copy(f.at[0, :, 8:24, r, :], rows.at[p, k], sem.at[p, k]))
    for c in copies:
        c.start()
    own = lab[...].astype(jnp.float32)
    up[0:8] = dens[...]
    up[8:16] = own
    down[0:8] = dens[...]
    down[8:16] = own
    tile = sublanes((8, NX))
    for p in range(2):
        for k in range(4):
            copies[4 * p + k].wait()

        def row(k, c, p=p):
            return pltpu.roll(rows[p, k, c], 12, 0)

        ex, ey, ez = row(0, 0), row(0, 1), row(0, 2)
        ex_n, ez_n = row(1, 0), row(1, 2)
        hx = row(0, 3) - COURANT * ((ez_n - ez) - (roll_up(ey) - ey))
        hy = row(0, 4) - COURANT * ((roll_up(ex) - ex) - (x_up(ez) - ez))
        hz = row(0, 5) - COURANT * ((x_up(ey) - ey) - (ex_n - ex))
        cx = hz - (hy - roll_down(hy))
        cz = (hy - x_down(hy)) - hx
        base = 16 + p * DOWN_ROWS
        down[base : base + 8] = ex[0:8]
        down[base + 8 : base + 16] = ez[0:8]
        down[base + 16 : base + 24] = cx[0:8]
        down[base + 24 : base + 32] = cz[0:8]
        extra = jnp.where((tile == 1) | (tile == 2), pltpu.roll(ex[8:16], 2, 0), ez[8:16])
        down[base + 32 : base + 40] = jnp.where(tile == 3, pltpu.roll(cz[8:16], 4, 0), extra)

        ex_l, ey_l, ez_l = row(2, 0), row(2, 1), row(2, 2)
        ex, ey, ez = row(3, 0), row(3, 1), row(3, 2)
        u1 = (x_up(ey) - ey) + ex
        u2 = ez + (roll_up(ey) - ey)
        hx = row(3, 3) + COURANT * u2
        hy = row(3, 4) - COURANT * ((roll_up(ex) - ex) - (x_up(ez) - ez))
        hz = row(3, 5) - COURANT * u1
        hx_l = row(2, 3) - COURANT * ((ez - ez_l) - (roll_up(ey_l) - ey_l))
        hz_l = row(2, 5) - COURANT * ((x_up(ey_l) - ey_l) - (ex - ex_l))
        cx = (hz - hz_l) - (hy - roll_down(hy))
        cy = (hx - roll_down(hx)) - (hz - x_down(hz))
        cz = (hy - x_down(hy)) - (hx - hx_l)
        base = 16 + p * UP_ROWS
        for k, v in enumerate((hx, hz, u1, u2, cx, cy, cz)):
            up[base + 8 * k : base + 8 * k + 8] = v[0:8]
        extra = jnp.where((tile == 1) | (tile == 2), pltpu.roll(hz[8:16], 2, 0), hx[8:16])
        up[base + 56 : base + 64] = jnp.where(tile == 3, pltpu.roll(cy[8:16], 3, 0), extra)

    even = ip[0] % 2 == 0

    def send(to_up, to_down):
        a = pltpu.make_async_copy(up, to_up, out_sem.at[0])
        b = pltpu.make_async_copy(down, to_down.at[0 : 16 + 2 * DOWN_ROWS], out_sem.at[1])
        a.start()
        b.start()
        a.wait()
        b.wait()

    @pl.when(even)
    def _():
        send(ev, od)

    @pl.when(jnp.logical_not(even))
    def _():
        send(od, ev)


def from_neighbours(ip, ev, od, below, above, below_rows, above_rows, sem):
    even = ip[0] % 2 == 0

    def get(from_below, from_above):
        a = pltpu.make_async_copy(from_below.at[below_rows], below, sem.at[0])
        b = pltpu.make_async_copy(from_above.at[above_rows], above, sem.at[1])
        a.start()
        b.start()
        a.wait()
        b.wait()

    @pl.when(even)
    def _():
        get(od, ev)

    @pl.when(jnp.logical_not(even))
    def _():
        get(ev, od)


def cyclic_rows(shape):
    i = sublanes(shape)
    return jnp.where(i < 12, i, i - 16)


def window_start(first):
    return pl.multiple_of(jnp.clip((first // 128) * 128, 0, NX - 256), 128)


def layer_inverse(z, middle):
    if z < SLAB:
        return 1.0 / OXIDE
    if z >= SLAB + DZ:
        return 1.0
    return middle


def material_kernel(
    grid_rows, ip, fp, ev, od, dens, lab, monitor, shape_zy, ff, inv_out, design_out, part_out,
    below, above, fw, sem, win_sem,
):
    strip, plane = ip[0], ip[1]
    w0 = window_start(plane - 2)
    window = pltpu.make_async_copy(ff.at[0, :, :, :, pl.ds(w0, 256)], fw, win_sem)
    window.start()
    from_neighbours(ip, ev, od, below, above, pl.ds(0, 16), pl.ds(0, 16), sem)
    own = lab[...].astype(jnp.float32)
    wide = jnp.concatenate([below[0:8], dens[...], above[0:8]], 0)
    kinds = jnp.concatenate([below[8:16], own, above[8:16]], 0)[4:20]
    filtered = x_smooth(y_smooth(wide, 16))
    lower = math.tanh(SHARPNESS * MIDPOINT)
    spread = lower + math.tanh(SHARPNESS * (1.0 - MIDPOINT))
    bent = jnp.tanh(SHARPNESS * (filtered - MIDPOINT))
    projected = (lower + bent) / spread
    steepness = SHARPNESS * (1.0 - bent * bent) / spread
    mixed = OXIDE + (SILICON - OXIDE) * projected
    material = jnp.where(kinds == 2.0, mixed, jnp.where(kinds == 1.0, SILICON, OXIDE))
    inv_out[...] = pltpu.roll(1.0 / material, 12, 0)
    design = jnp.where(kinds == 2.0, steepness * fp[36], 0.0)
    design_out[...] = pltpu.roll(design, 12, 0)[0:8]

    small = (16, 128)
    shift = (64 + w0 - plane + 256) % 256
    middle = pltpu.roll(inv_out[:, pl.ds(w0, 256)], shift, 1)[:, 0:128]
    rows_here = cyclic_rows(small) + ROWS * strip
    xs = lanes(small) + (plane - 64)
    inside = (rows_here >= 0) & (rows_here < grid_rows) & (xs >= 0) & (xs < NX)
    mask = jnp.where(inside, 1.0, 0.0)
    half = COURANT * mask
    ramp = 1.0 + 2.0 * (rows_here.astype(jnp.float32) + 0.5) / grid_rows
    seed_base = jnp.where(lanes(small) == 64, ramp * mask, 0.0)
    source_base = jnp.where(lanes(small) == 64, ramp, 0.0)[0:8]
    zero = jnp.zeros(small, jnp.float32)

    def at(values, z):
        return values[z] if 0 <= z < NZ else zero

    def xu(v):
        return pltpu.roll(v, 127, 1)

    def xd(v):
        return pltpu.roll(v, 1, 1)

    zs = range(NZ)
    inv = [layer_inverse(z, middle) for z in zs]
    seed = [seed_base * fp[z] for z in zs]
    w = [inv[z] * seed[z] for z in zs]
    hx = [half * (roll_up(w[z]) - w[z]) for z in zs]
    hy = [half * (w[z] - xu(w[z])) for z in zs]
    ex = [half * (hy[z] - at(hy, z - 1)) for z in zs]
    ey = [half * (at(hx, z - 1) - hx[z]) for z in zs]
    ez = [
        (seed[z] - COURANT * ((hy[z] - xd(hy[z])) - (hx[z] - roll_down(hx[z])))) * mask for z in zs
    ]
    wx = [inv[z] * ex[z] for z in zs]
    wy = [inv[z] * ey[z] for z in zs]
    wz = [inv[z] * ez[z] for z in zs]
    hx2 = [hx[z] + half * ((roll_up(wz[z]) - wz[z]) - (at(wy, z + 1) - wy[z])) for z in zs]
    hy2 = [hy[z] + half * ((at(wx, z + 1) - wx[z]) - (xu(wz[z]) - wz[z])) for z in zs]
    hz2 = [half * ((xu(wy[z]) - wy[z]) - (roll_up(wx[z]) - wx[z])) for z in zs]
    window.wait()
    one = jnp.zeros((8, 128), jnp.float32)
    two = jnp.zeros((8, 128), jnp.float32)
    c0, s0, c1, s1 = fp[32], fp[33], fp[34], fp[35]
    for z in zs:
        ex2 = ex[z] - half * (
            (hz2[z] - roll_down(hz2[z])) - (hy2[z] - at(hy2, z - 1))
        )
        ey2 = ey[z] - half * ((hx2[z] - at(hx2, z - 1)) - (hz2[z] - xd(hz2[z])))
        ez2 = ez[z] - half * ((hy2[z] - xd(hy2[z])) - (hx2[z] - roll_down(hx2[z])))
        f = [pltpu.roll(fw[c, z], shift, 1)[:, 0:128] for c in range(6)]
        one += ex[z][0:8] * f[0] + ey[z][0:8] * f[1] + ez[z][0:8] * f[2]
        one += hx[z][0:8] * f[3] + hy[z][0:8] * f[4]
        two += ex2[0:8] * f[0] + ey2[0:8] * f[1] + ez2[0:8] * f[2]
        two += hx2[z][0:8] * f[3] + hy2[z][0:8] * f[4] + hz2[z][0:8] * f[5]
        pulse = source_base * (COURANT * fp[z])
        one -= pulse * (w[z][0:8] * c0)
        two -= pulse * (wz[z][0:8] * c0 + w[z][0:8] * c1)
    first, second = jnp.sum(one), jnp.sum(two)
    real = jnp.sum(monitor[0, 0] * shape_zy[...]) + c0 * first + c1 * second
    imaginary = jnp.sum(monitor[0, 1] * shape_zy[...]) - s0 * first - s1 * second
    ids = lanes((8, 128))
    part_out[...] = jnp.where(ids == 0, real, jnp.where(ids == 1, imaginary, 0.0))


def main_kernel(
    strips, grid_rows, ip, fp, ev, od, ff, fs, af, asums, inv_ref, design,
    ev_out, od_out, s_out, p_out,
    field, sums, below, above, hmx, hmz, hmx2, hmz2, ezp, exp, pscr, sem, halo_sem,
):
    strip, source, plane = ip[0], ip[1], ip[2]
    c0, s0, c1, s1 = fp[32], fp[33], fp[34], fp[35]
    copies = []
    for p, f in enumerate((ff, af)):
        copies.append(
            (
                pltpu.make_async_copy(f.at[0, :, 12:24], field.at[p, :, 0:12], sem.at[p, 0]),
                pltpu.make_async_copy(f.at[0, :, 8:12], field.at[p, :, 12:16], sem.at[p, 1]),
            )
        )
    sum_copies = [
        pltpu.make_async_copy(f.at[0], sums.at[p], sem.at[p, 2]) for p, f in enumerate((fs, asums))
    ]
    for p in range(2):
        copies[p][0].start()
        copies[p][1].start()
        sum_copies[p].start()
    from_neighbours(
        ip, ev, od, below, above, pl.ds(16, 2 * UP_ROWS), pl.ds(16, 2 * DOWN_ROWS), halo_sem
    )
    full = (8, NX)
    row_ids = sublanes(full)
    ids = lanes(full)
    first_row, last_row = row_ids == 0, row_ids == 7
    has_below = jnp.where(strip > 0, 1.0, 0.0)
    has_above = jnp.where(strip < strips - 1, 1.0, 0.0)
    base_row = (ROWS * strip).astype(jnp.float32)
    step = 2.0 / grid_rows
    ramp = 1.0 + step * (base_row + row_ids.astype(jnp.float32) + 0.5)
    pulse = jnp.where(ids == source, ramp, 0.0)
    sine_rows = jnp.zeros(full, jnp.float32)
    for k in range(8):
        sine_rows = jnp.where(row_ids == k, fp[SLAB + k], sine_rows)
    sine_rows = jnp.where(ids == source, sine_rows, 0.0)
    ramp_above = 1.0 + step * (base_row + 8.5)
    ramp_below = 1.0 + step * (base_row - 0.5)
    inv_below = inv_ref[15:16]
    inv_above = inv_ref[8:9]

    def y_up(f, halo):
        return jnp.where(last_row, halo, roll_up(f))

    def y_down(f, halo):
        return jnp.where(first_row, halo, roll_down(f))

    for p in range(2):
        up0 = p * UP_ROWS
        down0 = p * DOWN_ROWS
        forward = p == 0

        def get(c, z, p=p):
            return field[p, c, slot(z)]

        def strip_row(c, r, p=p):
            return field[p, c, :, r, :]

        copies[p][0].wait()
        copies[p][1].wait()

        def ex0_above(z):
            k = down0 + z - SLAB if 12 <= z <= 19 else down0 + 32 + {20: 2, 11: 1}[z]
            return above[k : k + 1]

        def ez0_above(z):
            k = down0 + 8 + z - SLAB if 12 <= z <= 19 else down0 + 32 + {20: 0, 11: 7, 10: 6}[z]
            return above[k : k + 1]

        for z in range(10, 21):
            ex, ey, ez = get(0, z), get(1, z), get(2, z)
            hx = get(3, z) - COURANT * ((y_up(ez, ez0_above(z)) - ez) - (get(1, z + 1) - ey))
            hy = get(4, z) - COURANT * ((get(0, z + 1) - ex) - (x_up(ez) - ez))
            field[p, 3, slot(z)] = hx
            field[p, 4, slot(z)] = hy
            if z > 10:
                hz = get(5, z) - COURANT * ((x_up(ey) - ey) - (y_up(ex, ex0_above(z)) - ex))
                field[p, 5, slot(z)] = hz
        dhx = -COURANT * strip_row(2, 0)
        dhz = COURANT * strip_row(0, 0)
        block = [below[up0 + 8 * k : up0 + 8 * k + 8] for k in range(8)]
        extra = block[7]
        hmx[0:8] = has_below * (block[0] + dhx[0:8])
        hmx[8:16] = has_below * (extra + dhx[8:16])
        hmz[0:8] = has_below * (block[1] + dhz[0:8])
        hmz[8:16] = has_below * (pltpu.roll(extra, 6, 0) + dhz[8:16])
        cx = block[4] + dhz[0:8]
        cy = jnp.concatenate([block[5], pltpu.roll(extra, 5, 0)], 0)
        cy = cy + (dhx - roll_down(dhx)) - (dhz - x_down(dhz))
        cz = block[6] - dhx[0:8]
        if forward:
            cz = cz - sine_rows * (c0 * ramp_below)
        both = jnp.concatenate([cy[0:8] * inv_below, cy[8:16]], 0)
        t1 = block[2] + COURANT * ((x_up(both[0:8]) - both[0:8]) + inv_below * cx)
        t2 = block[3] + COURANT * (inv_below * cz + (roll_up(both) - both)[0:8])
        hx7, hz7 = strip_row(3, 7), strip_row(5, 7)
        ab = [above[down0 + 8 * k : down0 + 8 * k + 8] for k in range(5)]
        exp[...] = has_above * (ab[0] + COURANT * inv_above * (ab[2] - hz7[0:8]))
        drive = ab[3] + hx7[0:8]
        if forward:
            drive = drive - sine_rows * (c0 * ramp_above)
        ezp[0:8] = has_above * (ab[1] + COURANT * inv_above * drive)
        drive = ab[4][3:4] + hx7[15:16]
        if forward:
            here = lanes((1, NX)) == source
            drive = drive - jnp.where(here, fp[11] * (c0 * ramp_above), 0.0)
        ezp[15:16] = has_above * (ab[4][7:8] + (COURANT / OXIDE) * drive)
        for z in range(11, 21):
            k = slot(z)
            scale = COURANT * layer_inverse(z, inv_ref[0:8])
            hx, hy, hz = get(3, z), get(4, z), get(5, z)
            ex = get(0, z) + scale * ((hz - y_down(hz, hmz[k : k + 1])) - (hy - get(4, z - 1)))
            ey = get(1, z) + scale * ((hx - get(3, z - 1)) - (hz - x_down(hz)))
            field[p, 0, k] = ex
            field[p, 1, k] = ey
            if z < 20:
                curl = (hy - x_down(hy)) - (hx - y_down(hx, hmx[k : k + 1]))
                if forward:
                    curl = curl - pulse * (fp[z] * c0)
                field[p, 2, k] = get(2, z) + scale * curl
        hmx2[...] = has_below * (hmx[0:8] - COURANT * (strip_row(2, 0)[0:8] - t2))
        hmz2[...] = has_below * (hmz[0:8] - COURANT * (t1 - strip_row(0, 0)[0:8]))
        for z in range(11, 20):
            k = slot(z)
            ex, ey, ez = get(0, z), get(1, z), get(2, z)
            field[p, 3, k] = get(3, z) - COURANT * (
                (y_up(ez, ezp[k : k + 1]) - ez) - (get(1, z + 1) - ey)
            )
            field[p, 4, k] = get(4, z) - COURANT * ((get(0, z + 1) - ex) - (x_up(ez) - ez))
            if z > 11:
                field[p, 5, k] = get(5, z) - COURANT * (
                    (x_up(ey) - ey) - (y_up(ex, exp[k : k + 1]) - ex)
                )
        sum_copies[p].wait()
        scale = COURANT * inv_ref[0:8]
        total = jnp.zeros(full, jnp.float32)
        for z in range(12, 20):
            k = slot(z)
            hx, hy, hz = get(3, z), get(4, z), get(5, z)
            curl_z = (hy - x_down(hy)) - (hx - y_down(hx, hmx2[k : k + 1]))
            if forward:
                curl_z = curl_z - pulse * (fp[z] * c1)
            curls = (
                (hz - y_down(hz, hmz2[k : k + 1])) - (hy - get(4, z - 1)),
                (hx - get(3, z - 1)) - (hz - x_down(hz)),
                curl_z,
            )
            for c in range(3):
                early = get(c, z)
                late = early + scale * curls[c]
                real = sums[p, c, k] + c0 * early + c1 * late
                imaginary = sums[p, 3 + c, k] - s0 * early - s1 * late
                if forward:
                    sums[0, c, k] = real
                    sums[0, 3 + c, k] = imaginary
                else:
                    total = total + (sums[0, c, k] * real - sums[0, 3 + c, k] * imaginary)

    w1 = window_start(plane - 1)
    wide = (16, 256)
    rows_here = cyclic_rows(wide) + ROWS * strip
    valid = (rows_here >= 0) & (rows_here < grid_rows)
    keep = jnp.where(valid, 1.0, 0.0)
    ramps = 1.0 + step * (rows_here.astype(jnp.float32) + 0.5)
    spot = jnp.where(valid & (lanes(wide) + w1 == plane), ramps, 0.0)
    inv_w = inv_ref[:, pl.ds(w1, 256)]
    own_scale = COURANT * inv_w[0:8]
    drive_0 = jnp.zeros((8, 256), jnp.float32)
    drive_1 = jnp.zeros((8, 256), jnp.float32)
    hx_last = hy_last = None
    for z in range(11, 20):
        d1 = spot * layer_inverse(z, inv_w) * (-COURANT * fp[z])
        hy = COURANT * (x_up(d1[0:8]) - d1[0:8])
        hx = keep * (-COURANT * (roll_up(d1) - d1))
        if z > 11:
            k = slot(z)
            e1z = d1[0:8]
            e2x = own_scale * (hy_last - hy)
            e2y = own_scale * (hx - hx_last)[0:8]
            e2z = e1z + own_scale * ((hy - x_down(hy)) - (hx - roll_down(hx))[0:8])
            part = [sums[0, c, k, :, pl.ds(w1, 256)] for c in range(6)]
            drive_0 += (c1 * part[0] + s1 * part[3]) * e2x
            drive_0 += (c1 * part[1] + s1 * part[4]) * e2y
            late = c1 * part[2] + s1 * part[5]
            drive_0 += (c0 * part[2] + s0 * part[5]) * e1z + late * e2z
            drive_1 += late * e1z
        hx_last, hy_last = hx, hy
    design_w = design[:, pl.ds(w1, 256)]
    s_own = total * design[...]
    pscr[:, 0:256] = drive_0 * design_w
    pscr[:, 256:512] = drive_1 * design_w
    pscr[:, 512:1024] = jnp.zeros((8, 512), jnp.float32)
    p_own = pscr[...]
    s_out[...] = s_own
    p_out[...] = p_own
    top = row_ids < 4
    to_up = jnp.where(top, pltpu.roll(s_own, 4, 0), p_own)
    to_down = jnp.where(top, s_own, pltpu.roll(p_own, 4, 0))
    even = strip % 2 == 0
    ev_out[...] = jnp.where(even, to_up, to_down)
    od_out[...] = jnp.where(even, to_down, to_up)


def final_kernel(norm, ip, fp, ev, od, s_own, p_own, totals, keep, send, scr):
    strip, plane, group = ip[0], ip[2], ip[3]
    even = strip % 2 == 0
    low = jnp.where(even, od[...], ev[...])
    high = jnp.where(even, ev[...], od[...])
    both = jnp.concatenate([low[0:4], s_own[...], high[0:4]], 0)
    extra = jnp.concatenate([low[4:8, 0:512], p_own[:, 0:512], high[4:8, 0:512]], 0)
    real = totals[0, 0] / norm
    imaginary = totals[0, 1] / norm
    g0 = real * fp[32] + imaginary * fp[33]
    g1 = real * fp[34] + imaginary * fp[35]
    more = y_smooth(extra, 8)
    w1 = window_start(plane - 1)
    scr[...] = y_smooth(both, 8)
    scr[:, pl.ds(w1, 256)] += g0 * more[:, 0:256] + g1 * more[:, 256:512]
    result = x_smooth(scr[...])
    count = keep.shape[0]
    width = NX // (2 * count)

    def split(mine):
        for k in range(count):
            a = (2 * k + mine) * width
            b = (2 * k + 1 - mine) * width
            keep[k] = result[:, a : a + width]
            send[k] = result[:, b : b + width]

    @pl.when(group % 2 == 0)
    def _():
        split(0)

    @pl.when(group % 2 == 1)
    def _():
        split(1)


def params(limit=VMEM_LIMIT):
    return pltpu.CompilerParams(vmem_limit_bytes=limit)


def swap(value, axis, pairs):
    return lax.ppermute(value, axis, pairs)


def local(
    forward_fields, forward_sums, adjoint_fields, adjoint_sums, monitor_sums, density, labels,
    source_plane, monitor_plane, mode_numbers, frequency, start_phase,
):
    groups = lax.axis_size("exc")
    strips = lax.axis_size("space")
    grid_rows = ROWS * strips
    strip = lax.axis_index("space").astype(jnp.int32)
    group = lax.axis_index("exc").astype(jnp.int32)
    f32 = jnp.float32

    def shaped(*shape):
        return jax.ShapeDtypeStruct(shape, f32)

    even_pairs = [(i, i ^ 1) for i in range(strips)]
    odd_pairs = [(i, ((i - 1) ^ 1) + 1) for i in range(1, strips - 1)]

    ip = jnp.stack([strip, source_plane[0], monitor_plane[0], group])
    layers = jnp.arange(NZ, dtype=f32) + 0.5
    sines = jnp.sin(math.pi * (mode_numbers[0] + 1).astype(f32) * layers / NZ)
    phases = start_phase[0] + frequency[0] * jnp.arange(2, dtype=f32)
    cosines, phase_sines = jnp.cos(phases), jnp.sin(phases)
    factor = frequency[0] * frequency[0] * ((SILICON - OXIDE) / math.sqrt(groups * DZ))
    fp = jnp.concatenate(
        [sines, jnp.stack([cosines[0], phase_sines[0], cosines[1], phase_sines[1], factor])]
    )
    own_rows = (strip * ROWS + jnp.arange(ROWS, dtype=jnp.int32)).astype(f32)
    shape_zy = sines[:, None] * (1.0 + 2.0 * (own_rows + 0.5) / grid_rows)[None, :]

    dens = lax.all_gather(density.T, "exc", axis=1, tiled=True)

    ev, od = pl.pallas_call(
        pack_kernel,
        out_shape=[shaped(PACK, NX), shaped(PACK, NX)],
        in_specs=[SMEM_SPEC, ANY_SPEC, ANY_SPEC, VMEM_SPEC, VMEM_SPEC],
        out_specs=[ANY_SPEC, ANY_SPEC],
        scratch_shapes=[
            pltpu.VMEM((2, 4, 6, 16, NX), f32),
            pltpu.VMEM((PACK, NX), f32),
            pltpu.VMEM((16 + 2 * DOWN_ROWS, NX), f32),
            pltpu.SemaphoreType.DMA((2, 4)),
            pltpu.SemaphoreType.DMA((2,)),
        ],
        compiler_params=params(),
        name="pack",
    )(ip, forward_fields, adjoint_fields, dens, labels)
    ev = swap(ev, "space", even_pairs)
    od = swap(od, "space", odd_pairs)

    def material(*refs):
        material_kernel(grid_rows, *refs)

    inv, design, part = pl.pallas_call(
        material,
        out_shape=[shaped(16, NX), shaped(8, NX), shaped(8, 128)],
        in_specs=[SMEM_SPEC, SMEM_SPEC, ANY_SPEC, ANY_SPEC] + [VMEM_SPEC] * 4 + [ANY_SPEC],
        out_specs=[VMEM_SPEC] * 3,
        scratch_shapes=[
            pltpu.VMEM((16, NX), f32),
            pltpu.VMEM((16, NX), f32),
            pltpu.VMEM((6, NZ, ROWS, 256), f32),
            pltpu.SemaphoreType.DMA((2,)),
            pltpu.SemaphoreType.DMA,
        ],
        compiler_params=params(),
        name="material",
    )(ip, fp, ev, od, dens, labels, monitor_sums, shape_zy, forward_fields)

    totals = part[0:1]
    bit = 1
    while bit < strips:
        totals = totals + swap(totals, "space", [(i, i ^ bit) for i in range(strips)])
        bit *= 2

    def main(*refs):
        main_kernel(strips, grid_rows, *refs)

    ev3, od3, s_own, p_own = pl.pallas_call(
        main,
        out_shape=[shaped(8, NX)] * 4,
        in_specs=[SMEM_SPEC, SMEM_SPEC] + [ANY_SPEC] * 6 + [VMEM_SPEC] * 2,
        out_specs=[VMEM_SPEC] * 4,
        scratch_shapes=[
            pltpu.VMEM((2, 6, 16, ROWS, NX), f32),
            pltpu.VMEM((2, 6, DZ, ROWS, NX), f32),
            pltpu.VMEM((2 * UP_ROWS, NX), f32),
            pltpu.VMEM((2 * DOWN_ROWS, NX), f32),
            pltpu.VMEM((16, NX), f32),
            pltpu.VMEM((16, NX), f32),
            pltpu.VMEM((8, NX), f32),
            pltpu.VMEM((8, NX), f32),
            pltpu.VMEM((16, NX), f32),
            pltpu.VMEM((8, NX), f32),
            pltpu.VMEM((8, NX), f32),
            pltpu.SemaphoreType.DMA((2, 3)),
            pltpu.SemaphoreType.DMA((2,)),
        ],
        compiler_params=params(),
        name="main",
    )(ip, fp, ev, od, forward_fields, forward_sums, adjoint_fields, adjoint_sums, inv, design)
    ev3 = swap(ev3, "space", even_pairs)
    od3 = swap(od3, "space", odd_pairs)

    norm = math.sqrt(NZ * grid_rows)
    half_count = groups // 2

    def final(*refs):
        final_kernel(norm, *refs)

    width = NX // groups
    keep, send = pl.pallas_call(
        final,
        out_shape=[shaped(half_count, ROWS, width)] * 2,
        in_specs=[SMEM_SPEC, SMEM_SPEC] + [VMEM_SPEC] * 4 + [SMEM_SPEC],
        out_specs=[VMEM_SPEC] * 2,
        scratch_shapes=[pltpu.VMEM((8, NX), f32)],
        compiler_params=params(),
        name="final",
    )(ip, fp, ev3, od3, s_own, p_own, totals)
    block = keep + swap(send, "exc", [(i, i ^ 1) for i in range(groups)])
    bit = 2
    while bit < groups:
        count = block.shape[0] // 2
        pairs = block.reshape(count, 2, ROWS, width)
        mine = (group // bit) % 2
        kept = lax.dynamic_index_in_dim(pairs, mine, 1, keepdims=False)
        given = lax.dynamic_index_in_dim(pairs, 1 - mine, 1, keepdims=False)
        block = kept + swap(given, "exc", [(i, i ^ bit) for i in range(groups)])
        bit *= 2
    real, imaginary = totals[0, 0:1] / norm, totals[0, 1:2] / norm
    return block[0].T, real * real + imaginary * imaginary


def solution(mesh):
    in_specs = (
        P("exc", None, None, "space", None),
        P("exc", None, None, "space", None),
        P("exc", None, None, "space", None),
        P("exc", None, None, "space", None),
        P("exc", None, None, "space"),
        P("exc", "space"),
        P("space", None),
        P("exc"),
        P("exc"),
        P("exc"),
        P("exc"),
        P("exc"),
    )
    out_specs = (P("exc", "space"), P("exc"))
    return jax.shard_map(local, mesh=mesh, in_specs=in_specs, out_specs=out_specs, check_vma=False)
```

time: 288 us -> 80.5 us (0.28)
  blocking collectives: 84.7 us -> 5.41 us
  other arithmetic: 45 us -> 0.88 us
  local copies, waits for them, and re-layouts: 46.2 us -> 5.26 us
  starting transfers between devices: 49.3 us -> 21.5 us
  between operations: 25 us -> 7.78 us
  Pallas kernels: 0 us -> 12.8 us
  waiting for transfers between devices: 35.5 us -> 26.4 us
    psum x1 -> x0, blocking collectives: 79.2 us -> none  [local(): lax.psum(partial_value, 'space') / math.sqrt(layer_count * grid_rows)]
    ppermute x12 -> x11, starting transfers between devices: 49.2 us -> 21.5 us  [swap(): return lax.ppermute(value, axis, pairs)]
    slice x37 -> x4, local copies, waits for them, and re-layouts: 26.6 us -> 1.82 us  [the longest x1 0.65 us: local(): phase_sines[1]]
    reduce_scatter x1 -> x0, waiting for transfers between devices: 16.4 us -> none  [local(): lax.psum_scatter(smoothed, 'exc', scatter_dimension=0, tiled=True)]
    sub x4 -> x0, other arithmetic: 16.2 us -> none  [advance(): magnetic_y - COURANT * (upward(electric_x, 1) - upward(electric_z, 3))]
    add x9 -> x7, other arithmetic: 13.8 us -> 0.03 us  [the longest x5 0.02 us: local(): totals + swap(totals, 'space', [(i, i ^ bit) for i in range(strips)])]
    pallas_call x0 -> x4, Pallas kernels: none -> 12.8 us  [the longest x1 5.67 us: local(): pl.pallas_call(main, out_shape=[shaped(8, NX)] * 4, in_specs=[SMEM_SPEC,...]
    another operation x12 -> x1, other arithmetic: 10.2 us -> 0.08 us  [local(): ip = jnp.stack([strip, source_plane[0], monitor_plane[0], group])]
  transfers between devices with their start and end apart: 13 -> 11, of which waited for: 6 -> 7; matrix products, arithmetic and copies ran while one was open for 22% -> 6% of each run, Pallas kernels for 0% -> 7%
where the time goes in v1:
time: 80.5 us; the launch traced here: 80 us
  waiting for transfers between devices  26.4 us (33%)
  starting transfers between devices  21.5 us (27%)
  Pallas kernels  12.8 us (16%)
  between operations  7.78 us (10%)
  blocking collectives  5.41 us (7%)
  local copies, waits for them, and re-layouts  5.26 us (7%)
  other arithmetic  0.88 us (1%)
    ppermute x11, waiting for transfers between devices, swap(): return lax.ppermute(value, axis, pairs)  26.4 us
    ppermute x11, starting transfers between devices, swap(): return lax.ppermute(value, axis, pairs)  21.5 us
    pallas_call x1, Pallas kernels, local(): pl.pallas_call(main, out_shape=[shaped(8, NX)] * 4, in_specs=[SMEM_SPEC,...  5.67 us
    all_gather x1, blocking collectives, local(): dens = lax.all_gather(density.T, 'exc', axis=1, tiled=True)  5.41 us
    pallas_call x1, Pallas kernels, local(): pl.pallas_call(pack_kernel, out_shape=[shaped(PACK, NX), shaped(PACK, NX)...  3.66 us
    pallas_call x1, Pallas kernels, local(): pl.pallas_call(material, out_shape=[shaped(16, NX), shaped(8, NX), shaped...  2.68 us
    concatenate x1, local copies, waits for them, and re-layouts, local(): jnp.concatenate([sines, jnp.stack([cosines[0], phase_sines[0], cosines[1]...  2.59 us
  transfers between devices with their start and end apart: 11, of which 7 were waited for; matrix products, arithmetic and copies ran while one was open for 6% of the time, Pallas kernels for 7%

profile of v1, /device:TPU:6, one launch (start us, length us, event | category | flops | bytes accessed | tf_op | source)
XLA Modules:
  0.0 80.0 jit_solution(8021412866035024187)
XLA Ops:
  1.9 5.4 %all_gather.3.dens.refs_4_ = f32[8,1024]{1,0:T(8,128)S(1)} all-gather(f32[8,256]{1,0:T(8,128)} %bitcast.16), channel_id=1, replica_groups=mesh['exc'=4,'space'=32] {'exc'}, dimensions={1}, use_global_device_ids=true | all-gather | bytes 40960 | tf_op jit(solution)/shard_map/all_gather | solution.py:556
  7.4 0.8 copy-done.1
  8.2 3.7 %pack.1 = (f32[144,1024]{1,0:T(8,128)}, f32[144,1024]{1,0:T(8,128)S(1)}) custom-call(s32[4]{0:T(128)S(1)} %pad_add_fusion.ip.refs_0_, f32[1,6,32,8,1024]{4,3,2,1,0:T(8,128)} %refs_4_.1, f32[1,6,32,8,1024]{4,3,2,1,0:T(8,128)} %refs_6_.2, f32[8,1024]{1,0:T(8,128)S(1)} %all_gather.3.dens.refs_4_, s32[8,1024]{1,0:T(8,128)S(1)} %copy-done.1), custom_call_target="tpu_custom_call" | custom-call | tf_op jit(solution)/shard_map/pack/pallas_call | solution.py:558
  11.9 2.0 %collective-permute-start = (f32[144,1024]{1,0:T(8,128)}, f32[144,1024]{1,0:T(8,128)S(1)}, u32[]{:S(2)}, u32[]{:S(2)}) collective-permute-start(f32[144,1024]{1,0:T(8,128)} %get-tuple-element.13), channel_id=1, source_target_pairs={{0,1},{1,0},{2,3},{3,2},{4,5},{5,4},{6,7},{7,6},{8,9},{9,8},{10,11... | collective-permute-start | bytes 1769480 | tf_op jit(solution)/shard_map/ppermute | solution.py:524
  13.9 7.4 %collective-permute-start.1 = (f32[144,1024]{1,0:T(8,128)S(1)}, f32[144,1024]{1,0:T(8,128)S(1)}, u32[]{:S(2)}, u32[]{:S(2)}) collective-permute-start(f32[144,1024]{1,0:T(8,128)S(1)} %get-tuple-element.14), channel_id=1, source_target_pairs={{1,2},{2,1},{3,4},{4,3},{5,6},{6,5},{7,8},{8,7},{9,10},{10,9},{11,... | collective-permute-start | bytes 1769480 | tf_op jit(solution)/shard_map/ppermute | solution.py:524
  23.4 0.7 fusion.3
  24.1 0.6 fusion.4
  24.7 2.6 %concatenate.3.refs_1_ = f32[37]{0:T(128)S(1)} concatenate(f32[32]{0:T(128)S(1)} %multiply_sine_fusion, f32[1]{0:T(128)} %get-tuple-element.29, f32[1]{0:T(128)} %get-tuple-element.27, f32[1]{0:T(128)} %get-tuple-element.28, f32[1]{0:T(128)} %get-tuple-element.26, f32[1]{0:T(128)} %bitcast.5), dimensions={0} | concatenate | bytes 296 | tf_op jit(solution)/shard_map/concatenate | solution.py:550
  27.3 0.6 collective-permute-done.refs_2_
  27.9 7.6 %collective-permute-done.1.refs_3_ = f32[144,1024]{1,0:T(8,128)S(1)} collective-permute-done((f32[144,1024]{1,0:T(8,128)S(1)}, f32[144,1024]{1,0:T(8,128)S(1)}, u32[]{:S(2)}, u32[]{:S(2)}) %collective-permute-start.1) | collective-permute-done | bytes 589856 | tf_op jit(solution)/shard_map/ppermute | solution.py:524
  35.6 2.7 %material.1 = (f32[16,1024]{1,0:T(8,128)S(1)}, f32[8,1024]{1,0:T(8,128)S(1)}, f32[8,128]{1,0:T(8,128)S(1)}) custom-call(s32[4]{0:T(128)S(1)} %pad_add_fusion.ip.refs_0_, f32[37]{0:T(128)S(1)} %concatenate.3.refs_1_, f32[144,1024]{1,0:T(8,128)S(1)} %collective-permute-done.refs_2_, f32[144,1024]{1,0:T(8,128)S(1)} %collective-permute-done.1.refs_3_, ...), custom_call_target="tpu_custom_call" | custom-call | tf_op jit(solution)/shard_map/material/pallas_call | solution.py:579
  38.4 5.7 %main.1 = (f32[8,1024]{1,0:T(8,128)S(1)}, f32[8,1024]{1,0:T(8,128)S(1)}, f32[8,1024]{1,0:T(8,128)S(1)}, f32[8,1024]{1,0:T(8,128)S(1)}) custom-call(s32[4]{0:T(128)S(1)} %pad_add_fusion.ip.refs_0_, f32[37]{0:T(128)S(1)} %concatenate.3.refs_1_, f32[144,1024]{1,0:T(8,128)S(1)} %collective-permute-done.refs_2_, f32[144,1024]{1,0:T(8,128)S(1)} %collective-permute-done.1.refs_3_, ...), custom_call_target="tpu_custom_call" | custom-call | tf_op jit(solution)/shard_map/main/pallas_call | solution.py:604
  44.1 2.1 %collective-permute-start.2 = (f32[8,1024]{1,0:T(8,128)S(1)}, f32[8,1024]{1,0:T(8,128)S(1)}, u32[]{:S(2)}, u32[]{:S(2)}) collective-permute-start(f32[8,1024]{1,0:T(8,128)S(1)} %get-tuple-element.17), channel_id=1, source_target_pairs={{0,1},{1,0},{2,3},{3,2},{4,5},{5,4},{6,7},{7,6},{8,9},{9,8},{10,11... | collective-permute-start | bytes 98312 | tf_op jit(solution)/shard_map/ppermute | solution.py:524
  46.1 7.4 %collective-permute-start.3 = (f32[8,1024]{1,0:T(8,128)S(1)}, f32[8,1024]{1,0:T(8,128)S(1)}, u32[]{:S(2)}, u32[]{:S(2)}) collective-permute-start(f32[8,1024]{1,0:T(8,128)S(1)} %get-tuple-element.18), channel_id=1, source_target_pairs={{1,2},{2,1},{3,4},{4,3},{5,6},{6,5},{7,8},{8,7},{9,10},{10,9},{11,... | collective-permute-start | bytes 98312 | tf_op jit(solution)/shard_map/ppermute | solution.py:524
  53.7 5.0 %collective-permute-done.5 = f32[1,128]{1,0:T(1,128)S(1)} collective-permute-done((f32[1,128]{1,0:T(1,128)S(1)}, f32[1,128]{1,0:T(1,128)S(1)}, u32[]{:S(2)}, u32[]{:S(2)}) %collective-permute-start.5) | collective-permute-done | bytes 544 | tf_op jit(solution)/shard_map/ppermute | solution.py:524
  58.7 5.0 %collective-permute-done.6 = f32[1,128]{1,0:T(1,128)S(1)} collective-permute-done((f32[1,128]{1,0:T(1,128)S(1)}, f32[1,128]{1,0:T(1,128)S(1)}, u32[]{:S(2)}, u32[]{:S(2)}) %collective-permute-start.6) | collective-permute-done | bytes 544 | tf_op jit(solution)/shard_map/ppermute | solution.py:524
  64.3 3.0 %collective-permute-done.7 = f32[1,128]{1,0:T(1,128)S(1)} collective-permute-done((f32[1,128]{1,0:T(1,128)S(1)}, f32[1,128]{1,0:T(1,128)S(1)}, u32[]{:S(2)}, u32[]{:S(2)}) %collective-permute-start.7) | collective-permute-done | bytes 544 | tf_op jit(solution)/shard_map/ppermute | solution.py:524
  67.3 1.1 %collective-permute-start.8 = (f32[1,128]{1,0:T(1,128)S(1)}, f32[1,128]{1,0:T(1,128)S(1)}, u32[]{:S(2)}, u32[]{:S(2)}) collective-permute-start(f32[1,128]{1,0:T(1,128)S(1)} %add.96), channel_id=1, source_target_pairs={{0,16},{1,17},{2,18},{3,19},{4,20},{5,21},{6,22},{7,23},{8,24},{9,... | collective-permute-start | bytes 1544 | tf_op jit(solution)/shard_map/ppermute | solution.py:524
  68.4 3.9 %collective-permute-done.8 = f32[1,128]{1,0:T(1,128)S(1)} collective-permute-done((f32[1,128]{1,0:T(1,128)S(1)}, f32[1,128]{1,0:T(1,128)S(1)}, u32[]{:S(2)}, u32[]{:S(2)}) %collective-permute-start.8) | collective-permute-done | bytes 544 | tf_op jit(solution)/shard_map/ppermute | solution.py:524
  72.3 0.8 final.1
  73.3 1.1 %collective-permute-done.9 = f32[2,8,256]{2,1,0:T(8,128)S(1)} collective-permute-done((f32[2,8,256]{2,1,0:T(8,128)S(1)}, f32[2,8,256]{2,1,0:T(8,128)S(1)}, u32[]{:S(2)}, u32[]{:S(2)}) %collective-permute-start.9) | collective-permute-done | bytes 16416 | tf_op jit(solution)/shard_map/ppermute | solution.py:524
  74.4 0.7 collective-permute-start.10
  75.1 0.6 fusion.2
  78.3 0.6 add_bitcast_fusion
  (30 shorter events, 1.2 us)
Async XLA Ops:
  7.4 0.8 copy-start.1
  8.2 15.2 %copy-start.3 = (f32[1,2,32,8]{2,3,1,0:T(8,128)S(1)}, f32[1,2,32,8]{2,3,1,0:T(8,128)}, u32[]{:S(2)}) copy-start(f32[1,2,32,8]{2,3,1,0:T(8,128)} %param.16) | copy-start | bytes 6148
  8.2 27.4 %copy-start.2 = (s32[8,1024]{1,0:T(8,128)S(1)}, s32[8,1024]{1,0:T(8,128)}, u32[]{:S(2)}) copy-start(s32[8,1024]{1,0:T(8,128)} %refs_5_.2) | copy-start | bytes 98308
  11.8 26.5 %copy-start = (f32[1,6,8,8,1024]{4,3,2,1,0:T(8,128)S(1)}, f32[1,6,8,8,1024]{4,3,2,1,0:T(8,128)}, u32[]{:S(2)}) copy-start(f32[1,6,8,8,1024]{4,3,2,1,0:T(8,128)} %refs_5_.3) | copy-start | bytes 4718596
  11.9 16.1 %collective-permute-start = (f32[144,1024]{1,0:T(8,128)}, f32[144,1024]{1,0:T(8,128)S(1)}, u32[]{:S(2)}, u32[]{:S(2)}) collective-permute-start(f32[144,1024]{1,0:T(8,128)} %get-tuple-element.13), channel_id=1, source_target_pairs={{0,1},{1,0},{2,3},{3,2},{4,5},{5,4},{6,7},{7,6},{8,9},{9,8},{10,11... | collective-permute-start | bytes 1769480 | tf_op jit(solution)/shard_map/ppermute | solution.py:524
  13.9 21.7 %collective-permute-start.1 = (f32[144,1024]{1,0:T(8,128)S(1)}, f32[144,1024]{1,0:T(8,128)S(1)}, u32[]{:S(2)}, u32[]{:S(2)}) collective-permute-start(f32[144,1024]{1,0:T(8,128)S(1)} %get-tuple-element.14), channel_id=1, source_target_pairs={{1,2},{2,1},{3,4},{4,3},{5,6},{6,5},{7,8},{8,7},{9,10},{10,9},{11,... | collective-permute-start | bytes 1769480 | tf_op jit(solution)/shard_map/ppermute | solution.py:524
  38.3 15.3 %collective-permute-start.4 = (f32[1,128]{1,0:T(1,128)S(1)}, f32[1,128]{1,0:T(1,128)S(1)}, u32[]{:S(2)}, u32[]{:S(2)}) collective-permute-start(f32[1,128]{1,0:T(1,128)S(1)} %slice.25), channel_id=1, source_target_pairs={{0,1},{1,0},{2,3},{3,2},{4,5},{5,4},{6,7},{7,6},{8,9},{9,8},{10,11... | collective-permute-start | bytes 1544 | tf_op jit(solution)/shard_map/ppermute | solution.py:524
  44.1 28.3 %collective-permute-start.2 = (f32[8,1024]{1,0:T(8,128)S(1)}, f32[8,1024]{1,0:T(8,128)S(1)}, u32[]{:S(2)}, u32[]{:S(2)}) collective-permute-start(f32[8,1024]{1,0:T(8,128)S(1)} %get-tuple-element.17), channel_id=1, source_target_pairs={{0,1},{1,0},{2,3},{3,2},{4,5},{5,4},{6,7},{7,6},{8,9},{9,8},{10,11... | collective-permute-start | bytes 98312 | tf_op jit(solution)/shard_map/ppermute | solution.py:524
  46.1 26.2 %collective-permute-start.3 = (f32[8,1024]{1,0:T(8,128)S(1)}, f32[8,1024]{1,0:T(8,128)S(1)}, u32[]{:S(2)}, u32[]{:S(2)}) collective-permute-start(f32[8,1024]{1,0:T(8,128)S(1)} %get-tuple-element.18), channel_id=1, source_target_pairs={{1,2},{2,1},{3,4},{4,3},{5,6},{6,5},{7,8},{8,7},{9,10},{10,9},{11,... | collective-permute-start | bytes 98312 | tf_op jit(solution)/shard_map/ppermute | solution.py:524
  53.6 5.1 %collective-permute-start.5 = (f32[1,128]{1,0:T(1,128)S(1)}, f32[1,128]{1,0:T(1,128)S(1)}, u32[]{:S(2)}, u32[]{:S(2)}) collective-permute-start(f32[1,128]{1,0:T(1,128)S(1)} %slice_add_fusion), channel_id=1, source_target_pairs={{0,2},{1,3},{2,0},{3,1},{4,6},{5,7},{6,4},{7,5},{8,10},{9,11},{10,... | collective-permute-start | bytes 1544 | tf_op jit(solution)/shard_map/ppermute | solution.py:524
  58.7 5.0 %collective-permute-start.6 = (f32[1,128]{1,0:T(1,128)S(1)}, f32[1,128]{1,0:T(1,128)S(1)}, u32[]{:S(2)}, u32[]{:S(2)}) collective-permute-start(f32[1,128]{1,0:T(1,128)S(1)} %add.94), channel_id=1, source_target_pairs={{0,4},{1,5},{2,6},{3,7},{4,0},{5,1},{6,2},{7,3},{8,12},{9,13},{10,... | collective-permute-start | bytes 1544 | tf_op jit(solution)/shard_map/ppermute | solution.py:524
  63.7 3.5 %collective-permute-start.7 = (f32[1,128]{1,0:T(1,128)S(1)}, f32[1,128]{1,0:T(1,128)S(1)}, u32[]{:S(2)}, u32[]{:S(2)}) collective-permute-start(f32[1,128]{1,0:T(1,128)S(1)} %add.95), channel_id=1, source_target_pairs={{0,8},{1,9},{2,10},{3,11},{4,12},{5,13},{6,14},{7,15},{8,0},{9,1},... | collective-permute-start | bytes 1544 | tf_op jit(solution)/shard_map/ppermute | solution.py:524
  67.3 5.0 %collective-permute-start.8 = (f32[1,128]{1,0:T(1,128)S(1)}, f32[1,128]{1,0:T(1,128)S(1)}, u32[]{:S(2)}, u32[]{:S(2)}) collective-permute-start(f32[1,128]{1,0:T(1,128)S(1)} %add.96), channel_id=1, source_target_pairs={{0,16},{1,17},{2,18},{3,19},{4,20},{5,21},{6,22},{7,23},{8,24},{9,... | collective-permute-start | bytes 1544 | tf_op jit(solution)/shard_map/ppermute | solution.py:524
  73.1 1.3 %collective-permute-start.9 = (f32[2,8,256]{2,1,0:T(8,128)S(1)}, f32[2,8,256]{2,1,0:T(8,128)S(1)}, u32[]{:S(2)}, u32[]{:S(2)}) collective-permute-start(f32[2,8,256]{2,1,0:T(8,128)S(1)} %get-tuple-element.23), channel_id=1, source_target_pairs={{0,32},{32,0},{64,96},{96,64},{1,33},{33,1},{65,97},{97,65},{2,34}... | collective-permute-start | bytes 49160 | tf_op jit(solution)/shard_map/ppermute | solution.py:524
  74.4 3.9 %collective-permute-start.10 = (f32[1,8,256]{2,1,0:T(8,128)S(1)}, f32[1,8,256]{2,1,0:T(8,128)S(1)}, u32[]{:S(2)}, u32[]{:S(2)}) collective-permute-start(f32[1,8,256]{2,1,0:T(8,128)S(1)} %constant_dynamic-slice_fusion), channel_id=1, source_target_pairs={{0,64},{32,96},{64,0},{96,32},{1,65},{33,97},{65,1},{97,33},{2,66}... | collective-permute-start | bytes 24584 | tf_op jit(solution)/shard_map/ppermute | solution.py:524

commit v2 on v1

--- a/solution.py
+++ b/solution.py
@@ -21,7 +21,7 @@
 DZ = 8
 UP_ROWS = 64
 DOWN_ROWS = 40
-PACK = 16 + 2 * UP_ROWS
+PACK = 2 * UP_ROWS
 WEIGHTS = [(R + 1.0 - abs(k - R)) / ((R + 1.0) * (R + 1.0)) for k in range(2 * R + 1)]
 VMEM_LIMIT = 50 * 1024 * 1024
 
@@ -78,18 +78,13 @@
     return total
 
 
-def pack_kernel(ip, ff, af, dens, lab, ev, od, rows, up, down, sem, out_sem):
+def pack_kernel(ip, ff, af, ev, od, rows, up, down, sem, out_sem):
     copies = []
     for p, f in enumerate((ff, af)):
         for k, r in enumerate((0, 1, 6, 7)):
             copies.append(pltpu.make_async_copy(f.at[0, :, 8:24, r, :], rows.at[p, k], sem.at[p, k]))
     for c in copies:
         c.start()
-    own = lab[...].astype(jnp.float32)
-    up[0:8] = dens[...]
-    up[8:16] = own
-    down[0:8] = dens[...]
-    down[8:16] = own
     tile = sublanes((8, NX))
     for p in range(2):
         for k in range(4):
@@ -105,7 +100,7 @@
         hz = row(0, 5) - COURANT * ((x_up(ey) - ey) - (ex_n - ex))
         cx = hz - (hy - roll_down(hy))
         cz = (hy - x_down(hy)) - hx
-        base = 16 + p * DOWN_ROWS
+        base = p * DOWN_ROWS
         down[base : base + 8] = ex[0:8]
         down[base + 8 : base + 16] = ez[0:8]
         down[base + 16 : base + 24] = cx[0:8]
@@ -125,7 +120,7 @@
         cx = (hz - hz_l) - (hy - roll_down(hy))
         cy = (hx - roll_down(hx)) - (hz - x_down(hz))
         cz = (hy - x_down(hy)) - (hx - hx_l)
-        base = 16 + p * UP_ROWS
+        base = p * UP_ROWS
         for k, v in enumerate((hx, hz, u1, u2, cx, cy, cz)):
             up[base + 8 * k : base + 8 * k + 8] = v[0:8]
         extra = jnp.where((tile == 1) | (tile == 2), pltpu.roll(hz[8:16], 2, 0), hx[8:16])
@@ -135,7 +130,7 @@
 
     def send(to_up, to_down):
         a = pltpu.make_async_copy(up, to_up, out_sem.at[0])
-        b = pltpu.make_async_copy(down, to_down.at[0 : 16 + 2 * DOWN_ROWS], out_sem.at[1])
+        b = pltpu.make_async_copy(down, to_down.at[0 : 2 * DOWN_ROWS], out_sem.at[1])
         a.start()
         b.start()
         a.wait()
@@ -188,18 +183,29 @@
 
 
 def material_kernel(
-    grid_rows, ip, fp, ev, od, dens, lab, monitor, shape_zy, ff, inv_out, design_out, part_out,
-    below, above, fw, sem, win_sem,
+    grid_rows, ip, fp, ev, od, lab, first, second, third, monitor, shape_zy, ff,
+    inv_out, design_out, part_out, wide, fw, win_sem,
 ):
-    strip, plane = ip[0], ip[1]
+    strip, plane, group = ip[0], ip[1], ip[3]
     w0 = window_start(plane - 2)
     window = pltpu.make_async_copy(ff.at[0, :, :, :, pl.ds(w0, 256)], fw, win_sem)
     window.start()
-    from_neighbours(ip, ev, od, below, above, pl.ds(0, 16), pl.ds(0, 16), sem)
+    even = strip % 2 == 0
     own = lab[...].astype(jnp.float32)
-    wide = jnp.concatenate([below[0:8], dens[...], above[0:8]], 0)
-    kinds = jnp.concatenate([below[8:16], own, above[8:16]], 0)[4:20]
-    filtered = x_smooth(y_smooth(wide, 16))
+    low = jnp.where(even, od[4:8, 0:NX], ev[4:8, 0:NX])
+    high = jnp.where(even, ev[0:4, 0:NX], od[0:4, 0:NX])
+    kinds = jnp.concatenate([low, own, high], 0)
+    width = first.shape[1]
+    for k in range(4):
+        block = (first, second, third, third)[k]
+        base = 24 if k == 3 else 0
+        at = pl.ds(pl.multiple_of((group ^ k) * width, 128), width)
+        mine, from_ev = block[base : base + 8], block[base + 8 : base + 16]
+        from_od = block[base + 16 : base + 24]
+        wide[0:8, at] = jnp.where(even, from_od, from_ev)
+        wide[8:16, at] = mine
+        wide[16:24, at] = jnp.where(even, from_ev, from_od)
+    filtered = x_smooth(y_smooth(wide[...], 16))
     lower = math.tanh(SHARPNESS * MIDPOINT)
     spread = lower + math.tanh(SHARPNESS * (1.0 - MIDPOINT))
     bent = jnp.tanh(SHARPNESS * (filtered - MIDPOINT))
@@ -268,9 +274,9 @@
         pulse = source_base * (COURANT * fp[z])
         one -= pulse * (w[z][0:8] * c0)
         two -= pulse * (wz[z][0:8] * c0 + w[z][0:8] * c1)
-    first, second = jnp.sum(one), jnp.sum(two)
-    real = jnp.sum(monitor[0, 0] * shape_zy[...]) + c0 * first + c1 * second
-    imaginary = jnp.sum(monitor[0, 1] * shape_zy[...]) - s0 * first - s1 * second
+    total_1, total_2 = jnp.sum(one), jnp.sum(two)
+    real = jnp.sum(monitor[0, 0] * shape_zy[...]) + c0 * total_1 + c1 * total_2
+    imaginary = jnp.sum(monitor[0, 1] * shape_zy[...]) - s0 * total_1 - s1 * total_2
     ids = lanes((8, 128))
     part_out[...] = jnp.where(ids == 0, real, jnp.where(ids == 1, imaginary, 0.0))
 
@@ -298,7 +304,7 @@
         copies[p][1].start()
         sum_copies[p].start()
     from_neighbours(
-        ip, ev, od, below, above, pl.ds(16, 2 * UP_ROWS), pl.ds(16, 2 * DOWN_ROWS), halo_sem
+        ip, ev, od, below, above, pl.ds(0, 2 * UP_ROWS), pl.ds(0, 2 * DOWN_ROWS), halo_sem
     )
     full = (8, NX)
     row_ids = sublanes(full)
@@ -542,36 +548,49 @@
     odd_pairs = [(i, ((i - 1) ^ 1) + 1) for i in range(1, strips - 1)]
 
     ip = jnp.stack([strip, source_plane[0], monitor_plane[0], group])
+    number = jnp.arange(128, dtype=jnp.int32)
+    order = math.pi * (mode_numbers[0] + 1).astype(f32)
+    early = start_phase[0]
+    late = start_phase[0] + frequency[0]
+    angle = jnp.where(number < 34, early, late)
+    angle = jnp.where(number < NZ, order * (number.astype(f32) + 0.5) / NZ, angle)
+    fp = jnp.where((number == 32) | (number == 34), jnp.cos(angle), jnp.sin(angle))
+    factor = frequency[0] * frequency[0] * ((SILICON - OXIDE) / math.sqrt(groups * DZ))
+    fp = jnp.where(number == 36, factor, fp)
+    own_rows = (strip * ROWS + jnp.arange(ROWS, dtype=jnp.int32)).astype(f32)
     layers = jnp.arange(NZ, dtype=f32) + 0.5
-    sines = jnp.sin(math.pi * (mode_numbers[0] + 1).astype(f32) * layers / NZ)
-    phases = start_phase[0] + frequency[0] * jnp.arange(2, dtype=f32)
-    cosines, phase_sines = jnp.cos(phases), jnp.sin(phases)
-    factor = frequency[0] * frequency[0] * ((SILICON - OXIDE) / math.sqrt(groups * DZ))
-    fp = jnp.concatenate(
-        [sines, jnp.stack([cosines[0], phase_sines[0], cosines[1], phase_sines[1], factor])]
-    )
-    own_rows = (strip * ROWS + jnp.arange(ROWS, dtype=jnp.int32)).astype(f32)
-    shape_zy = sines[:, None] * (1.0 + 2.0 * (own_rows + 0.5) / grid_rows)[None, :]
-
-    dens = lax.all_gather(density.T, "exc", axis=1, tiled=True)
+    ramp = 1.0 + 2.0 * (own_rows + 0.5) / grid_rows
+    shape_zy = jnp.sin(order * layers / NZ)[:, None] * ramp[None, :]
+
+    quarter = density.T
+    width = quarter.shape[1]
+    small = jnp.concatenate([labels.astype(f32), quarter], 1)
+    od_small = swap(small, "space", odd_pairs)
+    ev_small = swap(small, "space", even_pairs)
 
     ev, od = pl.pallas_call(
         pack_kernel,
         out_shape=[shaped(PACK, NX), shaped(PACK, NX)],
-        in_specs=[SMEM_SPEC, ANY_SPEC, ANY_SPEC, VMEM_SPEC, VMEM_SPEC],
+        in_specs=[SMEM_SPEC, ANY_SPEC, ANY_SPEC],
         out_specs=[ANY_SPEC, ANY_SPEC],
         scratch_shapes=[
             pltpu.VMEM((2, 4, 6, 16, NX), f32),
             pltpu.VMEM((PACK, NX), f32),
-            pltpu.VMEM((16 + 2 * DOWN_ROWS, NX), f32),
+            pltpu.VMEM((2 * DOWN_ROWS, NX), f32),
             pltpu.SemaphoreType.DMA((2, 4)),
             pltpu.SemaphoreType.DMA((2,)),
         ],
         compiler_params=params(),
         name="pack",
-    )(ip, forward_fields, adjoint_fields, dens, labels)
+    )(ip, forward_fields, adjoint_fields)
+    od = swap(od, "space", odd_pairs)
     ev = swap(ev, "space", even_pairs)
-    od = swap(od, "space", odd_pairs)
+
+    first = jnp.concatenate([quarter, ev_small[:, NX:], od_small[:, NX:]], 0)
+    second = swap(first, "exc", [(i, i ^ 1) for i in range(groups)])
+    third = swap(
+        jnp.concatenate([first, second], 0), "exc", [(i, i ^ 2) for i in range(groups)]
+    )
 
     def material(*refs):
         material_kernel(grid_rows, *refs)
@@ -579,24 +598,23 @@
     inv, design, part = pl.pallas_call(
         material,
         out_shape=[shaped(16, NX), shaped(8, NX), shaped(8, 128)],
-        in_specs=[SMEM_SPEC, SMEM_SPEC, ANY_SPEC, ANY_SPEC] + [VMEM_SPEC] * 4 + [ANY_SPEC],
+        in_specs=[SMEM_SPEC, SMEM_SPEC] + [VMEM_SPEC] * 8 + [ANY_SPEC],
         out_specs=[VMEM_SPEC] * 3,
         scratch_shapes=[
-            pltpu.VMEM((16, NX), f32),
-            pltpu.VMEM((16, NX), f32),
+            pltpu.VMEM((24, NX), f32),
             pltpu.VMEM((6, NZ, ROWS, 256), f32),
-            pltpu.SemaphoreType.DMA((2,)),
             pltpu.SemaphoreType.DMA,
         ],
         compiler_params=params(),
         name="material",
-    )(ip, fp, ev, od, dens, labels, monitor_sums, shape_zy, forward_fields)
+    )(
+        ip, fp, ev_small, od_small, labels, first, second, third, monitor_sums, shape_zy,
+        forward_fields,
+    )
 
     totals = part[0:1]
-    bit = 1
-    while bit < strips:
+    for bit in (8, 24, 4, 1, 3):
         totals = totals + swap(totals, "space", [(i, i ^ bit) for i in range(strips)])
-        bit *= 2
 
     def main(*refs):
         main_kernel(strips, grid_rows, *refs)
@@ -633,7 +651,6 @@
     def final(*refs):
         final_kernel(norm, *refs)
 
-    width = NX // groups
     keep, send = pl.pallas_call(
         final,
         out_shape=[shaped(half_count, ROWS, width)] * 2,

time: 80.5 us -> 76 us (0.944)
  starting transfers between devices: 21.5 us -> 29.1 us
  blocking collectives: 5.41 us -> 0 us
  waiting for transfers between devices: 26.4 us -> 21.8 us
  local copies, waits for them, and re-layouts: 5.26 us -> 0.69 us
  other arithmetic: 0.88 us -> 2.35 us
    ppermute x11 -> x15, starting transfers between devices: 21.5 us -> 29.1 us  [swap(): return lax.ppermute(value, axis, pairs)]
    all_gather x1 -> x0, blocking collectives: 5.41 us -> none  [local(): dens = lax.all_gather(density.T, 'exc', axis=1, tiled=True)]
    ppermute x11 -> x15, waiting for transfers between devices: 26.4 us -> 21.8 us  [swap(): return lax.ppermute(value, axis, pairs)]
    concatenate x1 -> x0, local copies, waits for them, and re-layouts: 2.59 us -> none  [local(): jnp.concatenate([sines, jnp.stack([cosines[0], phase_sines[0], cosines[1]...]
    slice x2, local copies, waits for them, and re-layouts: 1.24 us -> 0.01 us  [local(): first = jnp.concatenate([quarter, ev_small[:, NX:], od_small[:, NX:]], 0)]
  transfers between devices with their start and end apart: 11 -> 15, of which waited for: 7 -> 7; matrix products, arithmetic and copies ran while one was open for 6% -> 1% of each run, Pallas kernels for 7% -> 17%
where the time goes in v2:
time: 76 us; the launch traced here: 75.3 us
  starting transfers between devices  29.1 us (38%)
  waiting for transfers between devices  21.8 us (29%)
  Pallas kernels  13.5 us (18%)
  between operations  7.87 us (10%)
  other arithmetic  2.35 us (3%)
    ppermute x15, starting transfers between devices, swap(): return lax.ppermute(value, axis, pairs)  29.1 us
    ppermute x15, waiting for transfers between devices, swap(): return lax.ppermute(value, axis, pairs)  21.8 us
    pallas_call x1, Pallas kernels, local(): pl.pallas_call(main, out_shape=[shaped(8, NX)] * 4, in_specs=[SMEM_SPEC,...  5.67 us
    pallas_call x1, Pallas kernels, local(): pl.pallas_call(pack_kernel, out_shape=[shaped(PACK, NX), shaped(PACK, NX)...  3.65 us
    pallas_call x1, Pallas kernels, local(): pl.pallas_call(material, out_shape=[shaped(16, NX), shaped(8, NX), shaped...  3.38 us
  transfers between devices with their start and end apart: 15, of which 7 were waited for; matrix products, arithmetic and copies ran while one was open for 1% of the time, Pallas kernels for 17%

profile of v2, /device:TPU:6, one launch (start us, length us, event | category | flops | bytes accessed | tf_op | source)
XLA Modules:
  0.0 75.3 jit_solution(13306882476208696877)
XLA Ops:
  0.6 0.8 %convert_element_type.19 = f32[8,1024]{1,0:T(8,128)S(1)} convert(s32[8,1024]{1,0:T(8,128)} %refs_4_.2) | non-fusion elementwise | flops 8192 | bytes 65536 | tf_op jit(solution)/shard_map/convert_element_type | solution.py:567
  1.4 0.7 pad_maximum_fusion.1
  2.1 1.9 %collective-permute-start.2 = (f32[8,1280]{1,0:T(8,128)S(1)}, f32[8,1280]{1,0:T(8,128)S(1)}, u32[]{:S(2)}, u32[]{:S(2)}) collective-permute-start(f32[8,1280]{1,0:T(8,128)S(1)} %pad_maximum_fusion.1), channel_id=1, source_target_pairs={{0,1},{1,0},{2,3},{3,2},{4,5},{5,4},{6,7},{7,6},{8,9},{9,8},{10,11... | collective-permute-start | bytes 122888 | tf_op jit(solution)/shard_map/ppermute | solution.py:530
  4.0 7.3 %collective-permute-start.3 = (f32[8,1280]{1,0:T(8,128)S(1)}, f32[8,1280]{1,0:T(8,128)S(1)}, u32[]{:S(2)}, u32[]{:S(2)}) collective-permute-start(f32[8,1280]{1,0:T(8,128)S(1)} %pad_maximum_fusion.1), channel_id=1, source_target_pairs={{1,2},{2,1},{3,4},{4,3},{5,6},{6,5},{7,8},{8,7},{9,10},{10,9},{11,... | collective-permute-start | bytes 122888 | tf_op jit(solution)/shard_map/ppermute | solution.py:530
  12.7 3.7 %pack.1 = (f32[128,1024]{1,0:T(8,128)}, f32[128,1024]{1,0:T(8,128)S(1)}) custom-call(s32[4]{0:T(128)S(1)} %pad_add_fusion.ip.refs_0_, f32[1,6,32,8,1024]{4,3,2,1,0:T(8,128)} %refs_4_.3, f32[1,6,32,8,1024]{4,3,2,1,0:T(8,128)} %refs_6_.1), custom_call_target="tpu_custom_call" | custom-call | tf_op jit(solution)/shard_map/pack/pallas_call | solution.py:571
  16.5 3.5 %collective-permute-start.1 = (f32[128,1024]{1,0:T(8,128)S(1)}, f32[128,1024]{1,0:T(8,128)S(1)}, u32[]{:S(2)}, u32[]{:S(2)}) collective-permute-start(f32[128,1024]{1,0:T(8,128)S(1)} %get-tuple-element.14), channel_id=1, source_target_pairs={{1,2},{2,1},{3,4},{4,3},{5,6},{6,5},{7,8},{8,7},{9,10},{10,9},{11,... | collective-permute-start | bytes 1572872 | tf_op jit(solution)/shard_map/ppermute | solution.py:530
  22.3 1.2 %collective-permute-start.5 = (f32[48,256]{1,0:T(8,128)S(1)}, f32[48,256]{1,0:T(8,128)S(1)}, u32[]{:S(2)}, u32[]{:S(2)}) collective-permute-start(f32[48,256]{1,0:T(8,128)S(1)} %pad_maximum_fusion), channel_id=1, source_target_pairs={{0,64},{32,96},{64,0},{96,32},{1,65},{33,97},{65,1},{97,33},{2,66}... | collective-permute-start | bytes 147464 | tf_op jit(solution)/shard_map/ppermute | solution.py:530
  23.7 2.8 %collective-permute-done.5.refs_7_ = f32[48,256]{1,0:T(8,128)S(1)} collective-permute-done((f32[48,256]{1,0:T(8,128)S(1)}, f32[48,256]{1,0:T(8,128)S(1)}, u32[]{:S(2)}, u32[]{:S(2)}) %collective-permute-start.5) | collective-permute-done | bytes 49184 | tf_op jit(solution)/shard_map/ppermute | solution.py:530
  26.5 3.4 %material.1 = (f32[16,1024]{1,0:T(8,128)S(1)}, f32[8,1024]{1,0:T(8,128)S(1)}, f32[8,128]{1,0:T(8,128)S(1)}) custom-call(s32[4]{0:T(128)S(1)} %pad_add_fusion.ip.refs_0_, f32[128]{0:T(128)S(1)} %compare_select_fusion.2.refs_1_, f32[8,1280]{1,0:T(8,128)S(1)} %collective-permute-done.2.refs_2_, f32[8,1280]{1,0:T(8,128)S(1)} %collective-permute-done.3.refs_3_, ...), custom_call_target="tpu_custom_call" | custom-call | tf_op jit(solution)/shard_map/material/pallas_call | solution.py:598
  29.9 8.3 %collective-permute-start.8 = (f32[1,128]{1,0:T(1,128)S(1)}, f32[1,128]{1,0:T(1,128)S(1)}, u32[]{:S(2)}, u32[]{:S(2)}) collective-permute-start(f32[1,128]{1,0:T(1,128)S(1)} %slice.17), channel_id=1, source_target_pairs={{0,8},{1,9},{2,10},{3,11},{4,12},{5,13},{6,14},{7,15},{8,0},{9,1},... | collective-permute-start | bytes 1544 | tf_op jit(solution)/shard_map/ppermute | solution.py:530
  38.2 5.7 %main.1 = (f32[8,1024]{1,0:T(8,128)S(1)}, f32[8,1024]{1,0:T(8,128)S(1)}, f32[8,1024]{1,0:T(8,128)S(1)}, f32[8,1024]{1,0:T(8,128)S(1)}) custom-call(s32[4]{0:T(128)S(1)} %pad_add_fusion.ip.refs_0_, f32[128]{0:T(128)S(1)} %compare_select_fusion.2.refs_1_, f32[128,1024]{1,0:T(8,128)S(1)} %collective-permute-done.refs_2_, ...), custom_call_target="tpu_custom_call" | custom-call | tf_op jit(solution)/shard_map/main/pallas_call | solution.py:622
  44.0 5.6 %collective-permute-start.7 = (f32[8,1024]{1,0:T(8,128)S(1)}, f32[8,1024]{1,0:T(8,128)S(1)}, u32[]{:S(2)}, u32[]{:S(2)}) collective-permute-start(f32[8,1024]{1,0:T(8,128)S(1)} %get-tuple-element.18), channel_id=1, source_target_pairs={{1,2},{2,1},{3,4},{4,3},{5,6},{6,5},{7,8},{8,7},{9,10},{10,9},{11,... | collective-permute-start | bytes 98312 | tf_op jit(solution)/shard_map/ppermute | solution.py:530
  49.8 4.7 %collective-permute-done.9 = f32[1,128]{1,0:T(1,128)S(1)} collective-permute-done((f32[1,128]{1,0:T(1,128)S(1)}, f32[1,128]{1,0:T(1,128)S(1)}, u32[]{:S(2)}, u32[]{:S(2)}) %collective-permute-start.9) | collective-permute-done | bytes 544 | tf_op jit(solution)/shard_map/ppermute | solution.py:530
  54.5 0.3 collective-permute-start.10
  54.8 4.8 %collective-permute-done.10 = f32[1,128]{1,0:T(1,128)S(1)} collective-permute-done((f32[1,128]{1,0:T(1,128)S(1)}, f32[1,128]{1,0:T(1,128)S(1)}, u32[]{:S(2)}, u32[]{:S(2)}) %collective-permute-start.10) | collective-permute-done | bytes 544 | tf_op jit(solution)/shard_map/ppermute | solution.py:530
  59.6 3.5 %collective-permute-done.11 = f32[1,128]{1,0:T(1,128)S(1)} collective-permute-done((f32[1,128]{1,0:T(1,128)S(1)}, f32[1,128]{1,0:T(1,128)S(1)}, u32[]{:S(2)}, u32[]{:S(2)}) %collective-permute-start.11) | collective-permute-done | bytes 544 | tf_op jit(solution)/shard_map/ppermute | solution.py:530
  63.1 0.3 collective-permute-start.12
  63.4 4.4 %collective-permute-done.12 = f32[1,128]{1,0:T(1,128)S(1)} collective-permute-done((f32[1,128]{1,0:T(1,128)S(1)}, f32[1,128]{1,0:T(1,128)S(1)}, u32[]{:S(2)}, u32[]{:S(2)}) %collective-permute-start.12) | collective-permute-done | bytes 544 | tf_op jit(solution)/shard_map/ppermute | solution.py:530
  67.9 0.8 %final.1 = (f32[2,8,256]{2,1,0:T(8,128)S(1)}, f32[2,8,256]{2,1,0:T(8,128)S(1)}) custom-call(s32[4]{0:T(128)S(1)} %pad_add_fusion.ip.refs_0_, f32[128]{0:T(128)S(1)} %compare_select_fusion.2.refs_1_, f32[8,1024]{1,0:T(8,128)S(1)} %collective-permute-done.6.refs_2_, f32[8,1024]{1,0:T(8,128)S(1)} %collective-permute-done.7.refs_3_, ...), custom_call_target="tpu_custom_call" | custom-call | tf_op jit(solution)/shard_map/final/pallas_call | solution.py:654
  68.8 1.1 %collective-permute-done.13 = f32[2,8,256]{2,1,0:T(8,128)S(1)} collective-permute-done((f32[2,8,256]{2,1,0:T(8,128)S(1)}, f32[2,8,256]{2,1,0:T(8,128)S(1)}, u32[]{:S(2)}, u32[]{:S(2)}) %collective-permute-start.13) | collective-permute-done | bytes 16416 | tf_op jit(solution)/shard_map/ppermute | solution.py:530
  69.9 0.1 collective-permute-start.14
  70.1 0.6 fusion
  73.2 0.3 collective-permute-done.14
  73.6 0.6 add_bitcast_fusion
  (40 shorter events, 0.8 us)
Async XLA Ops:
  2.1 18.7 %collective-permute-start.2 = (f32[8,1280]{1,0:T(8,128)S(1)}, f32[8,1280]{1,0:T(8,128)S(1)}, u32[]{:S(2)}, u32[]{:S(2)}) collective-permute-start(f32[8,1280]{1,0:T(8,128)S(1)} %pad_maximum_fusion.1), channel_id=1, source_target_pairs={{0,1},{1,0},{2,3},{3,2},{4,5},{5,4},{6,7},{7,6},{8,9},{9,8},{10,11... | collective-permute-start | bytes 122888 | tf_op jit(solution)/shard_map/ppermute | solution.py:530
  4.0 16.7 %collective-permute-start.3 = (f32[8,1280]{1,0:T(8,128)S(1)}, f32[8,1280]{1,0:T(8,128)S(1)}, u32[]{:S(2)}, u32[]{:S(2)}) collective-permute-start(f32[8,1280]{1,0:T(8,128)S(1)} %pad_maximum_fusion.1), channel_id=1, source_target_pairs={{1,2},{2,1},{3,4},{4,3},{5,6},{6,5},{7,8},{8,7},{9,10},{10,9},{11,... | collective-permute-start | bytes 122888 | tf_op jit(solution)/shard_map/ppermute | solution.py:530
  12.7 8.1 %copy-start.2 = (f32[256,8]{0,1:T(8,128)S(1)}, f32[256,8]{0,1:T(8,128)}, u32[]{:S(2)}) copy-start(f32[256,8]{0,1:T(8,128)} %param.17) | copy-start | bytes 24580
  12.7 10.9 %copy-start.3 = (f32[1,2,32,8]{2,3,1,0:T(8,128)S(1)}, f32[1,2,32,8]{2,3,1,0:T(8,128)}, u32[]{:S(2)}) copy-start(f32[1,2,32,8]{2,3,1,0:T(8,128)} %param.16) | copy-start | bytes 6148
  12.7 13.8 %copy-start.1 = (s32[8,1024]{1,0:T(8,128)S(1)}, s32[8,1024]{1,0:T(8,128)}, u32[]{:S(2)}) copy-start(s32[8,1024]{1,0:T(8,128)} %refs_4_.2) | copy-start | bytes 98308
  16.4 21.9 %copy-start = (f32[1,6,8,8,1024]{4,3,2,1,0:T(8,128)S(1)}, f32[1,6,8,8,1024]{4,3,2,1,0:T(8,128)}, u32[]{:S(2)}) copy-start(f32[1,6,8,8,1024]{4,3,2,1,0:T(8,128)} %refs_5_.1) | copy-start | bytes 4718596
  16.4 21.8 %collective-permute-start = (f32[128,1024]{1,0:T(8,128)}, f32[128,1024]{1,0:T(8,128)S(1)}, u32[]{:S(2)}, u32[]{:S(2)}) collective-permute-start(f32[128,1024]{1,0:T(8,128)} %get-tuple-element.13), channel_id=1, source_target_pairs={{0,1},{1,0},{2,3},{3,2},{4,5},{5,4},{6,7},{7,6},{8,9},{9,8},{10,11... | collective-permute-start | bytes 1572872 | tf_op jit(solution)/shard_map/ppermute | solution.py:530
  16.5 21.8 %collective-permute-start.1 = (f32[128,1024]{1,0:T(8,128)S(1)}, f32[128,1024]{1,0:T(8,128)S(1)}, u32[]{:S(2)}, u32[]{:S(2)}) collective-permute-start(f32[128,1024]{1,0:T(8,128)S(1)} %get-tuple-element.14), channel_id=1, source_target_pairs={{1,2},{2,1},{3,4},{4,3},{5,6},{6,5},{7,8},{8,7},{9,10},{10,9},{11,... | collective-permute-start | bytes 1572872 | tf_op jit(solution)/shard_map/ppermute | solution.py:530
  20.8 1.5 %collective-permute-start.4 = (f32[24,256]{1,0:T(8,128)S(1)}, f32[24,256]{1,0:T(8,128)S(1)}, u32[]{:S(2)}, u32[]{:S(2)}) collective-permute-start(f32[24,256]{1,0:T(8,128)S(1)} %pad_maximum_fusion.2.refs_5_), channel_id=1, source_target_pairs={{0,32},{32,0},{64,96},{96,64},{1,33},{33,1},{65,97},{97,65},{2,34}... | collective-permute-start | bytes 73736 | tf_op jit(solution)/shard_map/ppermute | solution.py:530
  22.3 4.2 %collective-permute-start.5 = (f32[48,256]{1,0:T(8,128)S(1)}, f32[48,256]{1,0:T(8,128)S(1)}, u32[]{:S(2)}, u32[]{:S(2)}) collective-permute-start(f32[48,256]{1,0:T(8,128)S(1)} %pad_maximum_fusion), channel_id=1, source_target_pairs={{0,64},{32,96},{64,0},{96,32},{1,65},{33,97},{65,1},{97,33},{2,66}... | collective-permute-start | bytes 147464 | tf_op jit(solution)/shard_map/ppermute | solution.py:530
  29.9 19.7 %collective-permute-start.8 = (f32[1,128]{1,0:T(1,128)S(1)}, f32[1,128]{1,0:T(1,128)S(1)}, u32[]{:S(2)}, u32[]{:S(2)}) collective-permute-start(f32[1,128]{1,0:T(1,128)S(1)} %slice.17), channel_id=1, source_target_pairs={{0,8},{1,9},{2,10},{3,11},{4,12},{5,13},{6,14},{7,15},{8,0},{9,1},... | collective-permute-start | bytes 1544 | tf_op jit(solution)/shard_map/ppermute | solution.py:530
  43.9 23.9 %collective-permute-start.6 = (f32[8,1024]{1,0:T(8,128)S(1)}, f32[8,1024]{1,0:T(8,128)S(1)}, u32[]{:S(2)}, u32[]{:S(2)}) collective-permute-start(f32[8,1024]{1,0:T(8,128)S(1)} %get-tuple-element.17), channel_id=1, source_target_pairs={{0,1},{1,0},{2,3},{3,2},{4,5},{5,4},{6,7},{7,6},{8,9},{9,8},{10,11... | collective-permute-start | bytes 98312 | tf_op jit(solution)/shard_map/ppermute | solution.py:530
  44.0 23.8 %collective-permute-start.7 = (f32[8,1024]{1,0:T(8,128)S(1)}, f32[8,1024]{1,0:T(8,128)S(1)}, u32[]{:S(2)}, u32[]{:S(2)}) collective-permute-start(f32[8,1024]{1,0:T(8,128)S(1)} %get-tuple-element.18), channel_id=1, source_target_pairs={{1,2},{2,1},{3,4},{4,3},{5,6},{6,5},{7,8},{8,7},{9,10},{10,9},{11,... | collective-permute-start | bytes 98312 | tf_op jit(solution)/shard_map/ppermute | solution.py:530
  49.7 4.8 %collective-permute-start.9 = (f32[1,128]{1,0:T(1,128)S(1)}, f32[1,128]{1,0:T(1,128)S(1)}, u32[]{:S(2)}, u32[]{:S(2)}) collective-permute-start(f32[1,128]{1,0:T(1,128)S(1)} %slice_add_fusion), channel_id=1, source_target_pairs={{0,24},{1,25},{2,26},{3,27},{4,28},{5,29},{6,30},{7,31},{8,16},{9,... | collective-permute-start | bytes 1544 | tf_op jit(solution)/shard_map/ppermute | solution.py:530
  54.5 5.0 %collective-permute-start.10 = (f32[1,128]{1,0:T(1,128)S(1)}, f32[1,128]{1,0:T(1,128)S(1)}, u32[]{:S(2)}, u32[]{:S(2)}) collective-permute-start(f32[1,128]{1,0:T(1,128)S(1)} %add.98), channel_id=1, source_target_pairs={{0,4},{1,5},{2,6},{3,7},{4,0},{5,1},{6,2},{7,3},{8,12},{9,13},{10,... | collective-permute-start | bytes 1544 | tf_op jit(solution)/shard_map/ppermute | solution.py:530
  59.5 3.5 %collective-permute-start.11 = (f32[1,128]{1,0:T(1,128)S(1)}, f32[1,128]{1,0:T(1,128)S(1)}, u32[]{:S(2)}, u32[]{:S(2)}) collective-permute-start(f32[1,128]{1,0:T(1,128)S(1)} %add.99), channel_id=1, source_target_pairs={{0,1},{1,0},{2,3},{3,2},{4,5},{5,4},{6,7},{7,6},{8,9},{9,8},{10,11... | collective-permute-start | bytes 1544 | tf_op jit(solution)/shard_map/ppermute | solution.py:530
  63.1 4.8 %collective-permute-start.12 = (f32[1,128]{1,0:T(1,128)S(1)}, f32[1,128]{1,0:T(1,128)S(1)}, u32[]{:S(2)}, u32[]{:S(2)}) collective-permute-start(f32[1,128]{1,0:T(1,128)S(1)} %add.100), channel_id=1, source_target_pairs={{0,3},{1,2},{2,1},{3,0},{4,7},{5,6},{6,5},{7,4},{8,11},{9,10},{10,... | collective-permute-start | bytes 1544 | tf_op jit(solution)/shard_map/ppermute | solution.py:530
  68.7 1.3 %collective-permute-start.13 = (f32[2,8,256]{2,1,0:T(8,128)S(1)}, f32[2,8,256]{2,1,0:T(8,128)S(1)}, u32[]{:S(2)}, u32[]{:S(2)}) collective-permute-start(f32[2,8,256]{2,1,0:T(8,128)S(1)} %get-tuple-element.23), channel_id=1, source_target_pairs={{0,32},{32,0},{64,96},{96,64},{1,33},{33,1},{65,97},{97,65},{2,34}... | collective-permute-start | bytes 49160 | tf_op jit(solution)/shard_map/ppermute | solution.py:530
  69.9 3.7 %collective-permute-start.14 = (f32[1,8,256]{2,1,0:T(8,128)S(1)}, f32[1,8,256]{2,1,0:T(8,128)S(1)}, u32[]{:S(2)}, u32[]{:S(2)}) collective-permute-start(f32[1,8,256]{2,1,0:T(8,128)S(1)} %constant_dynamic-slice_fusion), channel_id=1, source_target_pairs={{0,64},{32,96},{64,0},{96,32},{1,65},{33,97},{65,1},{97,33},{2,66}... | collective-permute-start | bytes 24584 | tf_op jit(solution)/shard_map/ppermute | solution.py:530

commit v3 on v2

--- a/solution.py
+++ b/solution.py
@@ -23,7 +23,8 @@
 DOWN_ROWS = 40
 PACK = 2 * UP_ROWS
 WEIGHTS = [(R + 1.0 - abs(k - R)) / ((R + 1.0) * (R + 1.0)) for k in range(2 * R + 1)]
-VMEM_LIMIT = 50 * 1024 * 1024
+VMEM_LIMIT = 32 * 1024 * 1024
+PACK_LIMIT = 50 * 1024 * 1024
 
 SMEM_SPEC = pl.BlockSpec(memory_space=pltpu.SMEM)
 VMEM_SPEC = pl.BlockSpec(memory_space=pltpu.VMEM)
@@ -78,7 +79,21 @@
     return total
 
 
-def pack_kernel(ip, ff, af, ev, od, rows, up, down, sem, out_sem):
+def prepare_kernel(grid_rows, scale, mode, rate, phase, fp, shape_yz):
+    order = math.pi * (mode[0] + 1).astype(jnp.float32)
+    number = lanes((1, 128))
+    early, late = phase[0], phase[0] + rate[0]
+    angle = jnp.where(number < 34, early, late)
+    angle = jnp.where(number < NZ, order * (number.astype(jnp.float32) + 0.5) / NZ, angle)
+    value = jnp.where((number == 32) | (number == 34), jnp.cos(angle), jnp.sin(angle))
+    fp[...] = jnp.where(number == 36, rate[0] * rate[0] * scale, value)
+    small = (ROWS, NZ)
+    rows = lax.axis_index("space") * ROWS + sublanes(small)
+    ramp = 1.0 + 2.0 * (rows.astype(jnp.float32) + 0.5) / grid_rows
+    shape_yz[...] = ramp * jnp.sin(order * (lanes(small).astype(jnp.float32) + 0.5) / NZ)
+
+
+def pack_kernel(after, ff, af, ev, od, rows, up, down, sem, out_sem):
     copies = []
     for p, f in enumerate((ff, af)):
         for k, r in enumerate((0, 1, 6, 7)):
@@ -126,7 +141,7 @@
         extra = jnp.where((tile == 1) | (tile == 2), pltpu.roll(hz[8:16], 2, 0), hx[8:16])
         up[base + 56 : base + 64] = jnp.where(tile == 3, pltpu.roll(cy[8:16], 3, 0), extra)
 
-    even = ip[0] % 2 == 0
+    even = lax.axis_index("space") % 2 == 0
 
     def send(to_up, to_down):
         a = pltpu.make_async_copy(up, to_up, out_sem.at[0])
@@ -145,8 +160,37 @@
         send(od, ev)
 
 
-def from_neighbours(ip, ev, od, below, above, below_rows, above_rows, sem):
-    even = ip[0] % 2 == 0
+def stage_kernel(after, ff, af, field, sem):
+    copies = []
+    for p, f in enumerate((ff, af)):
+        copies.append(
+            (
+                pltpu.make_async_copy(f.at[0, :, 12:22], field.at[p, :, 0:10], sem.at[p, 0]),
+                pltpu.make_async_copy(f.at[0, :, 10:12], field.at[p, :, 14:16], sem.at[p, 1]),
+            )
+        )
+    for pair in copies:
+        pair[0].start()
+        pair[1].start()
+    last_row = sublanes((8, NX)) == 7
+
+    def y_up(f):
+        return jnp.where(last_row, 0.0, roll_up(f))
+
+    for p in range(2):
+        copies[p][0].wait()
+        copies[p][1].wait()
+        for z in range(10, 21):
+            k, n = slot(z), slot(z + 1)
+            ex, ey, ez = field[p, 0, k], field[p, 1, k], field[p, 2, k]
+            field[p, 3, k] -= COURANT * ((y_up(ez) - ez) - (field[p, 1, n] - ey))
+            field[p, 4, k] -= COURANT * ((field[p, 0, n] - ex) - (x_up(ez) - ez))
+            if z > 10:
+                field[p, 5, k] -= COURANT * ((x_up(ey) - ey) - (y_up(ex) - ex))
+
+
+def from_neighbours(ev, od, below, above, below_rows, above_rows, sem):
+    even = lax.axis_index("space") % 2 == 0
 
     def get(from_below, from_above):
         a = pltpu.make_async_copy(from_below.at[below_rows], below, sem.at[0])
@@ -183,28 +227,22 @@
 
 
 def material_kernel(
-    grid_rows, ip, fp, ev, od, lab, first, second, third, monitor, shape_zy, ff,
+    grid_rows, source_at, fp, ev, od, own, monitor, shape_yz, ff,
     inv_out, design_out, part_out, wide, fw, win_sem,
 ):
-    strip, plane, group = ip[0], ip[1], ip[3]
+    strip, group = lax.axis_index("space"), lax.axis_index("exc")
+    plane = source_at[0]
     w0 = window_start(plane - 2)
     window = pltpu.make_async_copy(ff.at[0, :, :, :, pl.ds(w0, 256)], fw, win_sem)
     window.start()
     even = strip % 2 == 0
-    own = lab[...].astype(jnp.float32)
-    low = jnp.where(even, od[4:8, 0:NX], ev[4:8, 0:NX])
-    high = jnp.where(even, ev[0:4, 0:NX], od[0:4, 0:NX])
-    kinds = jnp.concatenate([low, own, high], 0)
-    width = first.shape[1]
+    both = jnp.concatenate(
+        [jnp.where(even, od[...], ev[...]), own[...], jnp.where(even, ev[...], od[...])], 0
+    )
+    kinds = both[4:20, NX:]
     for k in range(4):
-        block = (first, second, third, third)[k]
-        base = 24 if k == 3 else 0
-        at = pl.ds(pl.multiple_of((group ^ k) * width, 128), width)
-        mine, from_ev = block[base : base + 8], block[base + 8 : base + 16]
-        from_od = block[base + 16 : base + 24]
-        wide[0:8, at] = jnp.where(even, from_od, from_ev)
-        wide[8:16, at] = mine
-        wide[16:24, at] = jnp.where(even, from_ev, from_od)
+        at = pl.ds(pl.multiple_of((group ^ k) * 256, 128), 256)
+        wide[:, at] = both[:, 256 * k : 256 * k + 256]
     filtered = x_smooth(y_smooth(wide[...], 16))
     lower = math.tanh(SHARPNESS * MIDPOINT)
     spread = lower + math.tanh(SHARPNESS * (1.0 - MIDPOINT))
@@ -214,7 +252,7 @@
     mixed = OXIDE + (SILICON - OXIDE) * projected
     material = jnp.where(kinds == 2.0, mixed, jnp.where(kinds == 1.0, SILICON, OXIDE))
     inv_out[...] = pltpu.roll(1.0 / material, 12, 0)
-    design = jnp.where(kinds == 2.0, steepness * fp[36], 0.0)
+    design = jnp.where(kinds == 2.0, steepness * fp[0, 36], 0.0)
     design_out[...] = pltpu.roll(design, 12, 0)[0:8]
 
     small = (16, 128)
@@ -241,7 +279,7 @@
 
     zs = range(NZ)
     inv = [layer_inverse(z, middle) for z in zs]
-    seed = [seed_base * fp[z] for z in zs]
+    seed = [seed_base * fp[0, z] for z in zs]
     w = [inv[z] * seed[z] for z in zs]
     hx = [half * (roll_up(w[z]) - w[z]) for z in zs]
     hy = [half * (w[z] - xu(w[z])) for z in zs]
@@ -259,7 +297,7 @@
     window.wait()
     one = jnp.zeros((8, 128), jnp.float32)
     two = jnp.zeros((8, 128), jnp.float32)
-    c0, s0, c1, s1 = fp[32], fp[33], fp[34], fp[35]
+    c0, s0, c1, s1 = fp[0, 32], fp[0, 33], fp[0, 34], fp[0, 35]
     for z in zs:
         ex2 = ex[z] - half * (
             (hz2[z] - roll_down(hz2[z])) - (hy2[z] - at(hy2, z - 1))
@@ -271,40 +309,31 @@
         one += hx[z][0:8] * f[3] + hy[z][0:8] * f[4]
         two += ex2[0:8] * f[0] + ey2[0:8] * f[1] + ez2[0:8] * f[2]
         two += hx2[z][0:8] * f[3] + hy2[z][0:8] * f[4] + hz2[z][0:8] * f[5]
-        pulse = source_base * (COURANT * fp[z])
+        pulse = source_base * (COURANT * fp[0, z])
         one -= pulse * (w[z][0:8] * c0)
         two -= pulse * (wz[z][0:8] * c0 + w[z][0:8] * c1)
     total_1, total_2 = jnp.sum(one), jnp.sum(two)
-    real = jnp.sum(monitor[0, 0] * shape_zy[...]) + c0 * total_1 + c1 * total_2
-    imaginary = jnp.sum(monitor[0, 1] * shape_zy[...]) - s0 * total_1 - s1 * total_2
+    real = jnp.sum(monitor[0, 0] * shape_yz[...]) + c0 * total_1 + c1 * total_2
+    imaginary = jnp.sum(monitor[0, 1] * shape_yz[...]) - s0 * total_1 - s1 * total_2
     ids = lanes((8, 128))
     part_out[...] = jnp.where(ids == 0, real, jnp.where(ids == 1, imaginary, 0.0))
 
 
 def main_kernel(
-    strips, grid_rows, ip, fp, ev, od, ff, fs, af, asums, inv_ref, design,
+    strips, grid_rows, source_at, monitor_at, fp, ev, od, staged, fs, asums, inv_ref, design,
     ev_out, od_out, s_out, p_out,
     field, sums, below, above, hmx, hmz, hmx2, hmz2, ezp, exp, pscr, sem, halo_sem,
 ):
-    strip, source, plane = ip[0], ip[1], ip[2]
-    c0, s0, c1, s1 = fp[32], fp[33], fp[34], fp[35]
-    copies = []
-    for p, f in enumerate((ff, af)):
-        copies.append(
-            (
-                pltpu.make_async_copy(f.at[0, :, 12:24], field.at[p, :, 0:12], sem.at[p, 0]),
-                pltpu.make_async_copy(f.at[0, :, 8:12], field.at[p, :, 12:16], sem.at[p, 1]),
-            )
-        )
+    strip = lax.axis_index("space")
+    source, plane = source_at[0], monitor_at[0]
+    c0, s0, c1, s1 = fp[0, 32], fp[0, 33], fp[0, 34], fp[0, 35]
     sum_copies = [
         pltpu.make_async_copy(f.at[0], sums.at[p], sem.at[p, 2]) for p, f in enumerate((fs, asums))
     ]
     for p in range(2):
-        copies[p][0].start()
-        copies[p][1].start()
         sum_copies[p].start()
     from_neighbours(
-        ip, ev, od, below, above, pl.ds(0, 2 * UP_ROWS), pl.ds(0, 2 * DOWN_ROWS), halo_sem
+        ev, od, below, above, pl.ds(0, 2 * UP_ROWS), pl.ds(0, 2 * DOWN_ROWS), halo_sem
     )
     full = (8, NX)
     row_ids = sublanes(full)
@@ -318,7 +347,7 @@
     pulse = jnp.where(ids == source, ramp, 0.0)
     sine_rows = jnp.zeros(full, jnp.float32)
     for k in range(8):
-        sine_rows = jnp.where(row_ids == k, fp[SLAB + k], sine_rows)
+        sine_rows = jnp.where(row_ids == k, fp[0, SLAB + k], sine_rows)
     sine_rows = jnp.where(ids == source, sine_rows, 0.0)
     ramp_above = 1.0 + step * (base_row + 8.5)
     ramp_below = 1.0 + step * (base_row - 0.5)
@@ -342,8 +371,8 @@
         def strip_row(c, r, p=p):
             return field[p, c, :, r, :]
 
-        copies[p][0].wait()
-        copies[p][1].wait()
+        def start(c, z, p=p):
+            return staged[p, c, slot(z)]
 
         def ex0_above(z):
             k = down0 + z - SLAB if 12 <= z <= 19 else down0 + 32 + {20: 2, 11: 1}[z]
@@ -354,16 +383,12 @@
             return above[k : k + 1]
 
         for z in range(10, 21):
-            ex, ey, ez = get(0, z), get(1, z), get(2, z)
-            hx = get(3, z) - COURANT * ((y_up(ez, ez0_above(z)) - ez) - (get(1, z + 1) - ey))
-            hy = get(4, z) - COURANT * ((get(0, z + 1) - ex) - (x_up(ez) - ez))
-            field[p, 3, slot(z)] = hx
-            field[p, 4, slot(z)] = hy
+            k = slot(z)
+            field[p, 3, k] = start(3, z) - jnp.where(last_row, COURANT * ez0_above(z), 0.0)
             if z > 10:
-                hz = get(5, z) - COURANT * ((x_up(ey) - ey) - (y_up(ex, ex0_above(z)) - ex))
-                field[p, 5, slot(z)] = hz
-        dhx = -COURANT * strip_row(2, 0)
-        dhz = COURANT * strip_row(0, 0)
+                field[p, 5, k] = start(5, z) + jnp.where(last_row, COURANT * ex0_above(z), 0.0)
+        dhx = -COURANT * staged[p, 2, :, 0, :]
+        dhz = COURANT * staged[p, 0, :, 0, :]
         block = [below[up0 + 8 * k : up0 + 8 * k + 8] for k in range(8)]
         extra = block[7]
         hmx[0:8] = has_below * (block[0] + dhx[0:8])
@@ -389,21 +414,21 @@
         drive = ab[4][3:4] + hx7[15:16]
         if forward:
             here = lanes((1, NX)) == source
-            drive = drive - jnp.where(here, fp[11] * (c0 * ramp_above), 0.0)
+            drive = drive - jnp.where(here, fp[0, 11] * (c0 * ramp_above), 0.0)
         ezp[15:16] = has_above * (ab[4][7:8] + (COURANT / OXIDE) * drive)
         for z in range(11, 21):
             k = slot(z)
             scale = COURANT * layer_inverse(z, inv_ref[0:8])
-            hx, hy, hz = get(3, z), get(4, z), get(5, z)
-            ex = get(0, z) + scale * ((hz - y_down(hz, hmz[k : k + 1])) - (hy - get(4, z - 1)))
-            ey = get(1, z) + scale * ((hx - get(3, z - 1)) - (hz - x_down(hz)))
+            hx, hy, hz = get(3, z), start(4, z), get(5, z)
+            ex = start(0, z) + scale * ((hz - y_down(hz, hmz[k : k + 1])) - (hy - start(4, z - 1)))
+            ey = start(1, z) + scale * ((hx - get(3, z - 1)) - (hz - x_down(hz)))
             field[p, 0, k] = ex
             field[p, 1, k] = ey
             if z < 20:
                 curl = (hy - x_down(hy)) - (hx - y_down(hx, hmx[k : k + 1]))
                 if forward:
-                    curl = curl - pulse * (fp[z] * c0)
-                field[p, 2, k] = get(2, z) + scale * curl
+                    curl = curl - pulse * (fp[0, z] * c0)
+                field[p, 2, k] = start(2, z) + scale * curl
         hmx2[...] = has_below * (hmx[0:8] - COURANT * (strip_row(2, 0)[0:8] - t2))
         hmz2[...] = has_below * (hmz[0:8] - COURANT * (t1 - strip_row(0, 0)[0:8]))
         for z in range(11, 20):
@@ -412,7 +437,7 @@
             field[p, 3, k] = get(3, z) - COURANT * (
                 (y_up(ez, ezp[k : k + 1]) - ez) - (get(1, z + 1) - ey)
             )
-            field[p, 4, k] = get(4, z) - COURANT * ((get(0, z + 1) - ex) - (x_up(ez) - ez))
+            field[p, 4, k] = start(4, z) - COURANT * ((get(0, z + 1) - ex) - (x_up(ez) - ez))
             if z > 11:
                 field[p, 5, k] = get(5, z) - COURANT * (
                     (x_up(ey) - ey) - (y_up(ex, exp[k : k + 1]) - ex)
@@ -425,7 +450,7 @@
             hx, hy, hz = get(3, z), get(4, z), get(5, z)
             curl_z = (hy - x_down(hy)) - (hx - y_down(hx, hmx2[k : k + 1]))
             if forward:
-                curl_z = curl_z - pulse * (fp[z] * c1)
+                curl_z = curl_z - pulse * (fp[0, z] * c1)
             curls = (
                 (hz - y_down(hz, hmz2[k : k + 1])) - (hy - get(4, z - 1)),
                 (hx - get(3, z - 1)) - (hz - x_down(hz)),
@@ -455,7 +480,7 @@
     drive_1 = jnp.zeros((8, 256), jnp.float32)
     hx_last = hy_last = None
     for z in range(11, 20):
-        d1 = spot * layer_inverse(z, inv_w) * (-COURANT * fp[z])
+        d1 = spot * layer_inverse(z, inv_w) * (-COURANT * fp[0, z])
         hy = COURANT * (x_up(d1[0:8]) - d1[0:8])
         hx = keep * (-COURANT * (roll_up(d1) - d1))
         if z > 11:
@@ -487,17 +512,21 @@
     od_out[...] = jnp.where(even, to_down, to_up)
 
 
-def final_kernel(norm, ip, fp, ev, od, s_own, p_own, totals, keep, send, scr):
-    strip, plane, group = ip[0], ip[2], ip[3]
+def final_kernel(norm, monitor_at, fp, ev, od, s_own, p_own, totals, keep, send, merit, scr):
+    strip, group = lax.axis_index("space"), lax.axis_index("exc")
+    plane = monitor_at[0]
     even = strip % 2 == 0
     low = jnp.where(even, od[...], ev[...])
     high = jnp.where(even, ev[...], od[...])
+    sums = totals[...] + ev[4:5, 512:640]
+    ids = lanes((1, 128))
+    real = jnp.sum(jnp.where(ids == 0, sums, 0.0), axis=1, keepdims=True) / norm
+    imaginary = jnp.sum(jnp.where(ids == 1, sums, 0.0), axis=1, keepdims=True) / norm
     both = jnp.concatenate([low[0:4], s_own[...], high[0:4]], 0)
     extra = jnp.concatenate([low[4:8, 0:512], p_own[:, 0:512], high[4:8, 0:512]], 0)
-    real = totals[0, 0] / norm
-    imaginary = totals[0, 1] / norm
-    g0 = real * fp[32] + imaginary * fp[33]
-    g1 = real * fp[34] + imaginary * fp[35]
+    merit[...] = jnp.broadcast_to(real * real + imaginary * imaginary, (1, 128))
+    g0 = real * fp[0, 32] + imaginary * fp[0, 33]
+    g1 = real * fp[0, 34] + imaginary * fp[0, 35]
     more = y_smooth(extra, 8)
     w1 = window_start(plane - 1)
     scr[...] = y_smooth(both, 8)
@@ -537,7 +566,6 @@
     groups = lax.axis_size("exc")
     strips = lax.axis_size("space")
     grid_rows = ROWS * strips
-    strip = lax.axis_index("space").astype(jnp.int32)
     group = lax.axis_index("exc").astype(jnp.int32)
     f32 = jnp.float32
 
@@ -547,31 +575,30 @@
     even_pairs = [(i, i ^ 1) for i in range(strips)]
     odd_pairs = [(i, ((i - 1) ^ 1) + 1) for i in range(1, strips - 1)]
 
-    ip = jnp.stack([strip, source_plane[0], monitor_plane[0], group])
-    number = jnp.arange(128, dtype=jnp.int32)
-    order = math.pi * (mode_numbers[0] + 1).astype(f32)
-    early = start_phase[0]
-    late = start_phase[0] + frequency[0]
-    angle = jnp.where(number < 34, early, late)
-    angle = jnp.where(number < NZ, order * (number.astype(f32) + 0.5) / NZ, angle)
-    fp = jnp.where((number == 32) | (number == 34), jnp.cos(angle), jnp.sin(angle))
-    factor = frequency[0] * frequency[0] * ((SILICON - OXIDE) / math.sqrt(groups * DZ))
-    fp = jnp.where(number == 36, factor, fp)
-    own_rows = (strip * ROWS + jnp.arange(ROWS, dtype=jnp.int32)).astype(f32)
-    layers = jnp.arange(NZ, dtype=f32) + 0.5
-    ramp = 1.0 + 2.0 * (own_rows + 0.5) / grid_rows
-    shape_zy = jnp.sin(order * layers / NZ)[:, None] * ramp[None, :]
+    fp, shape_yz = pl.pallas_call(
+        lambda *refs: prepare_kernel(grid_rows, (SILICON - OXIDE) / math.sqrt(groups * DZ), *refs),
+        out_shape=[shaped(1, 128), shaped(ROWS, NZ)],
+        in_specs=[SMEM_SPEC] * 3,
+        out_specs=[VMEM_SPEC] * 2,
+        name="prepare",
+    )(mode_numbers, frequency, start_phase)
 
     quarter = density.T
     width = quarter.shape[1]
-    small = jnp.concatenate([labels.astype(f32), quarter], 1)
+    second = swap(quarter, "exc", [(i, i ^ 1) for i in range(groups)])
+    third = swap(
+        jnp.concatenate([quarter, second], 0), "exc", [(i, i ^ 2) for i in range(groups)]
+    )
+    small = jnp.concatenate(
+        [quarter, second, third[0:8], third[8:16], labels.astype(f32)], 1
+    )
     od_small = swap(small, "space", odd_pairs)
     ev_small = swap(small, "space", even_pairs)
 
     ev, od = pl.pallas_call(
         pack_kernel,
         out_shape=[shaped(PACK, NX), shaped(PACK, NX)],
-        in_specs=[SMEM_SPEC, ANY_SPEC, ANY_SPEC],
+        in_specs=[ANY_SPEC] * 3,
         out_specs=[ANY_SPEC, ANY_SPEC],
         scratch_shapes=[
             pltpu.VMEM((2, 4, 6, 16, NX), f32),
@@ -580,17 +607,22 @@
             pltpu.SemaphoreType.DMA((2, 4)),
             pltpu.SemaphoreType.DMA((2,)),
         ],
-        compiler_params=params(),
+        compiler_params=params(PACK_LIMIT),
         name="pack",
-    )(ip, forward_fields, adjoint_fields)
+    )(second, forward_fields, adjoint_fields)
+    staged = pl.pallas_call(
+        stage_kernel,
+        out_shape=shaped(2, 6, 16, ROWS, NX),
+        in_specs=[ANY_SPEC] * 3,
+        out_specs=VMEM_SPEC,
+        scratch_shapes=[pltpu.SemaphoreType.DMA((2, 2))],
+        compiler_params=params(PACK_LIMIT),
+        name="stage",
+    )(small, forward_fields, adjoint_fields)
     od = swap(od, "space", odd_pairs)
     ev = swap(ev, "space", even_pairs)
 
-    first = jnp.concatenate([quarter, ev_small[:, NX:], od_small[:, NX:]], 0)
-    second = swap(first, "exc", [(i, i ^ 1) for i in range(groups)])
-    third = swap(
-        jnp.concatenate([first, second], 0), "exc", [(i, i ^ 2) for i in range(groups)]
-    )
+    fp, staged = lax.optimization_barrier((fp, staged))
 
     def material(*refs):
         material_kernel(grid_rows, *refs)
@@ -598,7 +630,7 @@
     inv, design, part = pl.pallas_call(
         material,
         out_shape=[shaped(16, NX), shaped(8, NX), shaped(8, 128)],
-        in_specs=[SMEM_SPEC, SMEM_SPEC] + [VMEM_SPEC] * 8 + [ANY_SPEC],
+        in_specs=[SMEM_SPEC, SMEM_SPEC] + [VMEM_SPEC] * 5 + [ANY_SPEC],
         out_specs=[VMEM_SPEC] * 3,
         scratch_shapes=[
             pltpu.VMEM((24, NX), f32),
@@ -608,21 +640,23 @@
         compiler_params=params(),
         name="material",
     )(
-        ip, fp, ev_small, od_small, labels, first, second, third, monitor_sums, shape_zy,
+        source_plane, fp, ev_small, od_small, small, monitor_sums.transpose(0, 1, 3, 2), shape_yz,
         forward_fields,
     )
 
     totals = part[0:1]
-    for bit in (8, 24, 4, 1, 3):
-        totals = totals + swap(totals, "space", [(i, i ^ bit) for i in range(strips)])
-
+
+    def fold(totals, bit):
+        return totals + swap(totals, "space", [(i, i ^ bit) for i in range(strips)])
+
+    arriving = swap(totals, "space", [(i, i ^ 4) for i in range(strips)])
     def main(*refs):
         main_kernel(strips, grid_rows, *refs)
 
     ev3, od3, s_own, p_own = pl.pallas_call(
         main,
         out_shape=[shaped(8, NX)] * 4,
-        in_specs=[SMEM_SPEC, SMEM_SPEC] + [ANY_SPEC] * 6 + [VMEM_SPEC] * 2,
+        in_specs=[SMEM_SPEC] * 3 + [ANY_SPEC] * 2 + [VMEM_SPEC] + [ANY_SPEC] * 2 + [VMEM_SPEC] * 2,
         out_specs=[VMEM_SPEC] * 4,
         scratch_shapes=[
             pltpu.VMEM((2, 6, 16, ROWS, NX), f32),
@@ -641,9 +675,16 @@
         ],
         compiler_params=params(),
         name="main",
-    )(ip, fp, ev, od, forward_fields, forward_sums, adjoint_fields, adjoint_sums, inv, design)
-    ev3 = swap(ev3, "space", even_pairs)
+    )(
+        source_plane, monitor_plane, fp, ev, od, staged, forward_sums, adjoint_sums, inv, design,
+    )
+    od3, totals = lax.optimization_barrier((od3, totals))
+    totals = totals + arriving
     od3 = swap(od3, "space", odd_pairs)
+    totals = fold(totals, 8)
+    totals = fold(totals, 24)
+    totals = fold(totals, 3)
+    ev3 = swap(lax.dynamic_update_slice(ev3, totals, (4, 512)), "space", even_pairs)
 
     norm = math.sqrt(NZ * grid_rows)
     half_count = groups // 2
@@ -651,15 +692,15 @@
     def final(*refs):
         final_kernel(norm, *refs)
 
-    keep, send = pl.pallas_call(
+    keep, send, merit = pl.pallas_call(
         final,
-        out_shape=[shaped(half_count, ROWS, width)] * 2,
-        in_specs=[SMEM_SPEC, SMEM_SPEC] + [VMEM_SPEC] * 4 + [SMEM_SPEC],
-        out_specs=[VMEM_SPEC] * 2,
+        out_shape=[shaped(half_count, ROWS, width)] * 2 + [shaped(1, 128)],
+        in_specs=[SMEM_SPEC, SMEM_SPEC] + [VMEM_SPEC] * 5,
+        out_specs=[VMEM_SPEC] * 3,
         scratch_shapes=[pltpu.VMEM((8, NX), f32)],
         compiler_params=params(),
         name="final",
-    )(ip, fp, ev3, od3, s_own, p_own, totals)
+    )(monitor_plane, fp, ev3, od3, s_own, p_own, totals)
     block = keep + swap(send, "exc", [(i, i ^ 1) for i in range(groups)])
     bit = 2
     while bit < groups:
@@ -670,8 +711,7 @@
         given = lax.dynamic_index_in_dim(pairs, 1 - mine, 1, keepdims=False)
         block = kept + swap(given, "exc", [(i, i ^ bit) for i in range(groups)])
         bit *= 2
-    real, imaginary = totals[0, 0:1] / norm, totals[0, 1:2] / norm
-    return block[0].T, real * real + imaginary * imaginary
+    return block[0].T, merit[0, 0:1]
 
 
 def solution(mesh):

time: 76 us -> 67.5 us (0.89)
  starting transfers between devices: 29.1 us -> 22.9 us
  Pallas kernels: 13.5 us -> 17.4 us
  between operations: 7.87 us -> 4.13 us
  waiting for transfers between devices: 21.8 us -> 20.5 us
  other arithmetic: 2.35 us -> 1.33 us
    ppermute x15 -> x14, starting transfers between devices: 29.1 us -> 22.9 us  [swap(): return lax.ppermute(value, axis, pairs)]
    pallas_call x2 -> x4, Pallas kernels: 6.46 us -> 11.7 us  [the longest x1 5.9 us: local(): pl.pallas_call(stage_kernel, out_shape=shaped(2, 6, 16, ROWS, NX), in_spe...]
    ppermute x15 -> x14, waiting for transfers between devices: 21.8 us -> 20.5 us  [swap(): return lax.ppermute(value, axis, pairs)]
    pallas_call x1, Pallas kernels: 3.38 us -> 2.33 us  [local(): pl.pallas_call(material, out_shape=[shaped(16, NX), shaped(8, NX), shaped...]
    convert_element_type x1 -> x0, other arithmetic: 0.76 us -> none  [local(): small = jnp.concatenate([labels.astype(f32), quarter], 1)]
  transfers between devices with their start and end apart: 15 -> 14, of which waited for: 7 -> 7; matrix products, arithmetic and copies ran while one was open for 1% -> 1% of each run, Pallas kernels for 17% -> 24%
where the time goes in v3:
time: 67.5 us; the launch traced here: 67.2 us
  starting transfers between devices  22.9 us (34%)
  waiting for transfers between devices  20.5 us (30%)
  Pallas kernels  17.4 us (26%)
  between operations  4.13 us (6%)
  other arithmetic  1.33 us (2%)
  local copies, waits for them, and re-layouts  0.99 us (1%)
    ppermute x14, starting transfers between devices, swap(): return lax.ppermute(value, axis, pairs)  22.9 us
    ppermute x14, waiting for transfers between devices, swap(): return lax.ppermute(value, axis, pairs)  20.5 us
    pallas_call x1, Pallas kernels, local(): pl.pallas_call(stage_kernel, out_shape=shaped(2, 6, 16, ROWS, NX), in_spe...  5.9 us
    pallas_call x1, Pallas kernels, local(): pl.pallas_call(main, out_shape=[shaped(8, NX)] * 4, in_specs=[SMEM_SPEC]...  3.81 us
    pallas_call x1, Pallas kernels, local(): pl.pallas_call(pack_kernel, out_shape=[shaped(PACK, NX), shaped(PACK, NX)...  3.35 us
    pallas_call x1, Pallas kernels, local(): pl.pallas_call(material, out_shape=[shaped(16, NX), shaped(8, NX), shaped...  2.33 us
  transfers between devices with their start and end apart: 14, of which 7 were waited for; matrix products, arithmetic and copies ran while one was open for 1% of the time, Pallas kernels for 24%

profile of v3, /device:TPU:6, one launch (start us, length us, event | category | flops | bytes accessed | tf_op | source)
XLA Modules:
  0.0 67.2 jit_solution(14359051598978516574)
XLA Ops:
  0.7 0.7 %constant_dynamic-update-slice_fusion.3 = f32[8,2048]{1,0:T(8,128)S(1)} fusion(f32[256,8]{0,1:T(8,128)} %param.17), kind=kLoop, calls=%fused_computation.5 | loop fusion | bytes 16384
  1.4 0.7 collective-permute-done.after
  2.1 0.7 %pad_maximum_fusion = f32[16,256]{1,0:T(8,128)S(1)} fusion(f32[8,256]{1,0:T(8,128)S(1)} %collective-permute-done.after, f32[8,256]{1,0:T(8,128)} %bitcast.13), kind=kLoop, calls=%fused_computation.1 | loop fusion | flops 4096 | bytes 32768 | tf_op jit(solution)/shard_map/concatenate | solution.py:590
  2.8 1.6 %collective-permute-start.1 = (f32[16,256]{1,0:T(8,128)S(1)}, f32[16,256]{1,0:T(8,128)S(1)}, u32[]{:S(2)}, u32[]{:S(2)}) collective-permute-start(f32[16,256]{1,0:T(8,128)S(1)} %pad_maximum_fusion), channel_id=1, source_target_pairs={{0,64},{32,96},{64,0},{96,32},{1,65},{33,97},{65,1},{97,33},{2,66}... | collective-permute-start | bytes 49160 | tf_op jit(solution)/shard_map/ppermute | solution.py:559
  4.4 3.3 %pack.1 = (f32[128,1024]{1,0:T(8,128)}, f32[128,1024]{1,0:T(8,128)}) custom-call(f32[8,256]{1,0:T(8,128)S(1)} %collective-permute-done.after, f32[1,6,32,8,1024]{4,3,2,1,0:T(8,128)} %refs_7_.2, f32[1,6,32,8,1024]{4,3,2,1,0:T(8,128)} %af.3), custom_call_target="tpu_custom_call" | custom-call | tf_op jit(solution)/shard_map/pack/pallas_call | solution.py:598
  7.7 2.0 %collective-permute-start.2 = (f32[128,1024]{1,0:T(8,128)}, f32[128,1024]{1,0:T(8,128)S(1)}, u32[]{:S(2)}, u32[]{:S(2)}) collective-permute-start(f32[128,1024]{1,0:T(8,128)} %get-tuple-element.22), channel_id=1, source_target_pairs={{0,1},{1,0},{2,3},{3,2},{4,5},{5,4},{6,7},{7,6},{8,9},{9,8},{10,11... | collective-permute-start | bytes 1572872 | tf_op jit(solution)/shard_map/ppermute | solution.py:559
  9.7 7.0 %collective-permute-start.3 = (f32[128,1024]{1,0:T(8,128)}, f32[128,1024]{1,0:T(8,128)S(1)}, u32[]{:S(2)}, u32[]{:S(2)}) collective-permute-start(f32[128,1024]{1,0:T(8,128)} %get-tuple-element.23), channel_id=1, source_target_pairs={{1,2},{2,1},{3,4},{4,3},{5,6},{6,5},{7,8},{8,7},{9,10},{10,9},{11,... | collective-permute-start | bytes 1572872 | tf_op jit(solution)/shard_map/ppermute | solution.py:559
  16.8 3.3 %collective-permute-start.5 = (f32[8,2048]{1,0:T(8,128)S(1)}, f32[8,2048]{1,0:T(8,128)S(1)}, u32[]{:S(2)}, u32[]{:S(2)}) collective-permute-start(f32[8,2048]{1,0:T(8,128)S(1)} %convert_dynamic-update-slice_fusion.after.refs_4_), channel_id=1, source_target_pairs={{1,2},{2,1},{3,4},{4,3},{5,6},{6,5},{7,8},{8,7},{9,10},{10,9},{11,... | collective-permute-start | bytes 196616 | tf_op jit(solution)/shard_map/ppermute | solution.py:559
  23.5 0.6 prepare.1
  24.2 5.9 %stage.1.refs_5_ = f32[2,6,16,8,1024]{4,3,2,1,0:T(8,128)} custom-call(f32[8,2048]{1,0:T(8,128)S(1)} %convert_dynamic-update-slice_fusion.after.refs_4_, f32[1,6,32,8,1024]{4,3,2,1,0:T(8,128)} %refs_7_.2, f32[1,6,32,8,1024]{4,3,2,1,0:T(8,128)} %af.3), custom_call_target="tpu_custom_call" | custom-call | tf_op jit(solution)/shard_map/stage/pallas_call | solution.py:613
  30.1 1.1 %collective-permute-done.5.refs_3_ = f32[8,2048]{1,0:T(8,128)S(1)} collective-permute-done((f32[8,2048]{1,0:T(8,128)S(1)}, f32[8,2048]{1,0:T(8,128)S(1)}, u32[]{:S(2)}, u32[]{:S(2)}) %collective-permute-start.5) | collective-permute-done | bytes 65568 | tf_op jit(solution)/shard_map/ppermute | solution.py:559
  31.2 2.3 %material.1 = (f32[16,1024]{1,0:T(8,128)S(1)}, f32[8,1024]{1,0:T(8,128)S(1)}, f32[8,128]{1,0:T(8,128)S(1)}) custom-call(s32[1]{0:T(128)S(6)} %copy.19.refs_0_, f32[1,128]{1,0:T(1,128)S(1)} %copy-done.4, f32[8,2048]{1,0:T(8,128)S(1)} %collective-permute-done.4.refs_2_, f32[8,2048]{1,0:T(8,128)S(1)} %collective-permute-done.5.refs_3_, ...), custom_call_target="tpu_custom_call" | custom-call | tf_op jit(solution)/shard_map/material/pallas_call | solution.py:630
  33.6 2.1 %collective-permute-start.6 = (f32[1,128]{1,0:T(1,128)S(1)}, f32[1,128]{1,0:T(1,128)S(1)}, u32[]{:S(2)}, u32[]{:S(2)}) collective-permute-start(f32[1,128]{1,0:T(1,128)S(1)} %slice.14), channel_id=1, source_target_pairs={{0,4},{1,5},{2,6},{3,7},{4,0},{5,1},{6,2},{7,3},{8,12},{9,13},{10,... | collective-permute-start | bytes 1544 | tf_op jit(solution)/shard_map/ppermute | solution.py:559
  35.7 3.8 %main.1 = (f32[8,1024]{1,0:T(8,128)S(1)}, f32[8,1024]{1,0:T(8,128)S(1)}, f32[8,1024]{1,0:T(8,128)S(1)}, f32[8,1024]{1,0:T(8,128)S(1)}) custom-call(s32[1]{0:T(128)S(6)} %copy.19.refs_0_, s32[1]{0:T(128)S(6)} %copy.20.refs_1_.refs_0_, f32[1,128]{1,0:T(1,128)S(1)} %copy-done.4, f32[128,1024]{1,0:T(8,128)S(1)} %collective-permute-done.2.refs_3_, ...), custom_call_target="tpu_custom_call" | custom-call | tf_op jit(solution)/shard_map/main/pallas_call | solution.py:656
  39.5 0.9 %collective-permute-start.7 = (f32[1,128]{1,0:T(1,128)S(1)}, f32[1,128]{1,0:T(1,128)S(1)}, u32[]{:S(2)}, u32[]{:S(2)}) collective-permute-start(f32[1,128]{1,0:T(1,128)S(1)} %add.31), channel_id=1, source_target_pairs={{0,8},{1,9},{2,10},{3,11},{4,12},{5,13},{6,14},{7,15},{8,0},{9,1},... | collective-permute-start | bytes 1544 | tf_op jit(solution)/shard_map/ppermute | solution.py:559
  40.4 2.7 %collective-permute-done.7 = f32[1,128]{1,0:T(1,128)S(1)} collective-permute-done((f32[1,128]{1,0:T(1,128)S(1)}, f32[1,128]{1,0:T(1,128)S(1)}, u32[]{:S(2)}, u32[]{:S(2)}) %collective-permute-start.7) | collective-permute-done | bytes 544 | tf_op jit(solution)/shard_map/ppermute | solution.py:559
  43.6 4.3 %collective-permute-done.8 = f32[1,128]{1,0:T(1,128)S(1)} collective-permute-done((f32[1,128]{1,0:T(1,128)S(1)}, f32[1,128]{1,0:T(1,128)S(1)}, u32[]{:S(2)}, u32[]{:S(2)}) %collective-permute-start.8) | collective-permute-done | bytes 544 | tf_op jit(solution)/shard_map/ppermute | solution.py:559
  47.9 2.2 %collective-permute-start.9 = (f32[1,128]{1,0:T(1,128)S(1)}, f32[1,128]{1,0:T(1,128)S(1)}, u32[]{:S(2)}, u32[]{:S(2)}) collective-permute-start(f32[1,128]{1,0:T(1,128)S(1)} %add.33), channel_id=1, source_target_pairs={{0,3},{1,2},{2,1},{3,0},{4,7},{5,6},{6,5},{7,4},{8,11},{9,10},{10,... | collective-permute-start | bytes 1544 | tf_op jit(solution)/shard_map/ppermute | solution.py:559
  50.1 2.9 %collective-permute-start.11 = (f32[8,1024]{1,0:T(8,128)S(1)}, f32[8,1024]{1,0:T(8,128)S(1)}, u32[]{:S(2)}, u32[]{:S(2)}) collective-permute-start(f32[8,1024]{1,0:T(8,128)S(1)} %get-tuple-element.32), channel_id=1, source_target_pairs={{1,2},{2,1},{3,4},{4,3},{5,6},{6,5},{7,8},{8,7},{9,10},{10,9},{11,... | collective-permute-start | bytes 98312 | tf_op jit(solution)/shard_map/ppermute | solution.py:559
  53.4 7.0 %collective-permute-done.11.refs_3_ = f32[8,1024]{1,0:T(8,128)S(1)} collective-permute-done((f32[8,1024]{1,0:T(8,128)S(1)}, f32[8,1024]{1,0:T(8,128)S(1)}, u32[]{:S(2)}, u32[]{:S(2)}) %collective-permute-start.11) | collective-permute-done | bytes 32800 | tf_op jit(solution)/shard_map/ppermute | solution.py:559
  60.5 1.3 %final.1 = (f32[2,8,256]{2,1,0:T(8,128)S(1)}, f32[2,8,256]{2,1,0:T(8,128)S(1)}, f32[1,128]{1,0:T(1,128)}) custom-call(s32[1]{0:T(128)S(6)} %copy.20.refs_1_.refs_0_, f32[1,128]{1,0:T(1,128)S(1)} %copy-done.4, f32[8,1024]{1,0:T(8,128)S(1)} %collective-permute-done.10.refs_2_, f32[8,1024]{1,0:T(8,128)S(1)} %collective-permute-done.11.refs_3_, ...), custom_call_target="tpu_custom_call" | custom-call | tf_op jit(solution)/shard_map/final/pallas_call | solution.py:695
  61.8 1.2 %collective-permute-done.12 = f32[2,8,256]{2,1,0:T(8,128)S(1)} collective-permute-done((f32[2,8,256]{2,1,0:T(8,128)S(1)}, f32[2,8,256]{2,1,0:T(8,128)S(1)}, u32[]{:S(2)}, u32[]{:S(2)}) %collective-permute-start.12) | collective-permute-done | bytes 16416 | tf_op jit(solution)/shard_map/ppermute | solution.py:559
  63.1 3.5 %collective-permute-done.13 = f32[1,8,256]{2,1,0:T(8,128)S(1)} collective-permute-done((f32[1,8,256]{2,1,0:T(8,128)S(1)}, f32[1,8,256]{2,1,0:T(8,128)S(1)}, u32[]{:S(2)}, u32[]{:S(2)}) %collective-permute-start.13) | collective-permute-done | bytes 8224 | tf_op jit(solution)/shard_map/ppermute | solution.py:559
  66.6 0.6 add_bitcast_fusion
  (44 shorter events, 1.2 us)
Async XLA Ops:
  0.6 1.5 %collective-permute-start = (f32[8,256]{1,0:T(8,128)}, f32[8,256]{1,0:T(8,128)S(1)}, u32[]{:S(2)}, u32[]{:S(2)}) collective-permute-start(f32[8,256]{1,0:T(8,128)} %bitcast.12), channel_id=1, source_target_pairs={{0,32},{32,0},{64,96},{96,64},{1,33},{33,1},{65,97},{97,65},{2,34}... | collective-permute-start | bytes 24584 | tf_op jit(solution)/shard_map/ppermute | solution.py:559
  2.8 14.0 %copy-start.6 = (s32[8,1024]{1,0:T(8,128)S(1)}, s32[8,1024]{1,0:T(8,128)}, u32[]{:S(2)}) copy-start(s32[8,1024]{1,0:T(8,128)} %param.18) | copy-start | bytes 98308
  2.8 14.0 %collective-permute-start.1 = (f32[16,256]{1,0:T(8,128)S(1)}, f32[16,256]{1,0:T(8,128)S(1)}, u32[]{:S(2)}, u32[]{:S(2)}) collective-permute-start(f32[16,256]{1,0:T(8,128)S(1)} %pad_maximum_fusion), channel_id=1, source_target_pairs={{0,64},{32,96},{64,0},{96,32},{1,65},{33,97},{65,1},{97,33},{2,66}... | collective-permute-start | bytes 49160 | tf_op jit(solution)/shard_map/ppermute | solution.py:559
  4.4 26.8 %slice-start = ((s8[6291456]{0:T(1024)(128)(4,1)}), s8[2097152]{0:T(1024)(128)(4,1)S(1)}, s32[]{:S(2)}) async-start(s8[6291456]{0:T(1024)(128)(4,1)} %bitcast.9), calls=%async_computation | async-start | bytes 4194304
  7.7 27.9 %collective-permute-start.2 = (f32[128,1024]{1,0:T(8,128)}, f32[128,1024]{1,0:T(8,128)S(1)}, u32[]{:S(2)}, u32[]{:S(2)}) collective-permute-start(f32[128,1024]{1,0:T(8,128)} %get-tuple-element.22), channel_id=1, source_target_pairs={{0,1},{1,0},{2,3},{3,2},{4,5},{5,4},{6,7},{7,6},{8,9},{9,8},{10,11... | collective-permute-start | bytes 1572872 | tf_op jit(solution)/shard_map/ppermute | solution.py:559
  9.7 25.9 %collective-permute-start.3 = (f32[128,1024]{1,0:T(8,128)}, f32[128,1024]{1,0:T(8,128)S(1)}, u32[]{:S(2)}, u32[]{:S(2)}) collective-permute-start(f32[128,1024]{1,0:T(8,128)} %get-tuple-element.23), channel_id=1, source_target_pairs={{1,2},{2,1},{3,4},{4,3},{5,6},{6,5},{7,8},{8,7},{9,10},{10,9},{11,... | collective-permute-start | bytes 1572872 | tf_op jit(solution)/shard_map/ppermute | solution.py:559
  16.8 14.3 %collective-permute-start.5 = (f32[8,2048]{1,0:T(8,128)S(1)}, f32[8,2048]{1,0:T(8,128)S(1)}, u32[]{:S(2)}, u32[]{:S(2)}) collective-permute-start(f32[8,2048]{1,0:T(8,128)S(1)} %convert_dynamic-update-slice_fusion.after.refs_4_), channel_id=1, source_target_pairs={{1,2},{2,1},{3,4},{4,3},{5,6},{6,5},{7,8},{8,7},{9,10},{10,9},{11,... | collective-permute-start | bytes 196616 | tf_op jit(solution)/shard_map/ppermute | solution.py:559
  20.2 11.0 %collective-permute-start.4 = (f32[8,2048]{1,0:T(8,128)S(1)}, f32[8,2048]{1,0:T(8,128)S(1)}, u32[]{:S(2)}, u32[]{:S(2)}) collective-permute-start(f32[8,2048]{1,0:T(8,128)S(1)} %convert_dynamic-update-slice_fusion.after.refs_4_), channel_id=1, source_target_pairs={{0,1},{1,0},{2,3},{3,2},{4,5},{5,4},{6,7},{7,6},{8,9},{9,8},{10,11... | collective-permute-start | bytes 196616 | tf_op jit(solution)/shard_map/ppermute | solution.py:559
  24.1 7.0 %slice-start.1 = ((s8[6291456]{0:T(1024)(128)(4,1)}), s8[4194304]{0:T(1024)(128)(4,1)S(1)}, s32[]{:S(2)}) async-start(s8[6291456]{0:T(1024)(128)(4,1)} %bitcast.9), calls=%async_computation.1 | async-start | bytes 8388608
  24.1 7.1 %copy-start.3 = (f32[1,2,32,8]{2,3,1,0:T(8,128)S(1)}, f32[1,2,32,8]{2,3,1,0:T(8,128)}, u32[]{:S(2)}) copy-start(f32[1,2,32,8]{2,3,1,0:T(8,128)} %param.16) | copy-start | bytes 6148
  24.1 7.1 %copy-start.4 = (f32[1,128]{1,0:T(1,128)S(1)}, f32[1,128]{1,0:T(1,128)}, u32[]{:S(2)}) copy-start(f32[1,128]{1,0:T(1,128)} %get-tuple-element.21.refs_1_.refs_2_) | copy-start | bytes 1540
  24.1 7.1 %copy-start.5 = (f32[8,32]{1,0:T(8,128)S(1)}, f32[8,32]{1,0:T(8,128)}, u32[]{:S(2)}) copy-start(f32[8,32]{1,0:T(8,128)} %get-tuple-element.25.refs_6_) | copy-start | bytes 3076
  24.1 11.5 %copy-start.1 = (f32[1,6,8,8,1024]{4,3,2,1,0:T(8,128)S(1)}, f32[1,6,8,8,1024]{4,3,2,1,0:T(8,128)}, u32[]{:S(2)}) copy-start(f32[1,6,8,8,1024]{4,3,2,1,0:T(8,128)} %refs_6_.1) | copy-start | bytes 4718596
  24.2 11.5 %copy-start.2 = (f32[1,6,8,8,1024]{4,3,2,1,0:T(8,128)S(1)}, f32[1,6,8,8,1024]{4,3,2,1,0:T(8,128)}, u32[]{:S(2)}) copy-start(f32[1,6,8,8,1024]{4,3,2,1,0:T(8,128)} %refs_7_.3) | copy-start | bytes 4718596
  30.1 5.6 %copy-start = (f32[2,6,16,8,1024]{4,3,2,1,0:T(8,128)S(1)}, f32[2,6,16,8,1024]{4,3,2,1,0:T(8,128)}, u32[]{:S(2)}) copy-start(f32[2,6,16,8,1024]{4,3,2,1,0:T(8,128)} %stage.1.refs_5_) | copy-start | bytes 18874372
  33.6 5.9 %collective-permute-start.6 = (f32[1,128]{1,0:T(1,128)S(1)}, f32[1,128]{1,0:T(1,128)S(1)}, u32[]{:S(2)}, u32[]{:S(2)}) collective-permute-start(f32[1,128]{1,0:T(1,128)S(1)} %slice.14), channel_id=1, source_target_pairs={{0,4},{1,5},{2,6},{3,7},{4,0},{5,1},{6,2},{7,3},{8,12},{9,13},{10,... | collective-permute-start | bytes 1544 | tf_op jit(solution)/shard_map/ppermute | solution.py:559
  39.5 3.6 %collective-permute-start.7 = (f32[1,128]{1,0:T(1,128)S(1)}, f32[1,128]{1,0:T(1,128)S(1)}, u32[]{:S(2)}, u32[]{:S(2)}) collective-permute-start(f32[1,128]{1,0:T(1,128)S(1)} %add.31), channel_id=1, source_target_pairs={{0,8},{1,9},{2,10},{3,11},{4,12},{5,13},{6,14},{7,15},{8,0},{9,1},... | collective-permute-start | bytes 1544 | tf_op jit(solution)/shard_map/ppermute | solution.py:559
  43.2 4.8 %collective-permute-start.8 = (f32[1,128]{1,0:T(1,128)S(1)}, f32[1,128]{1,0:T(1,128)S(1)}, u32[]{:S(2)}, u32[]{:S(2)}) collective-permute-start(f32[1,128]{1,0:T(1,128)S(1)} %add.32), channel_id=1, source_target_pairs={{0,24},{1,25},{2,26},{3,27},{4,28},{5,29},{6,30},{7,31},{8,16},{9,... | collective-permute-start | bytes 1544 | tf_op jit(solution)/shard_map/ppermute | solution.py:559
  47.9 5.2 %collective-permute-start.9 = (f32[1,128]{1,0:T(1,128)S(1)}, f32[1,128]{1,0:T(1,128)S(1)}, u32[]{:S(2)}, u32[]{:S(2)}) collective-permute-start(f32[1,128]{1,0:T(1,128)S(1)} %add.33), channel_id=1, source_target_pairs={{0,3},{1,2},{2,1},{3,0},{4,7},{5,6},{6,5},{7,4},{8,11},{9,10},{10,... | collective-permute-start | bytes 1544 | tf_op jit(solution)/shard_map/ppermute | solution.py:559
  50.1 10.3 %collective-permute-start.11 = (f32[8,1024]{1,0:T(8,128)S(1)}, f32[8,1024]{1,0:T(8,128)S(1)}, u32[]{:S(2)}, u32[]{:S(2)}) collective-permute-start(f32[8,1024]{1,0:T(8,128)S(1)} %get-tuple-element.32), channel_id=1, source_target_pairs={{1,2},{2,1},{3,4},{4,3},{5,6},{6,5},{7,8},{8,7},{9,10},{10,9},{11,... | collective-permute-start | bytes 98312 | tf_op jit(solution)/shard_map/ppermute | solution.py:559
  53.3 7.1 %collective-permute-start.10 = (f32[8,1024]{1,0:T(8,128)S(1)}, f32[8,1024]{1,0:T(8,128)S(1)}, u32[]{:S(2)}, u32[]{:S(2)}) collective-permute-start(f32[8,1024]{1,0:T(8,128)S(1)} %dynamic_update_slice.3), channel_id=1, source_target_pairs={{0,1},{1,0},{2,3},{3,2},{4,5},{5,4},{6,7},{7,6},{8,9},{9,8},{10,11... | collective-permute-start | bytes 98312 | tf_op jit(solution)/shard_map/ppermute | solution.py:559
  61.8 1.2 %collective-permute-start.12 = (f32[2,8,256]{2,1,0:T(8,128)S(1)}, f32[2,8,256]{2,1,0:T(8,128)S(1)}, u32[]{:S(2)}, u32[]{:S(2)}) collective-permute-start(f32[2,8,256]{2,1,0:T(8,128)S(1)} %get-tuple-element.36), channel_id=1, source_target_pairs={{0,32},{32,0},{64,96},{96,64},{1,33},{33,1},{65,97},{97,65},{2,34}... | collective-permute-start | bytes 49160 | tf_op jit(solution)/shard_map/ppermute | solution.py:559
  63.0 3.7 %collective-permute-start.13 = (f32[1,8,256]{2,1,0:T(8,128)S(1)}, f32[1,8,256]{2,1,0:T(8,128)S(1)}, u32[]{:S(2)}, u32[]{:S(2)}) collective-permute-start(f32[1,8,256]{2,1,0:T(8,128)S(1)} %constant_dynamic-slice_fusion), channel_id=1, source_target_pairs={{0,64},{32,96},{64,0},{96,32},{1,65},{33,97},{65,1},{97,33},{2,66}... | collective-permute-start | bytes 24584 | tf_op jit(solution)/shard_map/ppermute | solution.py:559

commit v4 on v3

--- a/solution.py
+++ b/solution.py
@@ -79,85 +79,88 @@
     return total
 
 
-def prepare_kernel(grid_rows, scale, mode, rate, phase, fp, shape_yz):
-    order = math.pi * (mode[0] + 1).astype(jnp.float32)
+def prepare_kernel(grid_rows, scale, mode_at, rate_at, phase_at, source_at, monitor_at, fp, shape_yz):
+    order = math.pi * (mode_at[...] + 1).astype(jnp.float32)
+    rate, phase = rate_at[...], phase_at[...]
     number = lanes((1, 128))
-    early, late = phase[0], phase[0] + rate[0]
+    early, late = phase, phase + rate
     angle = jnp.where(number < 34, early, late)
     angle = jnp.where(number < NZ, order * (number.astype(jnp.float32) + 0.5) / NZ, angle)
     value = jnp.where((number == 32) | (number == 34), jnp.cos(angle), jnp.sin(angle))
-    fp[...] = jnp.where(number == 36, rate[0] * rate[0] * scale, value)
+    value = jnp.where(number == 36, rate * rate * scale, value)
+    value = jnp.where(number == 37, source_at[...].astype(jnp.float32), value)
+    fp[...] = jnp.where(number == 38, monitor_at[...].astype(jnp.float32), value)
     small = (ROWS, NZ)
     rows = lax.axis_index("space") * ROWS + sublanes(small)
     ramp = 1.0 + 2.0 * (rows.astype(jnp.float32) + 0.5) / grid_rows
     shape_yz[...] = ramp * jnp.sin(order * (lanes(small).astype(jnp.float32) + 0.5) / NZ)
 
 
-def pack_kernel(after, ff, af, ev, od, rows, up, down, sem, out_sem):
-    copies = []
-    for p, f in enumerate((ff, af)):
-        for k, r in enumerate((0, 1, 6, 7)):
-            copies.append(pltpu.make_async_copy(f.at[0, :, 8:24, r, :], rows.at[p, k], sem.at[p, k]))
-    for c in copies:
-        c.start()
+def pack_kernel(even_goes_up, after, ff, af, out, rows, sem):
     tile = sublanes((8, NX))
-    for p in range(2):
-        for k in range(4):
-            copies[4 * p + k].wait()
-
-        def row(k, c, p=p):
-            return pltpu.roll(rows[p, k, c], 12, 0)
-
-        ex, ey, ez = row(0, 0), row(0, 1), row(0, 2)
-        ex_n, ez_n = row(1, 0), row(1, 2)
-        hx = row(0, 3) - COURANT * ((ez_n - ez) - (roll_up(ey) - ey))
-        hy = row(0, 4) - COURANT * ((roll_up(ex) - ex) - (x_up(ez) - ez))
-        hz = row(0, 5) - COURANT * ((x_up(ey) - ey) - (ex_n - ex))
-        cx = hz - (hy - roll_down(hy))
-        cz = (hy - x_down(hy)) - hx
-        base = p * DOWN_ROWS
-        down[base : base + 8] = ex[0:8]
-        down[base + 8 : base + 16] = ez[0:8]
-        down[base + 16 : base + 24] = cx[0:8]
-        down[base + 24 : base + 32] = cz[0:8]
-        extra = jnp.where((tile == 1) | (tile == 2), pltpu.roll(ex[8:16], 2, 0), ez[8:16])
-        down[base + 32 : base + 40] = jnp.where(tile == 3, pltpu.roll(cz[8:16], 4, 0), extra)
-
-        ex_l, ey_l, ez_l = row(2, 0), row(2, 1), row(2, 2)
-        ex, ey, ez = row(3, 0), row(3, 1), row(3, 2)
-        u1 = (x_up(ey) - ey) + ex
-        u2 = ez + (roll_up(ey) - ey)
-        hx = row(3, 3) + COURANT * u2
-        hy = row(3, 4) - COURANT * ((roll_up(ex) - ex) - (x_up(ez) - ez))
-        hz = row(3, 5) - COURANT * u1
-        hx_l = row(2, 3) - COURANT * ((ez - ez_l) - (roll_up(ey_l) - ey_l))
-        hz_l = row(2, 5) - COURANT * ((x_up(ey_l) - ey_l) - (ex - ex_l))
-        cx = (hz - hz_l) - (hy - roll_down(hy))
-        cy = (hx - roll_down(hx)) - (hz - x_down(hz))
-        cz = (hy - x_down(hy)) - (hx - hx_l)
-        base = p * UP_ROWS
-        for k, v in enumerate((hx, hz, u1, u2, cx, cy, cz)):
-            up[base + 8 * k : base + 8 * k + 8] = v[0:8]
-        extra = jnp.where((tile == 1) | (tile == 2), pltpu.roll(hz[8:16], 2, 0), hx[8:16])
-        up[base + 56 : base + 64] = jnp.where(tile == 3, pltpu.roll(cy[8:16], 3, 0), extra)
-
     even = lax.axis_index("space") % 2 == 0
-
-    def send(to_up, to_down):
-        a = pltpu.make_async_copy(up, to_up, out_sem.at[0])
-        b = pltpu.make_async_copy(down, to_down.at[0 : 2 * DOWN_ROWS], out_sem.at[1])
-        a.start()
-        b.start()
-        a.wait()
-        b.wait()
-
-    @pl.when(even)
+    goes_up = even if even_goes_up else jnp.logical_not(even)
+
+    def load(first):
+        copies = []
+        for p, f in enumerate((ff, af)):
+            for k in range(2):
+                copies.append(
+                    pltpu.make_async_copy(f.at[0, :, 8:24, first + k, :], rows.at[p, k], sem.at[p, k])
+                )
+        for c in copies:
+            c.start()
+        return copies
+
+    def row_of(p):
+        return lambda k, c: pltpu.roll(rows[p, k, c], 12, 0)
+
+    @pl.when(jnp.logical_not(goes_up))
     def _():
-        send(ev, od)
-
-    @pl.when(jnp.logical_not(even))
+        copies = load(0)
+        for p in range(2):
+            copies[2 * p].wait()
+            copies[2 * p + 1].wait()
+            row = row_of(p)
+            ex, ey, ez = row(0, 0), row(0, 1), row(0, 2)
+            ex_n, ez_n = row(1, 0), row(1, 2)
+            hx = row(0, 3) - COURANT * ((ez_n - ez) - (roll_up(ey) - ey))
+            hy = row(0, 4) - COURANT * ((roll_up(ex) - ex) - (x_up(ez) - ez))
+            hz = row(0, 5) - COURANT * ((x_up(ey) - ey) - (ex_n - ex))
+            cx = hz - (hy - roll_down(hy))
+            cz = (hy - x_down(hy)) - hx
+            base = p * DOWN_ROWS
+            out[base : base + 8] = ex[0:8]
+            out[base + 8 : base + 16] = ez[0:8]
+            out[base + 16 : base + 24] = cx[0:8]
+            out[base + 24 : base + 32] = cz[0:8]
+            extra = jnp.where((tile == 1) | (tile == 2), pltpu.roll(ex[8:16], 2, 0), ez[8:16])
+            out[base + 32 : base + 40] = jnp.where(tile == 3, pltpu.roll(cz[8:16], 4, 0), extra)
+
+    @pl.when(goes_up)
     def _():
-        send(od, ev)
+        copies = load(6)
+        for p in range(2):
+            copies[2 * p].wait()
+            copies[2 * p + 1].wait()
+            row = row_of(p)
+            ex_l, ey_l, ez_l = row(0, 0), row(0, 1), row(0, 2)
+            ex, ey, ez = row(1, 0), row(1, 1), row(1, 2)
+            u1 = (x_up(ey) - ey) + ex
+            u2 = ez + (roll_up(ey) - ey)
+            hx = row(1, 3) + COURANT * u2
+            hy = row(1, 4) - COURANT * ((roll_up(ex) - ex) - (x_up(ez) - ez))
+            hz = row(1, 5) - COURANT * u1
+            hx_l = row(0, 3) - COURANT * ((ez - ez_l) - (roll_up(ey_l) - ey_l))
+            hz_l = row(0, 5) - COURANT * ((x_up(ey_l) - ey_l) - (ex - ex_l))
+            cx = (hz - hz_l) - (hy - roll_down(hy))
+            cy = (hx - roll_down(hx)) - (hz - x_down(hz))
+            cz = (hy - x_down(hy)) - (hx - hx_l)
+            base = p * UP_ROWS
+            for k, v in enumerate((hx, hz, u1, u2, cx, cy, cz)):
+                out[base + 8 * k : base + 8 * k + 8] = v[0:8]
+            extra = jnp.where((tile == 1) | (tile == 2), pltpu.roll(hz[8:16], 2, 0), hx[8:16])
+            out[base + 56 : base + 64] = jnp.where(tile == 3, pltpu.roll(cy[8:16], 3, 0), extra)
 
 
 def stage_kernel(after, ff, af, field, sem):
@@ -227,11 +230,11 @@
 
 
 def material_kernel(
-    grid_rows, source_at, fp, ev, od, own, monitor, shape_yz, ff,
+    grid_rows, fp, ev, od, own, monitor, shape_yz, ff,
     inv_out, design_out, part_out, wide, fw, win_sem,
 ):
     strip, group = lax.axis_index("space"), lax.axis_index("exc")
-    plane = source_at[0]
+    plane = fp[0, 37].astype(jnp.int32)
     w0 = window_start(plane - 2)
     window = pltpu.make_async_copy(ff.at[0, :, :, :, pl.ds(w0, 256)], fw, win_sem)
     window.start()
@@ -320,12 +323,12 @@
 
 
 def main_kernel(
-    strips, grid_rows, source_at, monitor_at, fp, ev, od, staged, fs, asums, inv_ref, design,
+    strips, grid_rows, fp, ev, od, staged, fs, asums, inv_ref, design,
     ev_out, od_out, s_out, p_out,
     field, sums, below, above, hmx, hmz, hmx2, hmz2, ezp, exp, pscr, sem, halo_sem,
 ):
     strip = lax.axis_index("space")
-    source, plane = source_at[0], monitor_at[0]
+    source, plane = fp[0, 37].astype(jnp.int32), fp[0, 38].astype(jnp.int32)
     c0, s0, c1, s1 = fp[0, 32], fp[0, 33], fp[0, 34], fp[0, 35]
     sum_copies = [
         pltpu.make_async_copy(f.at[0], sums.at[p], sem.at[p, 2]) for p, f in enumerate((fs, asums))
@@ -512,9 +515,9 @@
     od_out[...] = jnp.where(even, to_down, to_up)
 
 
-def final_kernel(norm, monitor_at, fp, ev, od, s_own, p_own, totals, keep, send, merit, scr):
+def final_kernel(norm, fp, ev, od, s_own, p_own, totals, keep, send, merit, scr):
     strip, group = lax.axis_index("space"), lax.axis_index("exc")
-    plane = monitor_at[0]
+    plane = fp[0, 38].astype(jnp.int32)
     even = strip % 2 == 0
     low = jnp.where(even, od[...], ev[...])
     high = jnp.where(even, ev[...], od[...])
@@ -578,45 +581,48 @@
     fp, shape_yz = pl.pallas_call(
         lambda *refs: prepare_kernel(grid_rows, (SILICON - OXIDE) / math.sqrt(groups * DZ), *refs),
         out_shape=[shaped(1, 128), shaped(ROWS, NZ)],
-        in_specs=[SMEM_SPEC] * 3,
+        in_specs=[VMEM_SPEC] * 5,
         out_specs=[VMEM_SPEC] * 2,
         name="prepare",
-    )(mode_numbers, frequency, start_phase)
+    )(
+        *(
+            value.reshape(1, 1)
+            for value in (mode_numbers, frequency, start_phase, source_plane, monitor_plane)
+        )
+    )
 
     quarter = density.T
     width = quarter.shape[1]
     second = swap(quarter, "exc", [(i, i ^ 1) for i in range(groups)])
-    third = swap(
-        jnp.concatenate([quarter, second], 0), "exc", [(i, i ^ 2) for i in range(groups)]
-    )
-    small = jnp.concatenate(
-        [quarter, second, third[0:8], third[8:16], labels.astype(f32)], 1
-    )
+    across = swap(quarter, "exc", [(i, i ^ 2) for i in range(groups)])
+    third = swap(second, "exc", [(i, i ^ 2) for i in range(groups)])
+    small = jnp.concatenate([quarter, second, across, third, labels.astype(f32)], 1)
     od_small = swap(small, "space", odd_pairs)
     ev_small = swap(small, "space", even_pairs)
 
-    ev, od = pl.pallas_call(
-        pack_kernel,
-        out_shape=[shaped(PACK, NX), shaped(PACK, NX)],
-        in_specs=[ANY_SPEC] * 3,
-        out_specs=[ANY_SPEC, ANY_SPEC],
-        scratch_shapes=[
-            pltpu.VMEM((2, 4, 6, 16, NX), f32),
-            pltpu.VMEM((PACK, NX), f32),
-            pltpu.VMEM((2 * DOWN_ROWS, NX), f32),
-            pltpu.SemaphoreType.DMA((2, 4)),
-            pltpu.SemaphoreType.DMA((2,)),
-        ],
-        compiler_params=params(PACK_LIMIT),
-        name="pack",
-    )(second, forward_fields, adjoint_fields)
+    def pack(even_goes_up, after, name):
+        return pl.pallas_call(
+            lambda *refs: pack_kernel(even_goes_up, *refs),
+            out_shape=shaped(PACK, NX),
+            in_specs=[ANY_SPEC] * 3,
+            out_specs=VMEM_SPEC,
+            scratch_shapes=[
+                pltpu.VMEM((2, 2, 6, 16, NX), f32),
+                pltpu.SemaphoreType.DMA((2, 2)),
+            ],
+            compiler_params=params(PACK_LIMIT),
+            name=name,
+        )(after, forward_fields, adjoint_fields)
+
+    od = pack(False, second, "pack_odd")
+    ev = pack(True, third, "pack_even")
     staged = pl.pallas_call(
         stage_kernel,
         out_shape=shaped(2, 6, 16, ROWS, NX),
         in_specs=[ANY_SPEC] * 3,
         out_specs=VMEM_SPEC,
         scratch_shapes=[pltpu.SemaphoreType.DMA((2, 2))],
-        compiler_params=params(PACK_LIMIT),
+        compiler_params=params(46 * 1024 * 1024),
         name="stage",
     )(small, forward_fields, adjoint_fields)
     od = swap(od, "space", odd_pairs)
@@ -630,7 +636,7 @@
     inv, design, part = pl.pallas_call(
         material,
         out_shape=[shaped(16, NX), shaped(8, NX), shaped(8, 128)],
-        in_specs=[SMEM_SPEC, SMEM_SPEC] + [VMEM_SPEC] * 5 + [ANY_SPEC],
+        in_specs=[SMEM_SPEC] + [VMEM_SPEC] * 5 + [ANY_SPEC],
         out_specs=[VMEM_SPEC] * 3,
         scratch_shapes=[
             pltpu.VMEM((24, NX), f32),
@@ -640,7 +646,7 @@
         compiler_params=params(),
         name="material",
     )(
-        source_plane, fp, ev_small, od_small, small, monitor_sums.transpose(0, 1, 3, 2), shape_yz,
+        fp, ev_small, od_small, small, monitor_sums.transpose(0, 1, 3, 2), shape_yz,
         forward_fields,
     )
 
@@ -656,7 +662,7 @@
     ev3, od3, s_own, p_own = pl.pallas_call(
         main,
         out_shape=[shaped(8, NX)] * 4,
-        in_specs=[SMEM_SPEC] * 3 + [ANY_SPEC] * 2 + [VMEM_SPEC] + [ANY_SPEC] * 2 + [VMEM_SPEC] * 2,
+        in_specs=[SMEM_SPEC] + [ANY_SPEC] * 2 + [VMEM_SPEC] + [ANY_SPEC] * 2 + [VMEM_SPEC] * 2,
         out_specs=[VMEM_SPEC] * 4,
         scratch_shapes=[
             pltpu.VMEM((2, 6, 16, ROWS, NX), f32),
@@ -676,7 +682,7 @@
         compiler_params=params(),
         name="main",
     )(
-        source_plane, monitor_plane, fp, ev, od, staged, forward_sums, adjoint_sums, inv, design,
+        fp, ev, od, staged, forward_sums, adjoint_sums, inv, design,
     )
     od3, totals = lax.optimization_barrier((od3, totals))
     totals = totals + arriving
@@ -695,12 +701,12 @@
     keep, send, merit = pl.pallas_call(
         final,
         out_shape=[shaped(half_count, ROWS, width)] * 2 + [shaped(1, 128)],
-        in_specs=[SMEM_SPEC, SMEM_SPEC] + [VMEM_SPEC] * 5,
+        in_specs=[SMEM_SPEC] + [VMEM_SPEC] * 5,
         out_specs=[VMEM_SPEC] * 3,
         scratch_shapes=[pltpu.VMEM((8, NX), f32)],
         compiler_params=params(),
         name="final",
-    )(monitor_plane, fp, ev3, od3, s_own, p_own, totals)
+    )(fp, ev3, od3, s_own, p_own, totals)
     block = keep + swap(send, "exc", [(i, i ^ 1) for i in range(groups)])
     bit = 2
     while bit < groups:

time: 67.5 us -> 66.3 us (0.982)
  Pallas kernels: 17.4 us -> 15.3 us
  starting transfers between devices: 22.9 us -> 24.2 us
  other arithmetic: 1.33 us -> 0.63 us
    pallas_call x1, Pallas kernels: 5.9 us -> 2.75 us  [local(): pl.pallas_call(stage_kernel, out_shape=shaped(2, 6, 16, ROWS, NX), in_spe...]
    ppermute x14 -> x15, starting transfers between devices: 22.9 us -> 24.2 us  [swap(): return lax.ppermute(value, axis, pairs)]
    pallas_call x1, Pallas kernels: 3.81 us -> 4.72 us  [local(): pl.pallas_call(main, out_shape=[shaped(8, NX)] * 4, in_specs=[SMEM_SPEC]...]
    concatenate x2 -> x1, other arithmetic: 0.7 us -> 0.01 us  [local(): jnp.concatenate([quarter, second, across, third, labels.astype(f32)], 1)]
    ppermute x14 -> x15, waiting for transfers between devices: 20.5 us -> 20.8 us  [swap(): return lax.ppermute(value, axis, pairs)]
    pallas_call x1 -> x2, Pallas kernels: 3.35 us -> 3.46 us  [pack(): pl.pallas_call(lambda *refs: pack_kernel(even_goes_up, *refs), out_shape=...]
  transfers between devices with their start and end apart: 14 -> 15, of which waited for: 7 -> 7; matrix products, arithmetic and copies ran while one was open for 1% -> 1% of each run, Pallas kernels for 24% -> 21%
where the time goes in v4:
time: 66.3 us; the launch traced here: 66 us
  starting transfers between devices  24.2 us (37%)
  waiting for transfers between devices  20.8 us (31%)
  Pallas kernels  15.3 us (23%)
  between operations  4.15 us (6%)
  local copies, waits for them, and re-layouts  0.99 us (1%)
    ppermute x15, starting transfers between devices, swap(): return lax.ppermute(value, axis, pairs)  24.2 us
    ppermute x15, waiting for transfers between devices, swap(): return lax.ppermute(value, axis, pairs)  20.8 us
    pallas_call x1, Pallas kernels, local(): pl.pallas_call(main, out_shape=[shaped(8, NX)] * 4, in_specs=[SMEM_SPEC]...  4.72 us
    pallas_call x2, Pallas kernels, pack(): pl.pallas_call(lambda *refs: pack_kernel(even_goes_up, *refs), out_shape=...  3.46 us
    pallas_call x1, Pallas kernels, local(): pl.pallas_call(stage_kernel, out_shape=shaped(2, 6, 16, ROWS, NX), in_spe...  2.75 us
    pallas_call x1, Pallas kernels, local(): pl.pallas_call(material, out_shape=[shaped(16, NX), shaped(8, NX), shaped...  2.33 us
  transfers between devices with their start and end apart: 15, of which 7 were waited for; matrix products, arithmetic and copies ran while one was open for 1% of the time, Pallas kernels for 21%

profile of v4, /device:TPU:6, one launch (start us, length us, event | category | flops | bytes accessed | tf_op | source)
XLA Modules:
  0.0 66.0 jit_solution(1755916318608601751)
XLA Ops:
  0.7 1.7 %collective-permute-start.1 = (f32[8,256]{1,0:T(8,128)}, f32[8,256]{1,0:T(8,128)S(1)}, u32[]{:S(2)}, u32[]{:S(2)}) collective-permute-start(f32[8,256]{1,0:T(8,128)} %bitcast.23), channel_id=1, source_target_pairs={{0,64},{32,96},{64,0},{96,32},{1,65},{33,97},{65,1},{97,33},{2,66}... | collective-permute-start | bytes 24584 | tf_op jit(solution)/shard_map/ppermute | solution.py:562
  2.4 1.3 %collective-permute-start.2 = (f32[8,256]{1,0:T(8,128)S(1)}, f32[8,256]{1,0:T(8,128)S(1)}, u32[]{:S(2)}, u32[]{:S(2)}) collective-permute-start(f32[8,256]{1,0:T(8,128)S(1)} %collective-permute-done.refs_0_), channel_id=1, source_target_pairs={{0,64},{32,96},{64,0},{96,32},{1,65},{33,97},{65,1},{97,33},{2,66}... | collective-permute-start | bytes 24584 | tf_op jit(solution)/shard_map/ppermute | solution.py:562
  3.7 0.7 %constant_dynamic-update-slice_fusion.3 = f32[8,2048]{1,0:T(8,128)S(1)} fusion(f32[256,8]{0,1:T(8,128)} %param.17), kind=kLoop, calls=%fused_computation.4 | loop fusion | bytes 16384
  4.4 1.6 %pack_odd.1 = f32[128,1024]{1,0:T(8,128)S(1)} custom-call(f32[8,256]{1,0:T(8,128)S(1)} %collective-permute-done.refs_0_, f32[1,6,32,8,1024]{4,3,2,1,0:T(8,128)} %refs_6_.1, f32[1,6,32,8,1024]{4,3,2,1,0:T(8,128)} %refs_2_.3), custom_call_target="tpu_custom_call" | custom-call | tf_op jit(solution)/shard_map/pack_odd/pallas_call | solution.py:604
  6.0 8.6 %collective-permute-start.4 = (f32[128,1024]{1,0:T(8,128)S(1)}, f32[128,1024]{1,0:T(8,128)}, u32[]{:S(2)}, u32[]{:S(2)}) collective-permute-start(f32[128,1024]{1,0:T(8,128)S(1)} %pack_odd.1), channel_id=1, source_target_pairs={{1,2},{2,1},{3,4},{4,3},{5,6},{6,5},{7,8},{8,7},{9,10},{10,9},{11,... | collective-permute-start | bytes 1572872 | tf_op jit(solution)/shard_map/ppermute | solution.py:562
  14.6 1.8 %pack_even.1 = f32[128,1024]{1,0:T(8,128)S(1)} custom-call(f32[8,256]{1,0:T(8,128)S(1)} %collective-permute-done.2.refs_0_, f32[1,6,32,8,1024]{4,3,2,1,0:T(8,128)} %refs_6_.1, f32[1,6,32,8,1024]{4,3,2,1,0:T(8,128)} %refs_2_.3), custom_call_target="tpu_custom_call" | custom-call | tf_op jit(solution)/shard_map/pack_even/pallas_call | solution.py:604
  16.6 2.4 %collective-permute-start.6 = (f32[8,2048]{1,0:T(8,128)S(1)}, f32[8,2048]{1,0:T(8,128)S(1)}, u32[]{:S(2)}, u32[]{:S(2)}) collective-permute-start(f32[8,2048]{1,0:T(8,128)S(1)} %convert_dynamic-update-slice_fusion.after.refs_3_), channel_id=1, source_target_pairs={{1,2},{2,1},{3,4},{4,3},{5,6},{6,5},{7,8},{8,7},{9,10},{10,9},{11,... | collective-permute-start | bytes 196616 | tf_op jit(solution)/shard_map/ppermute | solution.py:562
  19.0 1.6 %collective-permute-start.5 = (f32[8,2048]{1,0:T(8,128)S(1)}, f32[8,2048]{1,0:T(8,128)S(1)}, u32[]{:S(2)}, u32[]{:S(2)}) collective-permute-start(f32[8,2048]{1,0:T(8,128)S(1)} %convert_dynamic-update-slice_fusion.after.refs_3_), channel_id=1, source_target_pairs={{0,1},{1,0},{2,3},{3,2},{4,5},{5,4},{6,7},{7,6},{8,9},{9,8},{10,11... | collective-permute-start | bytes 196616 | tf_op jit(solution)/shard_map/ppermute | solution.py:562
  23.8 0.7 %prepare.1 = (f32[1,128]{1,0:T(1,128)}, f32[8,32]{1,0:T(8,128)}) custom-call(s32[1,1]{1,0:T(1,128)} %bitcast.16.refs_0_, f32[1,1]{1,0:T(1,128)} %bitcast.17.refs_1_, f32[1,1]{1,0:T(1,128)} %bitcast.18.refs_2_, s32[1,1]{1,0:T(1,128)} %bitcast.14.refs_3_, s32[1,1]{1,0:T(1,128)} %bitcast.15.refs_4_), custom_call_target="tpu_custom_call" | custom-call | tf_op jit(solution)/shard_map/prepare/pallas_call | solution.py:581
  24.6 2.8 %stage.1.refs_3_ = f32[2,6,16,8,1024]{4,3,2,1,0:T(8,128)S(1)} custom-call(f32[8,2048]{1,0:T(8,128)S(1)} %convert_dynamic-update-slice_fusion.after.refs_3_, f32[1,6,32,8,1024]{4,3,2,1,0:T(8,128)} %refs_6_.1, f32[1,6,32,8,1024]{4,3,2,1,0:T(8,128)} %refs_2_.3), custom_call_target="tpu_custom_call" | custom-call | tf_op jit(solution)/shard_map/stage/pallas_call | solution.py:619
  27.3 0.6 collective-permute-done.6.refs_2_
  28.0 3.4 %collective-permute-done.5.refs_1_ = f32[8,2048]{1,0:T(8,128)S(1)} collective-permute-done((f32[8,2048]{1,0:T(8,128)S(1)}, f32[8,2048]{1,0:T(8,128)S(1)}, u32[]{:S(2)}, u32[]{:S(2)}) %collective-permute-start.5) | collective-permute-done | bytes 65568 | tf_op jit(solution)/shard_map/ppermute | solution.py:562
  31.4 2.3 %material.1 = (f32[16,1024]{1,0:T(8,128)S(1)}, f32[8,1024]{1,0:T(8,128)S(1)}, f32[8,128]{1,0:T(8,128)S(1)}) custom-call(f32[1,128]{1,0:T(1,128)S(1)} %copy-done.3, f32[8,2048]{1,0:T(8,128)S(1)} %collective-permute-done.5.refs_1_, f32[8,2048]{1,0:T(8,128)S(1)} %collective-permute-done.6.refs_2_, f32[8,2048]{1,0:T(8,128)S(1)} %convert_dynamic-update-slice_fusion.after.refs_3_, ...), custom_call_target="tpu_custom_call" | custom-call | tf_op jit(solution)/shard_map/material/pallas_call | solution.py:636
  34.2 4.7 %main.1 = (f32[8,1024]{1,0:T(8,128)S(1)}, f32[8,1024]{1,0:T(8,128)S(1)}, f32[8,1024]{1,0:T(8,128)S(1)}, f32[8,1024]{1,0:T(8,128)S(1)}) custom-call(f32[1,128]{1,0:T(1,128)S(1)} %copy-done.3, f32[128,1024]{1,0:T(8,128)} %collective-permute-done.3.refs_1_, f32[128,1024]{1,0:T(8,128)} %collective-permute-done.4.refs_2_, ...), custom_call_target="tpu_custom_call" | custom-call | tf_op jit(solution)/shard_map/main/pallas_call | solution.py:662
  39.0 0.9 %collective-permute-start.8 = (f32[1,128]{1,0:T(1,128)S(1)}, f32[1,128]{1,0:T(1,128)S(1)}, u32[]{:S(2)}, u32[]{:S(2)}) collective-permute-start(f32[1,128]{1,0:T(1,128)S(1)} %add.31), channel_id=1, source_target_pairs={{0,8},{1,9},{2,10},{3,11},{4,12},{5,13},{6,14},{7,15},{8,0},{9,1},... | collective-permute-start | bytes 1544 | tf_op jit(solution)/shard_map/ppermute | solution.py:562
  39.9 2.7 %collective-permute-done.8 = f32[1,128]{1,0:T(1,128)S(1)} collective-permute-done((f32[1,128]{1,0:T(1,128)S(1)}, f32[1,128]{1,0:T(1,128)S(1)}, u32[]{:S(2)}, u32[]{:S(2)}) %collective-permute-start.8) | collective-permute-done | bytes 544 | tf_op jit(solution)/shard_map/ppermute | solution.py:562
  43.1 4.3 %collective-permute-done.9 = f32[1,128]{1,0:T(1,128)S(1)} collective-permute-done((f32[1,128]{1,0:T(1,128)S(1)}, f32[1,128]{1,0:T(1,128)S(1)}, u32[]{:S(2)}, u32[]{:S(2)}) %collective-permute-start.9) | collective-permute-done | bytes 544 | tf_op jit(solution)/shard_map/ppermute | solution.py:562
  47.3 1.6 %collective-permute-start.10 = (f32[1,128]{1,0:T(1,128)S(1)}, f32[1,128]{1,0:T(1,128)S(1)}, u32[]{:S(2)}, u32[]{:S(2)}) collective-permute-start(f32[1,128]{1,0:T(1,128)S(1)} %add.33), channel_id=1, source_target_pairs={{0,3},{1,2},{2,1},{3,0},{4,7},{5,6},{6,5},{7,4},{8,11},{9,10},{10,... | collective-permute-start | bytes 1544 | tf_op jit(solution)/shard_map/ppermute | solution.py:562
  48.9 4.9 %collective-permute-start.12 = (f32[8,1024]{1,0:T(8,128)S(1)}, f32[8,1024]{1,0:T(8,128)S(1)}, u32[]{:S(2)}, u32[]{:S(2)}) collective-permute-start(f32[8,1024]{1,0:T(8,128)S(1)} %get-tuple-element.28), channel_id=1, source_target_pairs={{1,2},{2,1},{3,4},{4,3},{5,6},{6,5},{7,8},{8,7},{9,10},{10,9},{11,... | collective-permute-start | bytes 98312 | tf_op jit(solution)/shard_map/ppermute | solution.py:562
  54.2 5.0 %collective-permute-done.12.refs_2_ = f32[8,1024]{1,0:T(8,128)S(1)} collective-permute-done((f32[8,1024]{1,0:T(8,128)S(1)}, f32[8,1024]{1,0:T(8,128)S(1)}, u32[]{:S(2)}, u32[]{:S(2)}) %collective-permute-start.12) | collective-permute-done | bytes 32800 | tf_op jit(solution)/shard_map/ppermute | solution.py:562
  59.3 1.3 %final.1 = (f32[2,8,256]{2,1,0:T(8,128)S(1)}, f32[2,8,256]{2,1,0:T(8,128)S(1)}, f32[1,128]{1,0:T(1,128)}) custom-call(f32[1,128]{1,0:T(1,128)S(1)} %copy-done.3, f32[8,1024]{1,0:T(8,128)S(1)} %collective-permute-done.11.refs_1_, f32[8,1024]{1,0:T(8,128)S(1)} %collective-permute-done.12.refs_2_, f32[8,1024]{1,0:T(8,128)S(1)} %get-tuple-element.29.refs_3_, ...), custom_call_target="tpu_custom_call" | custom-call | tf_op jit(solution)/shard_map/final/pallas_call | solution.py:701
  60.6 1.2 %collective-permute-done.13 = f32[2,8,256]{2,1,0:T(8,128)S(1)} collective-permute-done((f32[2,8,256]{2,1,0:T(8,128)S(1)}, f32[2,8,256]{2,1,0:T(8,128)S(1)}, u32[]{:S(2)}, u32[]{:S(2)}) %collective-permute-start.13) | collective-permute-done | bytes 16416 | tf_op jit(solution)/shard_map/ppermute | solution.py:562
  61.9 3.5 %collective-permute-done.14 = f32[1,8,256]{2,1,0:T(8,128)S(1)} collective-permute-done((f32[1,8,256]{2,1,0:T(8,128)S(1)}, f32[1,8,256]{2,1,0:T(8,128)S(1)}, u32[]{:S(2)}, u32[]{:S(2)}) %collective-permute-start.14) | collective-permute-done | bytes 8224 | tf_op jit(solution)/shard_map/ppermute | solution.py:562
  65.4 0.6 add_bitcast_fusion
  (44 shorter events, 1.6 us)
Async XLA Ops:
  0.6 1.8 %collective-permute-start = (f32[8,256]{1,0:T(8,128)}, f32[8,256]{1,0:T(8,128)S(1)}, u32[]{:S(2)}, u32[]{:S(2)}) collective-permute-start(f32[8,256]{1,0:T(8,128)} %bitcast.22), channel_id=1, source_target_pairs={{0,32},{32,0},{64,96},{96,64},{1,33},{33,1},{65,97},{97,65},{2,34}... | collective-permute-start | bytes 24584 | tf_op jit(solution)/shard_map/ppermute | solution.py:562
  0.7 15.8 %collective-permute-start.1 = (f32[8,256]{1,0:T(8,128)}, f32[8,256]{1,0:T(8,128)S(1)}, u32[]{:S(2)}, u32[]{:S(2)}) collective-permute-start(f32[8,256]{1,0:T(8,128)} %bitcast.23), channel_id=1, source_target_pairs={{0,64},{32,96},{64,0},{96,32},{1,65},{33,97},{65,1},{97,33},{2,66}... | collective-permute-start | bytes 24584 | tf_op jit(solution)/shard_map/ppermute | solution.py:562
  2.4 12.2 %collective-permute-start.2 = (f32[8,256]{1,0:T(8,128)S(1)}, f32[8,256]{1,0:T(8,128)S(1)}, u32[]{:S(2)}, u32[]{:S(2)}) collective-permute-start(f32[8,256]{1,0:T(8,128)S(1)} %collective-permute-done.refs_0_), channel_id=1, source_target_pairs={{0,64},{32,96},{64,0},{96,32},{1,65},{33,97},{65,1},{97,33},{2,66}... | collective-permute-start | bytes 24584 | tf_op jit(solution)/shard_map/ppermute | solution.py:562
  6.0 10.6 %copy-start.5 = (s32[8,1024]{1,0:T(8,128)S(1)}, s32[8,1024]{1,0:T(8,128)}, u32[]{:S(2)}) copy-start(s32[8,1024]{1,0:T(8,128)} %param.18) | copy-start | bytes 98308
  6.0 28.2 %collective-permute-start.4 = (f32[128,1024]{1,0:T(8,128)S(1)}, f32[128,1024]{1,0:T(8,128)}, u32[]{:S(2)}, u32[]{:S(2)}) collective-permute-start(f32[128,1024]{1,0:T(8,128)S(1)} %pack_odd.1), channel_id=1, source_target_pairs={{1,2},{2,1},{3,4},{4,3},{5,6},{6,5},{7,8},{8,7},{9,10},{10,9},{11,... | collective-permute-start | bytes 1572872 | tf_op jit(solution)/shard_map/ppermute | solution.py:562
  14.6 16.8 %slice-start = ((s8[6291456]{0:T(1024)(128)(4,1)}), s8[2097152]{0:T(1024)(128)(4,1)S(1)}, s32[]{:S(2)}) async-start(s8[6291456]{0:T(1024)(128)(4,1)} %bitcast.19), calls=%async_computation | async-start | bytes 4194304
  16.4 17.8 %collective-permute-start.3 = (f32[128,1024]{1,0:T(8,128)S(1)}, f32[128,1024]{1,0:T(8,128)}, u32[]{:S(2)}, u32[]{:S(2)}) collective-permute-start(f32[128,1024]{1,0:T(8,128)S(1)} %pack_even.1), channel_id=1, source_target_pairs={{0,1},{1,0},{2,3},{3,2},{4,5},{5,4},{6,7},{7,6},{8,9},{9,8},{10,11... | collective-permute-start | bytes 1572872 | tf_op jit(solution)/shard_map/ppermute | solution.py:562
  16.6 11.4 %collective-permute-start.6 = (f32[8,2048]{1,0:T(8,128)S(1)}, f32[8,2048]{1,0:T(8,128)S(1)}, u32[]{:S(2)}, u32[]{:S(2)}) collective-permute-start(f32[8,2048]{1,0:T(8,128)S(1)} %convert_dynamic-update-slice_fusion.after.refs_3_), channel_id=1, source_target_pairs={{1,2},{2,1},{3,4},{4,3},{5,6},{6,5},{7,8},{8,7},{9,10},{10,9},{11,... | collective-permute-start | bytes 196616 | tf_op jit(solution)/shard_map/ppermute | solution.py:562
  19.0 12.4 %collective-permute-start.5 = (f32[8,2048]{1,0:T(8,128)S(1)}, f32[8,2048]{1,0:T(8,128)S(1)}, u32[]{:S(2)}, u32[]{:S(2)}) collective-permute-start(f32[8,2048]{1,0:T(8,128)S(1)} %convert_dynamic-update-slice_fusion.after.refs_3_), channel_id=1, source_target_pairs={{0,1},{1,0},{2,3},{3,2},{4,5},{5,4},{6,7},{7,6},{8,9},{9,8},{10,11... | collective-permute-start | bytes 196616 | tf_op jit(solution)/shard_map/ppermute | solution.py:562
  24.5 6.8 %slice-start.1 = ((s8[6291456]{0:T(1024)(128)(4,1)}), s8[4194304]{0:T(1024)(128)(4,1)S(1)}, s32[]{:S(2)}) async-start(s8[6291456]{0:T(1024)(128)(4,1)} %bitcast.19), calls=%async_computation.1 | async-start | bytes 8388608
  24.6 6.8 %copy-start.2 = (f32[1,2,32,8]{2,3,1,0:T(8,128)S(1)}, f32[1,2,32,8]{2,3,1,0:T(8,128)}, u32[]{:S(2)}) copy-start(f32[1,2,32,8]{2,3,1,0:T(8,128)} %param.16) | copy-start | bytes 6148
  24.6 6.8 %copy-start.3 = (f32[1,128]{1,0:T(1,128)S(1)}, f32[1,128]{1,0:T(1,128)}, u32[]{:S(2)}) copy-start(f32[1,128]{1,0:T(1,128)} %get-tuple-element.19.refs_0_) | copy-start | bytes 1540
  24.6 6.8 %copy-start.4 = (f32[8,32]{1,0:T(8,128)S(1)}, f32[8,32]{1,0:T(8,128)}, u32[]{:S(2)}) copy-start(f32[8,32]{1,0:T(8,128)} %get-tuple-element.21.refs_5_) | copy-start | bytes 3076
  27.3 6.9 %copy-start = (f32[1,6,8,8,1024]{4,3,2,1,0:T(8,128)S(1)}, f32[1,6,8,8,1024]{4,3,2,1,0:T(8,128)}, u32[]{:S(2)}) copy-start(f32[1,6,8,8,1024]{4,3,2,1,0:T(8,128)} %refs_4_.1) | copy-start | bytes 4718596
  27.3 6.9 %copy-start.1 = (f32[1,6,8,8,1024]{4,3,2,1,0:T(8,128)S(1)}, f32[1,6,8,8,1024]{4,3,2,1,0:T(8,128)}, u32[]{:S(2)}) copy-start(f32[1,6,8,8,1024]{4,3,2,1,0:T(8,128)} %refs_5_.1) | copy-start | bytes 4718596
  33.8 5.2 %collective-permute-start.7 = (f32[1,128]{1,0:T(1,128)S(1)}, f32[1,128]{1,0:T(1,128)S(1)}, u32[]{:S(2)}, u32[]{:S(2)}) collective-permute-start(f32[1,128]{1,0:T(1,128)S(1)} %slice.6), channel_id=1, source_target_pairs={{0,4},{1,5},{2,6},{3,7},{4,0},{5,1},{6,2},{7,3},{8,12},{9,13},{10,... | collective-permute-start | bytes 1544 | tf_op jit(solution)/shard_map/ppermute | solution.py:562
  39.0 3.6 %collective-permute-start.8 = (f32[1,128]{1,0:T(1,128)S(1)}, f32[1,128]{1,0:T(1,128)S(1)}, u32[]{:S(2)}, u32[]{:S(2)}) collective-permute-start(f32[1,128]{1,0:T(1,128)S(1)} %add.31), channel_id=1, source_target_pairs={{0,8},{1,9},{2,10},{3,11},{4,12},{5,13},{6,14},{7,15},{8,0},{9,1},... | collective-permute-start | bytes 1544 | tf_op jit(solution)/shard_map/ppermute | solution.py:562
  42.6 4.8 %collective-permute-start.9 = (f32[1,128]{1,0:T(1,128)S(1)}, f32[1,128]{1,0:T(1,128)S(1)}, u32[]{:S(2)}, u32[]{:S(2)}) collective-permute-start(f32[1,128]{1,0:T(1,128)S(1)} %add.32), channel_id=1, source_target_pairs={{0,24},{1,25},{2,26},{3,27},{4,28},{5,29},{6,30},{7,31},{8,16},{9,... | collective-permute-start | bytes 1544 | tf_op jit(solution)/shard_map/ppermute | solution.py:562
  47.3 6.5 %collective-permute-start.10 = (f32[1,128]{1,0:T(1,128)S(1)}, f32[1,128]{1,0:T(1,128)S(1)}, u32[]{:S(2)}, u32[]{:S(2)}) collective-permute-start(f32[1,128]{1,0:T(1,128)S(1)} %add.33), channel_id=1, source_target_pairs={{0,3},{1,2},{2,1},{3,0},{4,7},{5,6},{6,5},{7,4},{8,11},{9,10},{10,... | collective-permute-start | bytes 1544 | tf_op jit(solution)/shard_map/ppermute | solution.py:562
  48.9 10.3 %collective-permute-start.12 = (f32[8,1024]{1,0:T(8,128)S(1)}, f32[8,1024]{1,0:T(8,128)S(1)}, u32[]{:S(2)}, u32[]{:S(2)}) collective-permute-start(f32[8,1024]{1,0:T(8,128)S(1)} %get-tuple-element.28), channel_id=1, source_target_pairs={{1,2},{2,1},{3,4},{4,3},{5,6},{6,5},{7,8},{8,7},{9,10},{10,9},{11,... | collective-permute-start | bytes 98312 | tf_op jit(solution)/shard_map/ppermute | solution.py:562
  54.1 5.1 %collective-permute-start.11 = (f32[8,1024]{1,0:T(8,128)S(1)}, f32[8,1024]{1,0:T(8,128)S(1)}, u32[]{:S(2)}, u32[]{:S(2)}) collective-permute-start(f32[8,1024]{1,0:T(8,128)S(1)} %dynamic_update_slice.3), channel_id=1, source_target_pairs={{0,1},{1,0},{2,3},{3,2},{4,5},{5,4},{6,7},{7,6},{8,9},{9,8},{10,11... | collective-permute-start | bytes 98312 | tf_op jit(solution)/shard_map/ppermute | solution.py:562
  60.6 1.2 %collective-permute-start.13 = (f32[2,8,256]{2,1,0:T(8,128)S(1)}, f32[2,8,256]{2,1,0:T(8,128)S(1)}, u32[]{:S(2)}, u32[]{:S(2)}) collective-permute-start(f32[2,8,256]{2,1,0:T(8,128)S(1)} %get-tuple-element.32), channel_id=1, source_target_pairs={{0,32},{32,0},{64,96},{96,64},{1,33},{33,1},{65,97},{97,65},{2,34}... | collective-permute-start | bytes 49160 | tf_op jit(solution)/shard_map/ppermute | solution.py:562
  61.8 3.7 %collective-permute-start.14 = (f32[1,8,256]{2,1,0:T(8,128)S(1)}, f32[1,8,256]{2,1,0:T(8,128)S(1)}, u32[]{:S(2)}, u32[]{:S(2)}) collective-permute-start(f32[1,8,256]{2,1,0:T(8,128)S(1)} %constant_dynamic-slice_fusion), channel_id=1, source_target_pairs={{0,64},{32,96},{64,0},{96,32},{1,65},{33,97},{65,1},{97,33},{2,66}... | collective-permute-start | bytes 24584 | tf_op jit(solution)/shard_map/ppermute | solution.py:562

commit v5 on v4

--- a/solution.py
+++ b/solution.py
@@ -515,7 +515,8 @@
     od_out[...] = jnp.where(even, to_down, to_up)
 
 
-def final_kernel(norm, fp, ev, od, s_own, p_own, totals, keep, send, merit, scr):
+def final_kernel(norm, fp, ev, od, s_own, p_own, totals, *outs):
+    *blocks, merit, scr = outs
     strip, group = lax.axis_index("space"), lax.axis_index("exc")
     plane = fp[0, 38].astype(jnp.int32)
     even = strip % 2 == 0
@@ -534,24 +535,11 @@
     w1 = window_start(plane - 1)
     scr[...] = y_smooth(both, 8)
     scr[:, pl.ds(w1, 256)] += g0 * more[:, 0:256] + g1 * more[:, 256:512]
-    result = x_smooth(scr[...])
-    count = keep.shape[0]
-    width = NX // (2 * count)
-
-    def split(mine):
-        for k in range(count):
-            a = (2 * k + mine) * width
-            b = (2 * k + 1 - mine) * width
-            keep[k] = result[:, a : a + width]
-            send[k] = result[:, b : b + width]
-
-    @pl.when(group % 2 == 0)
-    def _():
-        split(0)
-
-    @pl.when(group % 2 == 1)
-    def _():
-        split(1)
+    scr[...] = x_smooth(scr[...])
+    width = NX // len(blocks)
+    for k, block in enumerate(blocks):
+        at = pl.multiple_of((group ^ k) * width, 128)
+        block[...] = scr[:, pl.ds(at, width)]
 
 
 def params(limit=VMEM_LIMIT):
@@ -569,7 +557,6 @@
     groups = lax.axis_size("exc")
     strips = lax.axis_size("space")
     grid_rows = ROWS * strips
-    group = lax.axis_index("exc").astype(jnp.int32)
     f32 = jnp.float32
 
     def shaped(*shape):
@@ -693,31 +680,23 @@
     ev3 = swap(lax.dynamic_update_slice(ev3, totals, (4, 512)), "space", even_pairs)
 
     norm = math.sqrt(NZ * grid_rows)
-    half_count = groups // 2
 
     def final(*refs):
         final_kernel(norm, *refs)
 
-    keep, send, merit = pl.pallas_call(
+    *blocks, merit = pl.pallas_call(
         final,
-        out_shape=[shaped(half_count, ROWS, width)] * 2 + [shaped(1, 128)],
+        out_shape=[shaped(ROWS, width)] * groups + [shaped(1, 128)],
         in_specs=[SMEM_SPEC] + [VMEM_SPEC] * 5,
-        out_specs=[VMEM_SPEC] * 3,
+        out_specs=[VMEM_SPEC] * (groups + 1),
         scratch_shapes=[pltpu.VMEM((8, NX), f32)],
         compiler_params=params(),
         name="final",
     )(fp, ev3, od3, s_own, p_own, totals)
-    block = keep + swap(send, "exc", [(i, i ^ 1) for i in range(groups)])
-    bit = 2
-    while bit < groups:
-        count = block.shape[0] // 2
-        pairs = block.reshape(count, 2, ROWS, width)
-        mine = (group // bit) % 2
-        kept = lax.dynamic_index_in_dim(pairs, mine, 1, keepdims=False)
-        given = lax.dynamic_index_in_dim(pairs, 1 - mine, 1, keepdims=False)
-        block = kept + swap(given, "exc", [(i, i ^ bit) for i in range(groups)])
-        bit *= 2
-    return block[0].T, merit[0, 0:1]
+    block = blocks[0]
+    for k in reversed(range(1, groups)):
+        block = block + swap(blocks[k], "exc", [(i, i ^ k) for i in range(groups)])
+    return block.T, merit[0, 0:1]
 
 
 def solution(mesh):

time: 66.3 us -> 65 us (0.980)
  waiting for transfers between devices: 20.8 us -> 17.9 us
  starting transfers between devices: 24.2 us -> 25.9 us
    ppermute x15 -> x16, waiting for transfers between devices: 20.8 us -> 17.9 us  [swap(): return lax.ppermute(value, axis, pairs)]
    ppermute x15 -> x16, starting transfers between devices: 24.2 us -> 25.9 us  [swap(): return lax.ppermute(value, axis, pairs)]
  transfers between devices with their start and end apart: 15 -> 16, of which waited for: 7 -> 7; matrix products, arithmetic and copies ran while one was open for 1% -> 1% of each run, Pallas kernels for 21% -> 22%
where the time goes in v5:
time: 65 us; the launch traced here: 64.7 us
  starting transfers between devices  25.9 us (40%)
  waiting for transfers between devices  17.9 us (28%)
  Pallas kernels  15.1 us (23%)
  between operations  4.15 us (6%)
  local copies, waits for them, and re-layouts  0.99 us (2%)
    ppermute x16, starting transfers between devices, swap(): return lax.ppermute(value, axis, pairs)  25.9 us
    ppermute x16, waiting for transfers between devices, swap(): return lax.ppermute(value, axis, pairs)  17.9 us
    pallas_call x1, Pallas kernels, local(): pl.pallas_call(main, out_shape=[shaped(8, NX)] * 4, in_specs=[SMEM_SPEC]...  4.71 us
    pallas_call x2, Pallas kernels, pack(): pl.pallas_call(lambda *refs: pack_kernel(even_goes_up, *refs), out_shape=...  3.46 us
    pallas_call x1, Pallas kernels, local(): pl.pallas_call(stage_kernel, out_shape=shaped(2, 6, 16, ROWS, NX), in_spe...  2.75 us
    pallas_call x1, Pallas kernels, local(): pl.pallas_call(material, out_shape=[shaped(16, NX), shaped(8, NX), shaped...  2.34 us
  transfers between devices with their start and end apart: 16, of which 7 were waited for; matrix products, arithmetic and copies ran while one was open for 1% of the time, Pallas kernels for 22%

profile of v5, /device:TPU:6, one launch (start us, length us, event | category | flops | bytes accessed | tf_op | source)
XLA Modules:
  0.0 64.7 jit_solution(921313439557664694)
XLA Ops:
  0.7 1.7 %collective-permute-start.1 = (f32[8,256]{1,0:T(8,128)}, f32[8,256]{1,0:T(8,128)S(1)}, u32[]{:S(2)}, u32[]{:S(2)}) collective-permute-start(f32[8,256]{1,0:T(8,128)} %bitcast.21), channel_id=1, source_target_pairs={{0,64},{32,96},{64,0},{96,32},{1,65},{33,97},{65,1},{97,33},{2,66}... | collective-permute-start | bytes 24584 | tf_op jit(solution)/shard_map/ppermute | solution.py:550
  2.4 1.3 %collective-permute-start.2 = (f32[8,256]{1,0:T(8,128)S(1)}, f32[8,256]{1,0:T(8,128)S(1)}, u32[]{:S(2)}, u32[]{:S(2)}) collective-permute-start(f32[8,256]{1,0:T(8,128)S(1)} %collective-permute-done.refs_0_), channel_id=1, source_target_pairs={{0,64},{32,96},{64,0},{96,32},{1,65},{33,97},{65,1},{97,33},{2,66}... | collective-permute-start | bytes 24584 | tf_op jit(solution)/shard_map/ppermute | solution.py:550
  3.7 0.7 %constant_dynamic-update-slice_fusion.3 = f32[8,2048]{1,0:T(8,128)S(1)} fusion(f32[256,8]{0,1:T(8,128)} %param.17), kind=kLoop, calls=%fused_computation.4 | loop fusion | bytes 16384
  4.4 1.6 %pack_odd.1 = f32[128,1024]{1,0:T(8,128)S(1)} custom-call(f32[8,256]{1,0:T(8,128)S(1)} %collective-permute-done.refs_0_, f32[1,6,32,8,1024]{4,3,2,1,0:T(8,128)} %refs_6_.1, f32[1,6,32,8,1024]{4,3,2,1,0:T(8,128)} %refs_2_.3), custom_call_target="tpu_custom_call" | custom-call | tf_op jit(solution)/shard_map/pack_odd/pallas_call | solution.py:591
  6.0 8.6 %collective-permute-start.4 = (f32[128,1024]{1,0:T(8,128)S(1)}, f32[128,1024]{1,0:T(8,128)}, u32[]{:S(2)}, u32[]{:S(2)}) collective-permute-start(f32[128,1024]{1,0:T(8,128)S(1)} %pack_odd.1), channel_id=1, source_target_pairs={{1,2},{2,1},{3,4},{4,3},{5,6},{6,5},{7,8},{8,7},{9,10},{10,9},{11,... | collective-permute-start | bytes 1572872 | tf_op jit(solution)/shard_map/ppermute | solution.py:550
  14.6 1.8 %pack_even.1 = f32[128,1024]{1,0:T(8,128)S(1)} custom-call(f32[8,256]{1,0:T(8,128)S(1)} %collective-permute-done.2.refs_0_, f32[1,6,32,8,1024]{4,3,2,1,0:T(8,128)} %refs_6_.1, f32[1,6,32,8,1024]{4,3,2,1,0:T(8,128)} %refs_2_.3), custom_call_target="tpu_custom_call" | custom-call | tf_op jit(solution)/shard_map/pack_even/pallas_call | solution.py:591
  16.6 2.4 %collective-permute-start.6 = (f32[8,2048]{1,0:T(8,128)S(1)}, f32[8,2048]{1,0:T(8,128)S(1)}, u32[]{:S(2)}, u32[]{:S(2)}) collective-permute-start(f32[8,2048]{1,0:T(8,128)S(1)} %convert_dynamic-update-slice_fusion.after.refs_3_), channel_id=1, source_target_pairs={{1,2},{2,1},{3,4},{4,3},{5,6},{6,5},{7,8},{8,7},{9,10},{10,9},{11,... | collective-permute-start | bytes 196616 | tf_op jit(solution)/shard_map/ppermute | solution.py:550
  19.0 1.6 %collective-permute-start.5 = (f32[8,2048]{1,0:T(8,128)S(1)}, f32[8,2048]{1,0:T(8,128)S(1)}, u32[]{:S(2)}, u32[]{:S(2)}) collective-permute-start(f32[8,2048]{1,0:T(8,128)S(1)} %convert_dynamic-update-slice_fusion.after.refs_3_), channel_id=1, source_target_pairs={{0,1},{1,0},{2,3},{3,2},{4,5},{5,4},{6,7},{7,6},{8,9},{9,8},{10,11... | collective-permute-start | bytes 196616 | tf_op jit(solution)/shard_map/ppermute | solution.py:550
  23.8 0.7 %prepare.1 = (f32[1,128]{1,0:T(1,128)}, f32[8,32]{1,0:T(8,128)}) custom-call(s32[1,1]{1,0:T(1,128)} %bitcast.14.refs_0_, f32[1,1]{1,0:T(1,128)} %bitcast.15.refs_1_, f32[1,1]{1,0:T(1,128)} %bitcast.16.refs_2_, s32[1,1]{1,0:T(1,128)} %bitcast.12.refs_3_, s32[1,1]{1,0:T(1,128)} %bitcast.13.refs_4_), custom_call_target="tpu_custom_call" | custom-call | tf_op jit(solution)/shard_map/prepare/pallas_call | solution.py:568
  24.6 2.8 %stage.1.refs_3_ = f32[2,6,16,8,1024]{4,3,2,1,0:T(8,128)S(1)} custom-call(f32[8,2048]{1,0:T(8,128)S(1)} %convert_dynamic-update-slice_fusion.after.refs_3_, f32[1,6,32,8,1024]{4,3,2,1,0:T(8,128)} %refs_6_.1, f32[1,6,32,8,1024]{4,3,2,1,0:T(8,128)} %refs_2_.3), custom_call_target="tpu_custom_call" | custom-call | tf_op jit(solution)/shard_map/stage/pallas_call | solution.py:606
  27.3 0.6 collective-permute-done.6.refs_2_
  28.0 3.4 %collective-permute-done.5.refs_1_ = f32[8,2048]{1,0:T(8,128)S(1)} collective-permute-done((f32[8,2048]{1,0:T(8,128)S(1)}, f32[8,2048]{1,0:T(8,128)S(1)}, u32[]{:S(2)}, u32[]{:S(2)}) %collective-permute-start.5) | collective-permute-done | bytes 65568 | tf_op jit(solution)/shard_map/ppermute | solution.py:550
  31.4 2.3 %material.1 = (f32[16,1024]{1,0:T(8,128)S(1)}, f32[8,1024]{1,0:T(8,128)S(1)}, f32[8,128]{1,0:T(8,128)S(1)}) custom-call(f32[1,128]{1,0:T(1,128)S(1)} %copy-done.3, f32[8,2048]{1,0:T(8,128)S(1)} %collective-permute-done.5.refs_1_, f32[8,2048]{1,0:T(8,128)S(1)} %collective-permute-done.6.refs_2_, f32[8,2048]{1,0:T(8,128)S(1)} %convert_dynamic-update-slice_fusion.after.refs_3_, ...), custom_call_target="tpu_custom_call" | custom-call | tf_op jit(solution)/shard_map/material/pallas_call | solution.py:623
  34.2 4.7 %main.1 = (f32[8,1024]{1,0:T(8,128)S(1)}, f32[8,1024]{1,0:T(8,128)S(1)}, f32[8,1024]{1,0:T(8,128)S(1)}, f32[8,1024]{1,0:T(8,128)S(1)}) custom-call(f32[1,128]{1,0:T(1,128)S(1)} %copy-done.3, f32[128,1024]{1,0:T(8,128)} %collective-permute-done.3.refs_1_, f32[128,1024]{1,0:T(8,128)} %collective-permute-done.4.refs_2_, ...), custom_call_target="tpu_custom_call" | custom-call | tf_op jit(solution)/shard_map/main/pallas_call | solution.py:649
  39.0 0.9 %collective-permute-start.8 = (f32[1,128]{1,0:T(1,128)S(1)}, f32[1,128]{1,0:T(1,128)S(1)}, u32[]{:S(2)}, u32[]{:S(2)}) collective-permute-start(f32[1,128]{1,0:T(1,128)S(1)} %add.21), channel_id=1, source_target_pairs={{0,8},{1,9},{2,10},{3,11},{4,12},{5,13},{6,14},{7,15},{8,0},{9,1},... | collective-permute-start | bytes 1544 | tf_op jit(solution)/shard_map/ppermute | solution.py:550
  39.9 2.7 %collective-permute-done.8 = f32[1,128]{1,0:T(1,128)S(1)} collective-permute-done((f32[1,128]{1,0:T(1,128)S(1)}, f32[1,128]{1,0:T(1,128)S(1)}, u32[]{:S(2)}, u32[]{:S(2)}) %collective-permute-start.8) | collective-permute-done | bytes 544 | tf_op jit(solution)/shard_map/ppermute | solution.py:550
  43.1 4.3 %collective-permute-done.9 = f32[1,128]{1,0:T(1,128)S(1)} collective-permute-done((f32[1,128]{1,0:T(1,128)S(1)}, f32[1,128]{1,0:T(1,128)S(1)}, u32[]{:S(2)}, u32[]{:S(2)}) %collective-permute-start.9) | collective-permute-done | bytes 544 | tf_op jit(solution)/shard_map/ppermute | solution.py:550
  47.3 1.6 %collective-permute-start.10 = (f32[1,128]{1,0:T(1,128)S(1)}, f32[1,128]{1,0:T(1,128)S(1)}, u32[]{:S(2)}, u32[]{:S(2)}) collective-permute-start(f32[1,128]{1,0:T(1,128)S(1)} %add.23), channel_id=1, source_target_pairs={{0,3},{1,2},{2,1},{3,0},{4,7},{5,6},{6,5},{7,4},{8,11},{9,10},{10,... | collective-permute-start | bytes 1544 | tf_op jit(solution)/shard_map/ppermute | solution.py:550
  48.9 4.9 %collective-permute-start.12 = (f32[8,1024]{1,0:T(8,128)S(1)}, f32[8,1024]{1,0:T(8,128)S(1)}, u32[]{:S(2)}, u32[]{:S(2)}) collective-permute-start(f32[8,1024]{1,0:T(8,128)S(1)} %get-tuple-element.30), channel_id=1, source_target_pairs={{1,2},{2,1},{3,4},{4,3},{5,6},{6,5},{7,8},{8,7},{9,10},{10,9},{11,... | collective-permute-start | bytes 98312 | tf_op jit(solution)/shard_map/ppermute | solution.py:550
  54.2 5.0 %collective-permute-done.12.refs_2_ = f32[8,1024]{1,0:T(8,128)S(1)} collective-permute-done((f32[8,1024]{1,0:T(8,128)S(1)}, f32[8,1024]{1,0:T(8,128)S(1)}, u32[]{:S(2)}, u32[]{:S(2)}) %collective-permute-start.12) | collective-permute-done | bytes 32800 | tf_op jit(solution)/shard_map/ppermute | solution.py:550
  59.3 1.1 %final.1 = (f32[8,256]{1,0:T(8,128)S(1)}, f32[8,256]{1,0:T(8,128)S(1)}, f32[8,256]{1,0:T(8,128)S(1)}, f32[8,256]{1,0:T(8,128)S(1)}, f32[1,128]{1,0:T(1,128)}) custom-call(f32[1,128]{1,0:T(1,128)S(1)} %copy-done.3, f32[8,1024]{1,0:T(8,128)S(1)} %collective-permute-done.11.refs_1_, f32[8,1024]{1,0:T(8,128)S(1)} %collective-permute-done.12.refs_2_, ...), custom_call_target="tpu_custom_call" | custom-call | tf_op jit(solution)/shard_map/final/pallas_call | solution.py:687
  60.6 1.7 %collective-permute-start.15 = (f32[8,256]{1,0:T(8,128)S(1)}, f32[8,256]{1,0:T(8,128)S(1)}, u32[]{:S(2)}, u32[]{:S(2)}) collective-permute-start(f32[8,256]{1,0:T(8,128)S(1)} %get-tuple-element.36), channel_id=1, source_target_pairs={{0,32},{32,0},{64,96},{96,64},{1,33},{33,1},{65,97},{97,65},{2,34}... | collective-permute-start | bytes 24584 | tf_op jit(solution)/shard_map/ppermute | solution.py:550
  62.3 1.2 %collective-permute-done.13 = f32[8,256]{1,0:T(8,128)S(1)} collective-permute-done((f32[8,256]{1,0:T(8,128)S(1)}, f32[8,256]{1,0:T(8,128)S(1)}, u32[]{:S(2)}, u32[]{:S(2)}) %collective-permute-start.13) | collective-permute-done | bytes 8224 | tf_op jit(solution)/shard_map/ppermute | solution.py:550
  63.5 0.6 collective-permute-done.14
  (44 shorter events, 2.3 us)
Async XLA Ops:
  0.6 1.8 %collective-permute-start = (f32[8,256]{1,0:T(8,128)}, f32[8,256]{1,0:T(8,128)S(1)}, u32[]{:S(2)}, u32[]{:S(2)}) collective-permute-start(f32[8,256]{1,0:T(8,128)} %bitcast.20), channel_id=1, source_target_pairs={{0,32},{32,0},{64,96},{96,64},{1,33},{33,1},{65,97},{97,65},{2,34}... | collective-permute-start | bytes 24584 | tf_op jit(solution)/shard_map/ppermute | solution.py:550
  0.7 15.8 %collective-permute-start.1 = (f32[8,256]{1,0:T(8,128)}, f32[8,256]{1,0:T(8,128)S(1)}, u32[]{:S(2)}, u32[]{:S(2)}) collective-permute-start(f32[8,256]{1,0:T(8,128)} %bitcast.21), channel_id=1, source_target_pairs={{0,64},{32,96},{64,0},{96,32},{1,65},{33,97},{65,1},{97,33},{2,66}... | collective-permute-start | bytes 24584 | tf_op jit(solution)/shard_map/ppermute | solution.py:550
  2.4 12.2 %collective-permute-start.2 = (f32[8,256]{1,0:T(8,128)S(1)}, f32[8,256]{1,0:T(8,128)S(1)}, u32[]{:S(2)}, u32[]{:S(2)}) collective-permute-start(f32[8,256]{1,0:T(8,128)S(1)} %collective-permute-done.refs_0_), channel_id=1, source_target_pairs={{0,64},{32,96},{64,0},{96,32},{1,65},{33,97},{65,1},{97,33},{2,66}... | collective-permute-start | bytes 24584 | tf_op jit(solution)/shard_map/ppermute | solution.py:550
  6.0 10.6 %copy-start.5 = (s32[8,1024]{1,0:T(8,128)S(1)}, s32[8,1024]{1,0:T(8,128)}, u32[]{:S(2)}) copy-start(s32[8,1024]{1,0:T(8,128)} %param.18) | copy-start | bytes 98308
  6.0 28.2 %collective-permute-start.4 = (f32[128,1024]{1,0:T(8,128)S(1)}, f32[128,1024]{1,0:T(8,128)}, u32[]{:S(2)}, u32[]{:S(2)}) collective-permute-start(f32[128,1024]{1,0:T(8,128)S(1)} %pack_odd.1), channel_id=1, source_target_pairs={{1,2},{2,1},{3,4},{4,3},{5,6},{6,5},{7,8},{8,7},{9,10},{10,9},{11,... | collective-permute-start | bytes 1572872 | tf_op jit(solution)/shard_map/ppermute | solution.py:550
  14.6 16.8 %slice-start = ((s8[6291456]{0:T(1024)(128)(4,1)}), s8[2097152]{0:T(1024)(128)(4,1)S(1)}, s32[]{:S(2)}) async-start(s8[6291456]{0:T(1024)(128)(4,1)} %bitcast.17), calls=%async_computation | async-start | bytes 4194304
  16.4 17.8 %collective-permute-start.3 = (f32[128,1024]{1,0:T(8,128)S(1)}, f32[128,1024]{1,0:T(8,128)}, u32[]{:S(2)}, u32[]{:S(2)}) collective-permute-start(f32[128,1024]{1,0:T(8,128)S(1)} %pack_even.1), channel_id=1, source_target_pairs={{0,1},{1,0},{2,3},{3,2},{4,5},{5,4},{6,7},{7,6},{8,9},{9,8},{10,11... | collective-permute-start | bytes 1572872 | tf_op jit(solution)/shard_map/ppermute | solution.py:550
  16.6 11.4 %collective-permute-start.6 = (f32[8,2048]{1,0:T(8,128)S(1)}, f32[8,2048]{1,0:T(8,128)S(1)}, u32[]{:S(2)}, u32[]{:S(2)}) collective-permute-start(f32[8,2048]{1,0:T(8,128)S(1)} %convert_dynamic-update-slice_fusion.after.refs_3_), channel_id=1, source_target_pairs={{1,2},{2,1},{3,4},{4,3},{5,6},{6,5},{7,8},{8,7},{9,10},{10,9},{11,... | collective-permute-start | bytes 196616 | tf_op jit(solution)/shard_map/ppermute | solution.py:550
  19.0 12.4 %collective-permute-start.5 = (f32[8,2048]{1,0:T(8,128)S(1)}, f32[8,2048]{1,0:T(8,128)S(1)}, u32[]{:S(2)}, u32[]{:S(2)}) collective-permute-start(f32[8,2048]{1,0:T(8,128)S(1)} %convert_dynamic-update-slice_fusion.after.refs_3_), channel_id=1, source_target_pairs={{0,1},{1,0},{2,3},{3,2},{4,5},{5,4},{6,7},{7,6},{8,9},{9,8},{10,11... | collective-permute-start | bytes 196616 | tf_op jit(solution)/shard_map/ppermute | solution.py:550
  24.5 6.8 %slice-start.1 = ((s8[6291456]{0:T(1024)(128)(4,1)}), s8[4194304]{0:T(1024)(128)(4,1)S(1)}, s32[]{:S(2)}) async-start(s8[6291456]{0:T(1024)(128)(4,1)} %bitcast.17), calls=%async_computation.1 | async-start | bytes 8388608
  24.6 6.8 %copy-start.2 = (f32[1,2,32,8]{2,3,1,0:T(8,128)S(1)}, f32[1,2,32,8]{2,3,1,0:T(8,128)}, u32[]{:S(2)}) copy-start(f32[1,2,32,8]{2,3,1,0:T(8,128)} %param.16) | copy-start | bytes 6148
  24.6 6.8 %copy-start.3 = (f32[1,128]{1,0:T(1,128)S(1)}, f32[1,128]{1,0:T(1,128)}, u32[]{:S(2)}) copy-start(f32[1,128]{1,0:T(1,128)} %get-tuple-element.21.refs_0_) | copy-start | bytes 1540
  24.6 6.8 %copy-start.4 = (f32[8,32]{1,0:T(8,128)S(1)}, f32[8,32]{1,0:T(8,128)}, u32[]{:S(2)}) copy-start(f32[8,32]{1,0:T(8,128)} %get-tuple-element.23.refs_5_) | copy-start | bytes 3076
  27.3 6.9 %copy-start = (f32[1,6,8,8,1024]{4,3,2,1,0:T(8,128)S(1)}, f32[1,6,8,8,1024]{4,3,2,1,0:T(8,128)}, u32[]{:S(2)}) copy-start(f32[1,6,8,8,1024]{4,3,2,1,0:T(8,128)} %refs_4_.1) | copy-start | bytes 4718596
  27.3 6.9 %copy-start.1 = (f32[1,6,8,8,1024]{4,3,2,1,0:T(8,128)S(1)}, f32[1,6,8,8,1024]{4,3,2,1,0:T(8,128)}, u32[]{:S(2)}) copy-start(f32[1,6,8,8,1024]{4,3,2,1,0:T(8,128)} %refs_5_.1) | copy-start | bytes 4718596
  33.8 5.2 %collective-permute-start.7 = (f32[1,128]{1,0:T(1,128)S(1)}, f32[1,128]{1,0:T(1,128)S(1)}, u32[]{:S(2)}, u32[]{:S(2)}) collective-permute-start(f32[1,128]{1,0:T(1,128)S(1)} %slice.6), channel_id=1, source_target_pairs={{0,4},{1,5},{2,6},{3,7},{4,0},{5,1},{6,2},{7,3},{8,12},{9,13},{10,... | collective-permute-start | bytes 1544 | tf_op jit(solution)/shard_map/ppermute | solution.py:550
  39.0 3.6 %collective-permute-start.8 = (f32[1,128]{1,0:T(1,128)S(1)}, f32[1,128]{1,0:T(1,128)S(1)}, u32[]{:S(2)}, u32[]{:S(2)}) collective-permute-start(f32[1,128]{1,0:T(1,128)S(1)} %add.21), channel_id=1, source_target_pairs={{0,8},{1,9},{2,10},{3,11},{4,12},{5,13},{6,14},{7,15},{8,0},{9,1},... | collective-permute-start | bytes 1544 | tf_op jit(solution)/shard_map/ppermute | solution.py:550
  42.6 4.8 %collective-permute-start.9 = (f32[1,128]{1,0:T(1,128)S(1)}, f32[1,128]{1,0:T(1,128)S(1)}, u32[]{:S(2)}, u32[]{:S(2)}) collective-permute-start(f32[1,128]{1,0:T(1,128)S(1)} %add.22), channel_id=1, source_target_pairs={{0,24},{1,25},{2,26},{3,27},{4,28},{5,29},{6,30},{7,31},{8,16},{9,... | collective-permute-start | bytes 1544 | tf_op jit(solution)/shard_map/ppermute | solution.py:550
  47.3 6.5 %collective-permute-start.10 = (f32[1,128]{1,0:T(1,128)S(1)}, f32[1,128]{1,0:T(1,128)S(1)}, u32[]{:S(2)}, u32[]{:S(2)}) collective-permute-start(f32[1,128]{1,0:T(1,128)S(1)} %add.23), channel_id=1, source_target_pairs={{0,3},{1,2},{2,1},{3,0},{4,7},{5,6},{6,5},{7,4},{8,11},{9,10},{10,... | collective-permute-start | bytes 1544 | tf_op jit(solution)/shard_map/ppermute | solution.py:550
  48.9 10.3 %collective-permute-start.12 = (f32[8,1024]{1,0:T(8,128)S(1)}, f32[8,1024]{1,0:T(8,128)S(1)}, u32[]{:S(2)}, u32[]{:S(2)}) collective-permute-start(f32[8,1024]{1,0:T(8,128)S(1)} %get-tuple-element.30), channel_id=1, source_target_pairs={{1,2},{2,1},{3,4},{4,3},{5,6},{6,5},{7,8},{8,7},{9,10},{10,9},{11,... | collective-permute-start | bytes 98312 | tf_op jit(solution)/shard_map/ppermute | solution.py:550
  54.1 5.1 %collective-permute-start.11 = (f32[8,1024]{1,0:T(8,128)S(1)}, f32[8,1024]{1,0:T(8,128)S(1)}, u32[]{:S(2)}, u32[]{:S(2)}) collective-permute-start(f32[8,1024]{1,0:T(8,128)S(1)} %dynamic_update_slice.3), channel_id=1, source_target_pairs={{0,1},{1,0},{2,3},{3,2},{4,5},{5,4},{6,7},{7,6},{8,9},{9,8},{10,11... | collective-permute-start | bytes 98312 | tf_op jit(solution)/shard_map/ppermute | solution.py:550
  60.4 3.1 %collective-permute-start.13 = (f32[8,256]{1,0:T(8,128)S(1)}, f32[8,256]{1,0:T(8,128)S(1)}, u32[]{:S(2)}, u32[]{:S(2)}) collective-permute-start(f32[8,256]{1,0:T(8,128)S(1)} %get-tuple-element.34), channel_id=1, source_target_pairs={{0,96},{32,64},{64,32},{96,0},{1,97},{33,65},{65,33},{97,1},{2,98}... | collective-permute-start | bytes 24584 | tf_op jit(solution)/shard_map/ppermute | solution.py:550
  60.4 3.7 %collective-permute-start.14 = (f32[8,256]{1,0:T(8,128)S(1)}, f32[8,256]{1,0:T(8,128)S(1)}, u32[]{:S(2)}, u32[]{:S(2)}) collective-permute-start(f32[8,256]{1,0:T(8,128)S(1)} %get-tuple-element.35), channel_id=1, source_target_pairs={{0,64},{32,96},{64,0},{96,32},{1,65},{33,97},{65,1},{97,33},{2,66}... | collective-permute-start | bytes 24584 | tf_op jit(solution)/shard_map/ppermute | solution.py:550
  60.6 3.5 %collective-permute-start.15 = (f32[8,256]{1,0:T(8,128)S(1)}, f32[8,256]{1,0:T(8,128)S(1)}, u32[]{:S(2)}, u32[]{:S(2)}) collective-permute-start(f32[8,256]{1,0:T(8,128)S(1)} %get-tuple-element.36), channel_id=1, source_target_pairs={{0,32},{32,0},{64,96},{96,64},{1,33},{33,1},{65,97},{97,65},{2,34}... | collective-permute-start | bytes 24584 | tf_op jit(solution)/shard_map/ppermute | solution.py:550
